TPU v7x, 32 devices: a whole 2x2x4 slice. The times are simulated.
32 devices in a mesh: grid: 4 (over y, core), dom: 8 (over z, x).
Axes of the slice: x: 2, y: 2, z: 4, core: 2. Of those that a mesh axis runs over, the one named last changes fastest.
Arguments:
- state: float32 [5, 125, 4096], P(None, None, ('grid', 'dom')), as said below
- inv_size: float32 [3, 4096], P(None, ('grid', 'dom')), may hold values from 1 to 4
- plus_order: int32 [3, 4096], P(None, ('grid', 'dom')), may hold values from 0 to 127, as said below
- minus_order: int32 [3, 4096], P(None, ('grid', 'dom')), may hold values from 0 to 127, as said below
- donor_cell: int32 [32, 1184], P(('grid', 'dom')), may hold values from 0 to 127
- donor_weights: float32 [32, 3, 5, 1184], P(('grid', 'dom')), as said below
- recv_slot: int32 [32, 600], P(('grid', 'dom')), may hold values from 0 to 1183, as said below
Outputs:
- rhs: float32 [5, 125, 4096], P(None, None, ('grid', 'dom'))
Inputs may be any that keep to these rules, and one draw needn't show every extreme that they name: `plus_order`: within each device's block of 128 columns, every row is a permutation of the local element numbers. `minus_order`: within each device's block of 128 columns, every row is a permutation of the local element numbers. `state`: density lies in [0.9, 1.1], each momentum in [-0.1, 0.1], energy in [2.4, 2.6]. `donor_weights`: for each donor device, direction and slot, the five weights are the Lagrange basis of the five Gauss-Legendre points evaluated at one coordinate in [-0.8, 0.8]. `recv_slot`: entries of one device's row are distinct, and each names a slot whose source device (the slot // 37) lies in another grid than the row's device.
All inputs are finite; a program needn't handle non-finite values.
Results may differ from a plain program's by a relative error of at most 0.0003.
Values sent between devices are 32-bit elements; how exact they have to be, the bound alone decides.
No kernel may reach another device: no remote copies, remote signals or barrier semaphores. Data moves between devices by JAX's collectives and lax.ppermute only.
A program may use at most 64 MiB of HBM per device.

v0:
```python
import math

import jax
import jax.numpy as jnp
from jax import lax
from jax.sharding import PartitionSpec as P

precise = lax.Precision.HIGHEST
volume_forms = ("ia,vabce->vibce", "ib,vabce->vaice", "ic,vabce->vabie")
face_forms = ("a,vabce->vbce", "b,vabce->vace", "c,vabce->vabe")
lift_forms = ("i,vbce->vibce", "i,vace->vaice", "i,vabe->vabie")


def gauss_nodes():
    outer = math.sqrt(5.0 + 2.0 * math.sqrt(10.0 / 7.0)) / 3.0
    inner = math.sqrt(5.0 - 2.0 * math.sqrt(10.0 / 7.0)) / 3.0
    return [-outer, -inner, 0.0, inner, outer]


def basis_value(nodes, column, target_positions):
    value = 1.0
    for other in range(5):
        if other != column:
            value = value * (target_positions - nodes[other]) / (nodes[column] - nodes[other])
    return value


def basis_slope(nodes, column, target_positions):
    total = 0.0
    for skipped in range(5):
        if skipped != column:
            value = 1.0 / (nodes[column] - nodes[skipped])
            for other in range(5):
                if other != column and other != skipped:
                    value = (
                        value * (target_positions - nodes[other]) / (nodes[column] - nodes[other])
                    )
            total = total + value
    return total


def legendre_slopes(target_positions):
    values = [1.0, target_positions]
    slopes = [0.0, 1.0]
    for order in range(1, 5):
        values.append(
            ((2 * order + 1) * target_positions * values[order] - order * values[order - 1])
            / (order + 1)
        )
        slopes.append(slopes[order - 1] + (2 * order + 1) * values[order])
    return (slopes[4], slopes[5])


def tables():
    nodes = gauss_nodes()
    deriv = [[basis_slope(nodes, column, nodes[row]) for column in range(5)] for row in range(5)]
    lower = [basis_value(nodes, column, -1.0) for column in range(5)]
    upper = [basis_value(nodes, column, 1.0) for column in range(5)]
    lift_low = []
    lift_high = []
    for row in range(5):
        slope_four, slope_five = legendre_slopes(nodes[row])
        lift_low.append(-0.5 * (slope_five - slope_four))
        lift_high.append(0.5 * (slope_five + slope_four))
    return tuple(
        (jnp.asarray(matrix, jnp.float32) for matrix in (deriv, lower, upper, lift_low, lift_high))
    )


def euler_flux(state, direction):
    density = state[0]
    momenta = state[1:4]
    energy = state[4]
    speed = momenta[direction] / density
    pressure = 0.4 * (energy - 0.5 * jnp.sum(momenta * momenta, axis=0) / density)
    pieces = [
        momenta[direction],
        momenta[0] * speed,
        momenta[1] * speed,
        momenta[2] * speed,
        (energy + pressure) * speed,
    ]
    pieces[1 + direction] = pieces[1 + direction] + pressure
    sound = jnp.sqrt(1.4 * pressure / density)
    return (jnp.stack(pieces), jnp.abs(speed) + sound)


def common_flux(left_state, right_state, direction):
    left_flux, left_wave = euler_flux(left_state, direction)
    right_flux, right_wave = euler_flux(right_state, direction)
    wave = jnp.maximum(left_wave, right_wave)
    return 0.5 * (left_flux + right_flux) - 0.5 * wave * (right_state - left_state)


def remote_fluxes(left_states, right_states):
    return jnp.stack(
        [
            common_flux(left_states[direction], right_states[direction], direction)
            for direction in range(3)
        ]
    )


def slot_states(state, plus_rows, minus_rows):
    deriv, lower, upper, lift_low, lift_high = tables()
    columns = state.shape[-1]
    grid_form = state.reshape(5, 5, 5, 5, columns)
    high_slots = []
    low_slots = []
    for direction in range(3):
        high_face = jnp.einsum(face_forms[direction], upper, grid_form, precision=precise).reshape(
            5, 25, columns
        )
        low_face = jnp.einsum(face_forms[direction], lower, grid_form, precision=precise).reshape(
            5, 25, columns
        )
        high_slots.append(jnp.take(high_face, plus_rows[direction], axis=2))
        low_slots.append(jnp.take(low_face, minus_rows[direction], axis=2))
    return (jnp.stack(high_slots), jnp.stack(low_slots))


def interpolate(state, cells, weights, blocks):
    block_width = cells.shape[0] // blocks

    def one_block(index):
        block_cells = lax.dynamic_slice_in_dim(cells, index * block_width, block_width)
        block_weights = lax.dynamic_slice_in_dim(weights, index * block_width, block_width, axis=2)
        gathered = jnp.take(state, block_cells, axis=2).reshape(5, 5, 5, 5, block_width)
        reduced = jnp.einsum("as,vabcs->vbcs", block_weights[0], gathered, precision=precise)
        reduced = jnp.einsum("bs,vbcs->vcs", block_weights[1], reduced, precision=precise)
        return jnp.einsum("cs,vcs->vs", block_weights[2], reduced, precision=precise)

    values = lax.map(one_block, jnp.arange(blocks, dtype=jnp.int32))
    return jnp.transpose(values, (1, 0, 2)).reshape(5, blocks * block_width)


def inverse_order(rows):
    count = rows.shape[0]
    return jnp.zeros((count,), jnp.int32).at[rows].set(jnp.arange(count, dtype=jnp.int32))


def assemble(high_slots, low_slots, remote_plus, remote_minus, fringe, plus_rows, minus_rows):
    remote = remote_plus.shape[-1]
    start = remote + fringe.shape[-1]
    plus_parts = []
    minus_parts = []
    for direction in range(3):
        local_flux = common_flux(
            high_slots[direction][:, :, start:], low_slots[direction][:, :, start:], direction
        )
        fringe_high = common_flux(
            high_slots[direction][:, :, remote:start], fringe[direction, 1], direction
        )
        fringe_low = common_flux(
            fringe[direction, 0], low_slots[direction][:, :, remote:start], direction
        )
        plus_slots = jnp.concatenate([remote_plus[direction], fringe_high, local_flux], axis=2)
        minus_slots = jnp.concatenate([remote_minus[direction], fringe_low, local_flux], axis=2)
        plus_parts.append(jnp.take(plus_slots, inverse_order(plus_rows[direction]), axis=2))
        minus_parts.append(jnp.take(minus_slots, inverse_order(minus_rows[direction]), axis=2))
    return (jnp.stack(plus_parts), jnp.stack(minus_parts))


def divergence(state, scales, plus_common, minus_common):
    deriv, lower, upper, lift_low, lift_high = tables()
    columns = state.shape[-1]
    grid_form = state.reshape(5, 5, 5, 5, columns)
    total = jnp.zeros_like(grid_form)
    for direction in range(3):
        flux = euler_flux(grid_form, direction)[0]
        inner = jnp.einsum(volume_forms[direction], deriv, flux, precision=precise)
        low_jump = minus_common[direction].reshape(5, 5, 5, columns) - jnp.einsum(
            face_forms[direction], lower, flux, precision=precise
        )
        high_jump = plus_common[direction].reshape(5, 5, 5, columns) - jnp.einsum(
            face_forms[direction], upper, flux, precision=precise
        )
        inner = inner + jnp.einsum(lift_forms[direction], lift_low, low_jump, precision=precise)
        inner = inner + jnp.einsum(lift_forms[direction], lift_high, high_jump, precision=precise)
        total = total + scales[direction] * inner
    return (-total).reshape(5, 125, columns)


def body(state, inv_size, plus_order, minus_order, donor_cell, donor_weights, recv_slot):
    columns = state.shape[-1]
    part_count = lax.axis_size("dom")
    grid_count = lax.axis_size("grid")
    capacity = max(1, columns // (3 * part_count))
    remote = part_count * capacity
    fringe_count = recv_slot.shape[-1] // 150
    high_slots, low_slots = slot_states(state, plus_order, minus_order)
    values = interpolate(state, donor_cell[0], donor_weights[0], grid_count)
    slot_count = values.shape[1] // (grid_count * part_count)
    shaped = values.reshape(5, grid_count, part_count, slot_count)
    arrived = lax.all_to_all(
        lax.all_to_all(shaped, "grid", split_axis=1, concat_axis=1, tiled=True),
        "dom",
        split_axis=2,
        concat_axis=2,
        tiled=True,
    )
    arrived = arrived.reshape(5, grid_count * part_count * slot_count)
    fringe = jnp.take(arrived, recv_slot[0], axis=1)
    fringe = jnp.transpose(fringe.reshape(5, 3, 2, 25, fringe_count), (1, 2, 0, 3, 4))
    own_high = high_slots[..., :remote]
    own_low = low_slots[..., :remote]
    outgoing = own_low.reshape(3, 5, 25, part_count, capacity)
    partner_low = lax.all_to_all(outgoing, "dom", split_axis=3, concat_axis=3, tiled=True).reshape(
        3, 5, 25, remote
    )
    remote_plus = remote_fluxes(own_high, partner_low)
    returned = lax.all_to_all(
        remote_plus.reshape(3, 5, 25, part_count, capacity),
        "dom",
        split_axis=3,
        concat_axis=3,
        tiled=True,
    )
    remote_minus = returned.reshape(3, 5, 25, remote)
    plus_common, minus_common = assemble(
        high_slots, low_slots, remote_plus, remote_minus, fringe, plus_order, minus_order
    )
    return divergence(state, inv_size, plus_common, minus_common)


def solution(mesh):
    return jax.shard_map(
        body,
        mesh=mesh,
        in_specs=(
            P(None, None, ("grid", "dom")),
            P(None, ("grid", "dom")),
            P(None, ("grid", "dom")),
            P(None, ("grid", "dom")),
            P(("grid", "dom"), None),
            P(("grid", "dom"), None, None, None),
            P(("grid", "dom"), None),
        ),
        out_specs=P(None, None, ("grid", "dom")),
        check_vma=False,
    )
```

profile of v0, /device:TPU:0, one launch (start us, length us, event | category | flops | bytes accessed | tf_op | source)
XLA Modules:
  0.0 173.1 jit_solution(3909650818682447656)
XLA Ops:
  0.0 1.2 copy.2418
  1.2 0.9 copy.2752
  2.9 18.1 %while.10 = (s32[]{:T(128)}, f32[4,5,296]{2,1,0:T(8,128)S(1)}, s32[4]{0:T(128)S(1)}, s32[1184]{0:T(1024)S(1)}, f32[5,125,128]{1,0,2:T(8,128)S(1)}, /*index=5*/f3...) while((s32[]{:T(128)}, f32[4,5,296]{2,1,0:T(8,128)S(1)}, ...), condition=%wide.region_8.10_spmd, body=%wide.region_7.9_spmd.sunk | while | flops 600728 | bytes 5664139 | solution.py:133
  4.3 2.0 %gather_fusion = f32[296,5,125]{2,1,0:T(8,128)S(1)} fusion(f32[5,125,128]{1,0,2:T(8,128)S(1)} %get-tuple-element.417, s32[1024]{0:T(1024)S(1)} %pad_clamp_fusion.15), kind=kCustom, calls=%fused_computation.1.clone.1 | custom fusion | bytes 1481184 | tf_op jit(solution)/shard_map/while/body/eval_jaxpr/jit(_take)/gather | solution.py:128
  8.8 2.0 %gather_fusion = f32[296,5,125]{2,1,0:T(8,128)S(1)} fusion(f32[5,125,128]{1,0,2:T(8,128)S(1)} %get-tuple-element.417, s32[1024]{0:T(1024)S(1)} %pad_clamp_fusion.15), kind=kCustom, calls=%fused_computation.1.clone.1 | custom fusion | bytes 1481184 | tf_op jit(solution)/shard_map/while/body/eval_jaxpr/jit(_take)/gather | solution.py:128
  13.4 2.0 %gather_fusion = f32[296,5,125]{2,1,0:T(8,128)S(1)} fusion(f32[5,125,128]{1,0,2:T(8,128)S(1)} %get-tuple-element.417, s32[1024]{0:T(1024)S(1)} %pad_clamp_fusion.15), kind=kCustom, calls=%fused_computation.1.clone.1 | custom fusion | bytes 1481184 | tf_op jit(solution)/shard_map/while/body/eval_jaxpr/jit(_take)/gather | solution.py:128
  17.9 2.0 %gather_fusion = f32[296,5,125]{2,1,0:T(8,128)S(1)} fusion(f32[5,125,128]{1,0,2:T(8,128)S(1)} %get-tuple-element.417, s32[1024]{0:T(1024)S(1)} %pad_clamp_fusion.15), kind=kCustom, calls=%fused_computation.1.clone.1 | custom fusion | bytes 1481184 | tf_op jit(solution)/shard_map/while/body/eval_jaxpr/jit(_take)/gather | solution.py:128
  21.9 4.4 %all-to-all-start.2 = ((f32[4,1,1480]{2,1,0:T(1,128)}), f32[4,1,1480]{2,1,0:T(1,128)}, u32[]{:S(2)}, u32[]{:S(2)}) async-start(f32[4,1,1480]{2,1,0:T(1,128)} %reshape.3714), calls=%async_computation.2 | async-start | bytes 49152 | tf_op jit(solution)/shard_map/all_to_all | solution.py:196
  29.3 0.8 gather_fusion.6
  30.0 0.8 gather_fusion.7
  33.9 0.8 gather_fusion.5
  34.8 0.8 copy.2358
  38.1 1.2 fusion.202
  40.2 0.8 gather_fusion.4
  41.0 0.8 copy.2356
  42.7 0.8 gather_fusion.2
  48.9 1.0 scatter_custom_fusion.4
  52.3 1.0 scatter_custom_fusion.5
  56.9 1.0 scatter_custom_fusion.2
  60.6 0.8 gather_fusion.3
  61.4 0.8 fusion.37
  64.2 1.2 scatter_custom_fusion.1
  66.5 1.0 scatter_custom_fusion.3
  70.5 1.2 fusion.15
  71.7 1.2 fusion.13
  72.9 1.2 fusion.21
  74.2 1.2 fusion.19
  75.4 1.1 scatter_custom_fusion
  77.7 1.2 fusion.208
  78.9 1.2 fusion.207
  80.1 1.4 fusion.23
  81.5 1.4 fusion.17
  82.9 1.1 copy.2359
  84.4 0.8 copy.2401
  87.8 0.8 copy.2350
  91.5 0.8 copy.2380
  104.4 1.8 %fusion.31 = f32[5,25,84]{1,2,0:T(8,128)} fusion(f32[5,25,128]{1,2,0:T(8,128)S(1)} %get-tuple-element.326, f32[5,25,128]{1,2,0:T(8,128)S(1)} %fusion.27, f32[5,25,84]{1,2,0:T(8,128)} %copy-done.24, f32[5,25,84]{1,2,0:T(8,128)} %copy-done.27, f32[25,84]{0,1:T(8,128)} %get-tuple-element.142), kind=kLoop, calls=%fused_computation.257 | loop fusion | flops 52500 | bytes 218400 | tf_op jit(solution)/shard_map/sub | solution.py:92
  106.3 0.8 fusion.33
  107.1 0.8 fusion.35
  109.0 1.4 reduce.23
  111.3 6.9 %all-to-all-start.3 = ((f32[8,1,740]{2,1,0:T(1,128)}), f32[8,1,740]{2,1,0:T(1,128)}, u32[]{:S(2)}, u32[]{:S(2)}) async-start(f32[8,1,740]{2,1,0:T(1,128)} %reshape.3716), calls=%async_computation.3 | async-start | bytes 49152 | tf_op jit(solution)/shard_map/all_to_all | solution.py:195
  118.9 0.9 copy.2360
  119.8 1.0 reshape.3467
  120.8 1.0 copy.2753
  121.8 1.9 %reshape.3718 = f32[8,1,1875]{2,1,0:T(1,128)} reshape(f32[8,5,5,3,25]{4,3,2,1,0:T(4,128)} %bitcast.1064) | data formatting | bytes 120000
  124.7 0.7 copy.2572
  125.5 6.0 %all-to-all-start = ((f32[8,1,1875]{2,1,0:T(1,128)}), f32[8,1,1875]{2,1,0:T(1,128)}, u32[]{:S(2)}, u32[]{:S(2)}) async-start(f32[8,1,1875]{2,1,0:T(1,128)} %reshape.3718), calls=%async_computation | async-start | bytes 122880 | tf_op jit(solution)/shard_map/all_to_all | solution.py:208
  131.5 1.4 reduce.24
  133.4 2.3 %gather_fusion.1 = f32[600,5]{1,0:T(8,128)} fusion(f32[5,1184]{0,1:T(8,128)S(1)} %copy.2424, s32[1024]{0:T(1024)S(1)} %copy-done.75), kind=kCustom, calls=%fused_computation.13 | custom fusion | bytes 26400 | tf_op jit(solution)/shard_map/jit(_take)/gather | solution.py:203
  135.7 1.2 copy.2426
  138.9 1.6 reduce.25
  143.4 0.9 reshape.3720
  144.3 6.0 %all-to-all-start.1 = ((f32[8,1,1875]{2,1,0:T(1,128)}), f32[8,1,1875]{2,1,0:T(1,128)S(1)}, u32[]{:S(2)}, u32[]{:S(2)}) async-start(f32[8,1,1875]{2,1,0:T(1,128)} %reshape.3720), calls=%async_computation.1 | async-start | bytes 122880 | tf_op jit(solution)/shard_map/all_to_all | solution.py:212
  150.6 6.6 %all-to-all-done.1 = f32[8,1,1875]{2,1,0:T(1,128)S(1)} async-done(((f32[8,1,1875]{2,1,0:T(1,128)}), f32[8,1,1875]{2,1,0:T(1,128)S(1)}, u32[]{:S(2)}, u32[]{:S(2)}) %all-to-all-start.1) | async-done | bytes 60032 | tf_op jit(solution)/shard_map/all_to_all | solution.py:212
  157.2 0.8 reduce.26
  158.8 0.9 gather_fusion.12
  160.4 1.0 gather_fusion.13
  162.3 1.0 gather_fusion.10
  164.2 0.9 gather_fusion.9
  166.4 0.9 gather_fusion.11
  168.7 0.9 gather_fusion.8
  170.1 1.2 broadcast_multiply_fusion.1
  171.4 0.9 fusion.7
  172.3 0.8 reshape.3469
  (619 shorter events, 72.5 us)
Async XLA Ops:
  2.9 23.4 %copy-start = (f32[5,125,128]{2,1,0:T(8,128)S(1)}, f32[5,125,128]{2,1,0:T(8,128)}, u32[]{:S(2)}) copy-start(f32[5,125,128]{2,1,0:T(8,128)} %param.18) | copy-start | bytes 960004
  21.0 5.4 %copy-start.86 = (f32[5,1,1,1]{0,1,3,2:T(1,128)S(1)}, f32[5,1,1,1]{0,1,3,2:T(1,128)}, u32[]{:S(2)}) copy-start(f32[5,1,1,1]{0,1,3,2:T(1,128)} %constant.125) | copy-start | bytes 64
  21.9 5.7 %copy-start.85 = (f32[5,1,1,1]{0,1,3,2:T(1,128)S(1)}, f32[5,1,1,1]{0,1,3,2:T(1,128)}, u32[]{:S(2)}) copy-start(f32[5,1,1,1]{0,1,3,2:T(1,128)} %constant.124) | copy-start | bytes 64
  21.9 86.6 %all-to-all-start.2 = ((f32[4,1,1480]{2,1,0:T(1,128)}), f32[4,1,1480]{2,1,0:T(1,128)}, u32[]{:S(2)}, u32[]{:S(2)}) async-start(f32[4,1,1480]{2,1,0:T(1,128)} %reshape.3714), calls=%async_computation.2 | async-start | bytes 49152 | tf_op jit(solution)/shard_map/all_to_all | solution.py:196
  29.3 3.8 %copy-start.77 = (s32[1,600]{1,0:T(1,128)S(1)}, s32[1,600]{1,0:T(1,128)}, u32[]{:S(2)}) copy-start(s32[1,600]{1,0:T(1,128)} %param.24) | copy-start | bytes 7204
  31.2 3.5 %copy-start.5 = (f32[5,25,128]{2,1,0:T(8,128)}, f32[5,25,128]{2,1,0:T(8,128)S(1)}, u32[]{:S(2)}) copy-start(f32[5,25,128]{2,1,0:T(8,128)S(1)} %copy.2395) | copy-start | bytes 192004
  43.6 16.8 %copy-start.32 = (f32[1,5,25,128]{3,0,2,1:T(1,128)S(1)}, f32[1,5,25,128]{3,0,2,1:T(1,128)}, u32[]{:S(2)}) copy-start(f32[1,5,25,128]{3,0,2,1:T(1,128)} %fusion.202) | copy-start | bytes 192004
  43.7 16.8 %copy-start.7 = (f32[5,25,128]{2,1,0:T(8,128)}, f32[5,25,128]{2,1,0:T(8,128)S(1)}, u32[]{:S(2)}) copy-start(f32[5,25,128]{2,1,0:T(8,128)S(1)} %copy.2346) | copy-start | bytes 192004
  45.6 15.7 %copy-start.89 = (pred[128]{0:T(512)(128)(4,1)S(1)}, pred[128]{0:T(512)(128)(4,1)}, u32[]{:S(2)}) copy-start(pred[128]{0:T(512)(128)(4,1)} %get-tuple-element.178) | copy-start | bytes 388
  52.3 16.3 %copy-start.30 = (f32[1,125,128]{2,1,0:T(8,128)S(1)}, f32[1,125,128]{2,1,0:T(8,128)}, u32[]{:S(2)}) copy-start(f32[1,125,128]{2,1,0:T(8,128)} %get-tuple-element.241) | copy-start | bytes 192004
  59.7 9.2 %copy-start.31 = (f32[125,128]{1,0:T(8,128)S(1)}, f32[125,128]{1,0:T(8,128)}, u32[]{:S(2)}) copy-start(f32[125,128]{1,0:T(8,128)} %multiply_reduce_fusion.1) | copy-start | bytes 192004
  71.7 8.4 %copy-start.73 = (f32[5,5,1,1,1]{1,0,4,3,2:T(8,128)S(1)}, f32[5,5,1,1,1]{1,0,4,3,2:T(8,128)}, u32[]{:S(2)}) copy-start(f32[5,5,1,1,1]{1,0,4,3,2:T(8,128)} %constant.123) | copy-start | bytes 304
  78.9 5.1 %copy-start.64 = (f32[1,1,25,40]{3,2,1,0:T(8,128)S(1)}, f32[1,1,25,40]{3,2,1,0:T(8,128)}, u32[]{:S(2)}) copy-start(f32[1,1,25,40]{3,2,1,0:T(8,128)} %get-tuple-element.263) | copy-start | bytes 12004
  78.9 5.2 %copy-start.62 = (f32[1,1,25,40]{3,2,1,0:T(8,128)S(1)}, f32[1,1,25,40]{3,2,1,0:T(8,128)}, u32[]{:S(2)}) copy-start(f32[1,1,25,40]{3,2,1,0:T(8,128)} %get-tuple-element.264) | copy-start | bytes 12004
  78.9 5.3 %copy-start.61 = (f32[1,1,25,40]{3,2,1,0:T(8,128)S(1)}, f32[1,1,25,40]{3,2,1,0:T(8,128)}, u32[]{:S(2)}) copy-start(f32[1,1,25,40]{3,2,1,0:T(8,128)} %get-tuple-element.262) | copy-start | bytes 12004
  78.9 5.4 %copy-start.60 = (f32[1,1,25,40]{3,2,1,0:T(8,128)S(1)}, f32[1,1,25,40]{3,2,1,0:T(8,128)}, u32[]{:S(2)}) copy-start(f32[1,1,25,40]{3,2,1,0:T(8,128)} %get-tuple-element.261) | copy-start | bytes 12004
  78.9 6.3 %copy-start.52 = (f32[5,25,40]{1,2,0:T(8,128)S(1)}, f32[5,25,40]{1,2,0:T(8,128)}, u32[]{:S(2)}) copy-start(f32[5,25,40]{1,2,0:T(8,128)} %constant_dynamic-update-slice_fusion.149) | copy-start | bytes 60004
  80.1 5.4 %copy-start.43 = (f32[25,84]{0,1:T(8,128)S(1)}, f32[25,84]{0,1:T(8,128)}, u32[]{:S(2)}) copy-start(f32[25,84]{0,1:T(8,128)} %fusion.38) | copy-start | bytes 25204
  82.9 4.0 %copy-start.76 = (s32[600]{0:T(1024)S(1)}, s32[600]{0:T(1024)}, u32[]{:S(2)}) copy-start(s32[600]{0:T(1024)} %reduce.16) | copy-start | bytes 7204
  84.0 3.6 %copy-start.67 = (f32[1,1,25,40]{3,2,1,0:T(8,128)S(1)}, f32[1,1,25,40]{3,2,1,0:T(8,128)}, u32[]{:S(2)}) copy-start(f32[1,1,25,40]{3,2,1,0:T(8,128)} %get-tuple-element.259) | copy-start | bytes 12004
  84.0 3.7 %copy-start.66 = (f32[1,1,25,40]{3,2,1,0:T(8,128)S(1)}, f32[1,1,25,40]{3,2,1,0:T(8,128)}, u32[]{:S(2)}) copy-start(f32[1,1,25,40]{3,2,1,0:T(8,128)} %get-tuple-element.258) | copy-start | bytes 12004
  84.2 4.4 %copy-start.65 = (f32[1,1,25,40]{3,2,1,0:T(8,128)S(1)}, f32[1,1,25,40]{3,2,1,0:T(8,128)}, u32[]{:S(2)}) copy-start(f32[1,1,25,40]{3,2,1,0:T(8,128)} %get-tuple-element.257) | copy-start | bytes 12004
  84.3 4.4 %copy-start.63 = (f32[1,1,25,40]{3,2,1,0:T(8,128)S(1)}, f32[1,1,25,40]{3,2,1,0:T(8,128)}, u32[]{:S(2)}) copy-start(f32[1,1,25,40]{3,2,1,0:T(8,128)} %get-tuple-element.256) | copy-start | bytes 12004
  85.2 6.0 %copy-start.59 = (f32[1,1,25,40]{3,2,1,0:T(8,128)S(1)}, f32[1,1,25,40]{3,2,1,0:T(8,128)}, u32[]{:S(2)}) copy-start(f32[1,1,25,40]{3,2,1,0:T(8,128)} %get-tuple-element.268) | copy-start | bytes 12004
  85.2 6.0 %copy-start.58 = (f32[1,1,25,40]{3,2,1,0:T(8,128)S(1)}, f32[1,1,25,40]{3,2,1,0:T(8,128)}, u32[]{:S(2)}) copy-start(f32[1,1,25,40]{3,2,1,0:T(8,128)} %get-tuple-element.269) | copy-start | bytes 12004
  85.3 6.0 %copy-start.57 = (f32[1,1,25,40]{3,2,1,0:T(8,128)S(1)}, f32[1,1,25,40]{3,2,1,0:T(8,128)}, u32[]{:S(2)}) copy-start(f32[1,1,25,40]{3,2,1,0:T(8,128)} %get-tuple-element.267) | copy-start | bytes 12004
  85.5 6.8 %copy-start.56 = (f32[1,1,25,40]{3,2,1,0:T(8,128)S(1)}, f32[1,1,25,40]{3,2,1,0:T(8,128)}, u32[]{:S(2)}) copy-start(f32[1,1,25,40]{3,2,1,0:T(8,128)} %get-tuple-element.266) | copy-start | bytes 12004
  86.0 8.8 %copy-start.46 = (f32[1,5,25,40]{2,3,1,0:T(8,128)S(1)}, f32[1,5,25,40]{2,3,1,0:T(8,128)}, u32[]{:S(2)}) copy-start(f32[1,5,25,40]{2,3,1,0:T(8,128)} %constant_dynamic-update-slice_fusion.29) | copy-start | bytes 60004
  86.7 10.7 %copy-start.42 = (f32[25,84]{0,1:T(8,128)S(1)}, f32[25,84]{0,1:T(8,128)}, u32[]{:S(2)}) copy-start(f32[25,84]{0,1:T(8,128)} %fusion.41) | copy-start | bytes 25204
  86.7 10.9 %copy-start.41 = (f32[25,84]{0,1:T(8,128)S(1)}, f32[25,84]{0,1:T(8,128)}, u32[]{:S(2)}) copy-start(f32[25,84]{0,1:T(8,128)} %fusion.40) | copy-start | bytes 25204
  86.7 4.5 %copy-start.27 = (f32[5,25,84]{1,2,0:T(8,128)}, f32[5,25,84]{1,2,0:T(8,128)S(1)}, u32[]{:S(2)}) copy-start(f32[5,25,84]{1,2,0:T(8,128)S(1)} %constant_dynamic-update-slice_fusion.140) | copy-start | bytes 126004
  86.8 9.3 %copy-start.24 = (f32[5,25,84]{1,2,0:T(8,128)}, f32[5,25,84]{1,2,0:T(8,128)S(1)}, u32[]{:S(2)}) copy-start(f32[5,25,84]{1,2,0:T(8,128)S(1)} %constant_dynamic-update-slice_fusion.135) | copy-start | bytes 126004
  91.5 6.2 %copy-start.16 = (f32[1,1,25,40]{2,3,1,0:T(8,128)}, f32[1,1,25,40]{2,3,1,0:T(8,128)S(1)}, u32[]{:S(2)}) copy-start(f32[1,1,25,40]{2,3,1,0:T(8,128)S(1)} %copy.2570) | copy-start | bytes 12004
  92.3 5.4 %copy-start.18 = (f32[25,40]{0,1:T(8,128)}, f32[25,40]{0,1:T(8,128)S(1)}, u32[]{:S(2)}) copy-start(f32[25,40]{0,1:T(8,128)S(1)} %copy.2380) | copy-start | bytes 12004
  94.9 7.7 %copy-start.40 = (f32[25,84]{0,1:T(8,128)S(1)}, f32[25,84]{0,1:T(8,128)}, u32[]{:S(2)}) copy-start(f32[25,84]{0,1:T(8,128)} %fusion.42) | copy-start | bytes 25204
  95.5 7.2 %copy-start.39 = (f32[25,84]{0,1:T(8,128)S(1)}, f32[25,84]{0,1:T(8,128)}, u32[]{:S(2)}) copy-start(f32[25,84]{0,1:T(8,128)} %fusion.43) | copy-start | bytes 25204
  96.8 6.2 %copy-start.2 = (f32[5,25,128]{1,2,0:T(8,128)S(1)}, f32[5,25,128]{1,2,0:T(8,128)}, u32[]{:S(2)}) copy-start(f32[5,25,128]{1,2,0:T(8,128)} %copy-done.1) | copy-start | bytes 192004
  99.3 3.9 %copy-start.95 = (f32[3,128]{1,0:T(4,128)S(1)}, f32[3,128]{1,0:T(4,128)}, u32[]{:S(2)}) copy-start(f32[3,128]{1,0:T(4,128)} %param.19) | copy-start | bytes 4612
  99.3 4.5 %copy-start.102 = (s32[128]{0:T(128)S(1)}, s32[128]{0:T(128)}, u32[]{:S(2)}) copy-start(s32[128]{0:T(128)} %compare_select_fusion.4) | copy-start | bytes 1540
  99.3 4.5 %copy-start.105 = (s32[128]{0:T(128)S(1)}, s32[128]{0:T(128)}, u32[]{:S(2)}) copy-start(s32[128]{0:T(128)} %compare_select_fusion.3) | copy-start | bytes 1540
  99.3 5.1 %copy-start.22 = (f32[5,25,128]{2,1,0:T(8,128)S(1)}, f32[5,25,128]{2,1,0:T(8,128)}, u32[]{:S(2)}) copy-start(f32[5,25,128]{2,1,0:T(8,128)} %copy.2358) | copy-start | bytes 192004
  99.3 5.1 %copy-start.23 = (f32[5,25,128]{2,1,0:T(8,128)S(1)}, f32[5,25,128]{2,1,0:T(8,128)}, u32[]{:S(2)}) copy-start(f32[5,25,128]{2,1,0:T(8,128)} %copy.2356) | copy-start | bytes 192004
  104.4 3.4 %copy-start.103 = (s32[128]{0:T(128)S(1)}, s32[128]{0:T(128)}, u32[]{:S(2)}) copy-start(s32[128]{0:T(128)} %compare_select_fusion.6) | copy-start | bytes 1540
  106.3 12.0 %copy-start.104 = (s32[128]{0:T(128)S(1)}, s32[128]{0:T(128)}, u32[]{:S(2)}) copy-start(s32[128]{0:T(128)} %compare_select_fusion.7) | copy-start | bytes 1540
  106.3 12.0 %copy-start.107 = (s32[128]{0:T(128)S(1)}, s32[128]{0:T(128)}, u32[]{:S(2)}) copy-start(s32[128]{0:T(128)} %compare_select_fusion.8) | copy-start | bytes 1540
  110.5 13.2 %copy-start.6 = (f32[5,25,128]{2,1,0:T(8,128)S(1)}, f32[5,25,128]{2,1,0:T(8,128)}, u32[]{:S(2)}) copy-start(f32[5,25,128]{2,1,0:T(8,128)} %copy-done.5) | copy-start | bytes 192004
  110.6 13.9 %copy-start.55 = (pred[3,2,25,4]{3,2,1,0:T(8,128)(4,1)S(1)}, pred[3,2,25,4]{3,2,1,0:T(8,128)(4,1)}, u32[]{:S(2)}) copy-start(pred[3,2,25,4]{3,2,1,0:T(8,128)(4,1)} %compare_and_fusion.1) | copy-start | bytes 1804
  110.6 14.0 %copy-start.8 = (f32[5,25,128]{2,1,0:T(8,128)S(1)}, f32[5,25,128]{2,1,0:T(8,128)}, u32[]{:S(2)}) copy-start(f32[5,25,128]{2,1,0:T(8,128)} %copy-done.7) | copy-start | bytes 192004
  111.3 14.1 %all-to-all-start.3 = ((f32[8,1,740]{2,1,0:T(1,128)}), f32[8,1,740]{2,1,0:T(1,128)}, u32[]{:S(2)}, u32[]{:S(2)}) async-start(f32[8,1,740]{2,1,0:T(1,128)} %reshape.3716), calls=%async_computation.3 | async-start | bytes 49152 | tf_op jit(solution)/shard_map/all_to_all | solution.py:195
  118.9 5.9 %copy-start.10 = (f32[5,25,128]{2,1,0:T(8,128)S(1)}, f32[5,25,128]{2,1,0:T(8,128)}, u32[]{:S(2)}) copy-start(f32[5,25,128]{2,1,0:T(8,128)} %copy-done.9) | copy-start | bytes 192004
  120.8 12.6 %copy-start.75 = (s32[1024]{0:T(1024)S(1)}, s32[1024]{0:T(1024)}, u32[]{:S(2)}) copy-start(s32[1024]{0:T(1024)} %get-tuple-element.334) | copy-start | bytes 12292
  121.8 15.1 %copy-start.81 = (f32[25,4]{0,1:T(4,128)S(1)}, f32[25,4]{0,1:T(4,128)}, u32[]{:S(2)}) copy-start(f32[25,4]{0,1:T(4,128)} %fusion.115) | copy-start | bytes 1204
  121.8 15.2 %copy-start.78 = (f32[25,4]{0,1:T(4,128)S(1)}, f32[25,4]{0,1:T(4,128)}, u32[]{:S(2)}) copy-start(f32[25,4]{0,1:T(4,128)} %fusion.116) | copy-start | bytes 1204
  121.8 15.2 %copy-start.79 = (f32[25,4]{0,1:T(4,128)S(1)}, f32[25,4]{0,1:T(4,128)}, u32[]{:S(2)}) copy-start(f32[25,4]{0,1:T(4,128)} %fusion.119) | copy-start | bytes 1204
  121.8 15.4 %copy-start.82 = (f32[25,4]{0,1:T(4,128)S(1)}, f32[25,4]{0,1:T(4,128)}, u32[]{:S(2)}) copy-start(f32[25,4]{0,1:T(4,128)} %fusion.124) | copy-start | bytes 1204
  123.7 13.5 %copy-start.80 = (f32[25,4]{0,1:T(4,128)S(1)}, f32[25,4]{0,1:T(4,128)}, u32[]{:S(2)}) copy-start(f32[25,4]{0,1:T(4,128)} %fusion.120) | copy-start | bytes 1204
  125.5 13.4 %all-to-all-start = ((f32[8,1,1875]{2,1,0:T(1,128)}), f32[8,1,1875]{2,1,0:T(1,128)}, u32[]{:S(2)}, u32[]{:S(2)}) async-start(f32[8,1,1875]{2,1,0:T(1,128)} %reshape.3718), calls=%async_computation | async-start | bytes 122880 | tf_op jit(solution)/shard_map/all_to_all | solution.py:208
  142.9 7.6 %copy-start.54 = (f32[5,25,40]{1,2,0:T(8,128)S(1)}, f32[5,25,40]{1,2,0:T(8,128)}, u32[]{:S(2)}) copy-start(f32[5,25,40]{1,2,0:T(8,128)} %copy-done.53) | copy-start | bytes 60004
  143.0 7.5 %copy-start.49 = (f32[5,25,40]{1,2,0:T(8,128)S(1)}, f32[5,25,40]{1,2,0:T(8,128)}, u32[]{:S(2)}) copy-start(f32[5,25,40]{1,2,0:T(8,128)} %constant_dynamic-update-slice_fusion.100) | copy-start | bytes 60004
  143.0 7.6 %copy-start.45 = (f32[5,25,40]{1,2,0:T(8,128)S(1)}, f32[5,25,40]{1,2,0:T(8,128)}, u32[]{:S(2)}) copy-start(f32[5,25,40]{1,2,0:T(8,128)} %constant_dynamic-update-slice_fusion.55) | copy-start | bytes 60004
  144.3 12.9 %all-to-all-start.1 = ((f32[8,1,1875]{2,1,0:T(1,128)}), f32[8,1,1875]{2,1,0:T(1,128)S(1)}, u32[]{:S(2)}, u32[]{:S(2)}) async-start(f32[8,1,1875]{2,1,0:T(1,128)} %reshape.3720), calls=%async_computation.1 | async-start | bytes 122880 | tf_op jit(solution)/shard_map/all_to_all | solution.py:212
  150.5 8.0 %copy-start.15 = (f32[5,25,84]{1,2,0:T(8,128)S(1)}, f32[5,25,84]{1,2,0:T(8,128)}, u32[]{:S(2)}) copy-start(f32[5,25,84]{1,2,0:T(8,128)} %fusion.31) | copy-start | bytes 126004
  150.5 8.0 %copy-start.71 = (f32[5,25,4]{1,2,0:T(4,128)S(1)}, f32[5,25,4]{1,2,0:T(4,128)}, u32[]{:S(2)}) copy-start(f32[5,25,4]{1,2,0:T(4,128)} %get-tuple-element.283) | copy-start | bytes 6004
  150.5 8.0 %copy-start.72 = (f32[5,25,4]{1,2,0:T(4,128)S(1)}, f32[5,25,4]{1,2,0:T(4,128)}, u32[]{:S(2)}) copy-start(f32[5,25,4]{1,2,0:T(4,128)} %get-tuple-element.284) | copy-start | bytes 6004
  (48 other events, 78.0 us)
where the time goes:
time: 174 us; the launch traced here: 173 us
  local copies, waits for them, and re-layouts  72.3 us (42%)
  other arithmetic  50.5 us (29%)
  starting transfers between devices  23.3 us (13%)
  matrix products  14.9 us (9%)
  waiting for transfers between devices  6.57 us (4%)
  loops' own time  3.06 us (2%)
  between operations  2.57 us (1%)
    unnamed x256, local copies, waits for them, and re-layouts  16.2 us
    gather x12, local copies, waits for them, and re-layouts, one_block(): jnp.take(state, block_cells, axis=2).reshape(5, 5, 5, 5, block_width)  10.4 us
    unnamed x89, other arithmetic  10.1 us
    reduce_sum x18, other arithmetic, euler_flux(): jnp.sum(momenta * momenta, axis=0)  9.07 us
    all_to_all x1, starting transfers between devices, body(): lax.all_to_all(lax.all_to_all(shaped, 'grid', split_axis=1, concat_axis=1...  6.91 us
    all_to_all x1, waiting for transfers between devices, body(): lax.all_to_all(remote_plus.reshape(3, 5, 25, part_count, capacity), 'dom'...  6.56 us
    scatter x6, local copies, waits for them, and re-layouts, inverse_order(): jnp.zeros((count,), jnp.int32).at[rows]  6.15 us
    all_to_all x1, starting transfers between devices, body(): lax.all_to_all(remote_plus.reshape(3, 5, 25, part_count, capacity), 'dom'...  6 us
  transfers between devices with their start and end apart: 4, of which 1 were waited for; matrix products, arithmetic and copies ran while one was open for 54% of the time, Pallas kernels for 0%

commit v1 on v0

v1 whole, which is shorter than its diff:
```python
import functools
import math

import jax
import jax.numpy as jnp
import numpy as np
from jax import lax
from jax.experimental import pallas as pl
from jax.experimental.pallas import tpu as pltpu
from jax.sharding import PartitionSpec as P

precise = lax.Precision.HIGHEST
LANES = 128
ROWS = 32
VMEM = 48 * 1024 * 1024


def gauss_nodes():
    outer = math.sqrt(5.0 + 2.0 * math.sqrt(10.0 / 7.0)) / 3.0
    inner = math.sqrt(5.0 - 2.0 * math.sqrt(10.0 / 7.0)) / 3.0
    return [-outer, -inner, 0.0, inner, outer]


def basis_value(nodes, column, target):
    value = 1.0
    for other in range(5):
        if other != column:
            value = value * (target - nodes[other]) / (nodes[column] - nodes[other])
    return value


def basis_slope(nodes, column, target):
    total = 0.0
    for skipped in range(5):
        if skipped != column:
            value = 1.0 / (nodes[column] - nodes[skipped])
            for other in range(5):
                if other != column and other != skipped:
                    value = value * (target - nodes[other]) / (nodes[column] - nodes[other])
            total = total + value
    return total


def legendre_slopes(target):
    values = [1.0, target]
    slopes = [0.0, 1.0]
    for order in range(1, 5):
        values.append(
            ((2 * order + 1) * target * values[order] - order * values[order - 1]) / (order + 1)
        )
        slopes.append(slopes[order - 1] + (2 * order + 1) * values[order])
    return (slopes[4], slopes[5])


def tables():
    nodes = gauss_nodes()
    deriv = [[basis_slope(nodes, column, nodes[row]) for column in range(5)] for row in range(5)]
    lower = [basis_value(nodes, column, -1.0) for column in range(5)]
    upper = [basis_value(nodes, column, 1.0) for column in range(5)]
    lift_low = []
    lift_high = []
    for row in range(5):
        slope_four, slope_five = legendre_slopes(nodes[row])
        lift_low.append(-0.5 * (slope_five - slope_four))
        lift_high.append(0.5 * (slope_five + slope_four))
    return tuple(np.asarray(m, np.float64) for m in (deriv, lower, upper, lift_low, lift_high))


def split_point(point, direction):
    index = [point // 25, point // 5 % 5, point % 5]
    along = index.pop(direction)
    return along, 5 * index[0] + index[1]


def matrices():
    deriv, lower, upper, lift_low, lift_high = tables()
    faces = np.zeros((6 * ROWS, 125))
    volume = np.zeros((125, 3 * LANES))
    lift = np.zeros((125, 6 * ROWS))
    own = deriv - np.outer(lift_low, lower) - np.outer(lift_high, upper)
    for d in range(3):
        for p in range(125):
            i, t = split_point(p, d)
            faces[(2 * d) * ROWS + t, p] = lower[i]
            faces[(2 * d + 1) * ROWS + t, p] = upper[i]
            lift[p, (2 * d) * ROWS + t] = -lift_low[i]
            lift[p, (2 * d + 1) * ROWS + t] = -lift_high[i]
            for other in range(125):
                m, line = split_point(other, d)
                if line == t:
                    volume[p, d * LANES + other] = -own[i, m]
    for k in range(6):
        faces[k * ROWS + 25 : (k + 1) * ROWS] = faces[k * ROWS + 24]
    expand = np.zeros((3 * LANES, 15))
    for p in range(125):
        for axis, index in enumerate((p // 25, p // 5 % 5, p % 5)):
            expand[axis * LANES + p, 5 * axis + index] = 1.0
    return tuple(m.astype(np.float32) for m in (faces, volume, lift, expand))


def partner(index, step, count):
    if count & (count - 1) == 0:
        return index ^ step
    return (index + step) % count


def lane_gather(values, index):
    return jnp.take_along_axis(values, index, axis=1, mode="promise_in_bounds")


def euler(state, direction):
    density, momenta, energy = state[0], state[1:4], state[4]
    inverse = 1.0 / density
    speed = momenta[direction] * inverse
    squares = momenta[0] * momenta[0] + momenta[1] * momenta[1] + momenta[2] * momenta[2]
    pressure = 0.4 * (energy - 0.5 * squares * inverse)
    flux = [
        momenta[direction],
        momenta[0] * speed,
        momenta[1] * speed,
        momenta[2] * speed,
        (energy + pressure) * speed,
    ]
    flux[1 + direction] = flux[1 + direction] + pressure
    return flux, speed, pressure, inverse


def euler_wave(state, direction):
    flux, speed, pressure, inverse = euler(state, direction)
    return flux, jnp.abs(speed) + jnp.sqrt(1.4 * pressure * inverse)


def mix(left, left_flux, left_wave, right, right_flux, right_wave):
    wave = 0.5 * jnp.maximum(left_wave, right_wave)
    return [
        0.5 * (left_flux[v] + right_flux[v]) - wave * (right[v] - left[v]) for v in range(5)
    ]


def donor_kernel(
    grids, parts, count, state_ref, cell_ref, weight_ref, expand_ref, *refs
):
    outs = refs[: grids - 1]
    cells, weights, values, windows = refs[grids - 1 :]
    total = grids * parts * count
    blocks = cells.shape[1] // LANES
    cells[...] = jnp.zeros_like(cells)
    weights[...] = jnp.zeros_like(weights)
    cells[0:1, :total] = cell_ref[...]
    for k in range(15):
        weights[k : k + 1, :total] = weight_ref[k]
    expand = expand_ref[...]
    for block in range(blocks):
        lanes = slice(block * LANES, (block + 1) * LANES)
        wide = jnp.dot(
            expand, weights[:15, lanes], precision=precise, preferred_element_type=jnp.float32
        )
        weight = (wide[:LANES] * wide[LANES : 2 * LANES] * wide[2 * LANES :])[:125]
        index = jnp.broadcast_to(cells[0:1, lanes], (125, LANES))
        for v in range(5):
            picked = lane_gather(state_ref[v], index)
            values[v : v + 1, lanes] = jnp.sum(picked * weight, axis=0, keepdims=True)
    lane = lax.broadcasted_iota(jnp.int32, (8, LANES), 1)
    me = lax.axis_index("grid")
    for step in range(1, grids):
        wanted = (lane >= (step - 1) * count) & (lane < step * count)
        for g in range(grids):

            @pl.when(partner(me, step, grids) == g)
            def _():
                for q in range(parts):
                    start = (g * parts + q) * count
                    block = start // LANES
                    width = 2 * LANES if block + 1 < blocks else LANES
                    pair = values[:, block * LANES : block * LANES + width]
                    shift = ((step - 1) * count - (start - block * LANES)) % width
                    moved = pltpu.roll(pair, shift, 1)[:, :LANES] if shift else pair[:, :LANES]
                    outs[step - 1][q] = jnp.where(wanted, moved, 0.0)


def face_kernel(
    parts, capacity, rows, state_ref, plus_ref, minus_ref, faces_ref, lanes_ref, slots_ref, pay_ref, turn
):
    wide = jnp.concatenate([state_ref[v] for v in range(5)], axis=1)
    face = jnp.dot(
        faces_ref[...], wide, precision=precise, preferred_element_type=jnp.float32
    )
    to_slot = lanes_ref[...]
    turn[120:128, :] = jnp.zeros((8, LANES), jnp.float32)
    for k in range(6):
        order = (minus_ref, plus_ref)[k % 2][k // 2 : k // 2 + 1, :]
        index = lane_gather(jnp.broadcast_to(order, (8, LANES)), to_slot)
        index = jnp.concatenate([index] * (ROWS // 8), axis=0)
        for v in range(5):
            block = face[k * ROWS : (k + 1) * ROWS, v * LANES : (v + 1) * LANES]
            picked = lane_gather(block, index)
            slots_ref[k, v] = picked
            turn[25 * v : 25 * v + 25, :] = picked[:25]
        turned = turn[...].T
        for s in range(capacity):
            pay_ref[pl.ds(k * capacity + s, parts, stride=rows), :] = turned[
                s * parts : (s + 1) * parts
            ]


def volume_kernel(
    grids,
    parts,
    count,
    state_ref,
    size_ref,
    plus_ref,
    minus_ref,
    recv_ref,
    slots_ref,
    volume_ref,
    lanes_ref,
    part_ref,
    flux_ref,
    local_ref,
    back_ref,
    where_ref,
    wide,
    index,
):
    state = [state_ref[v] for v in range(5)]
    for d in range(3):
        flux = euler(state, d)[0]
        scale = size_ref[d : d + 1, :]
        wide[d * LANES + 120 : (d + 1) * LANES, :] = jnp.zeros((8, 5 * LANES), jnp.float32)
        for v in range(5):
            wide[d * LANES : d * LANES + 125, v * LANES : (v + 1) * LANES] = flux[v] * scale
    part_ref[...] = jnp.dot(
        volume_ref[...], wide[...], precision=precise, preferred_element_type=jnp.float32
    )
    for d in range(3):
        low = [slots_ref[2 * d, v] for v in range(5)]
        high = [slots_ref[2 * d + 1, v] for v in range(5)]
        low_flux, low_wave = euler_wave(low, d)
        high_flux, high_wave = euler_wave(high, d)
        local = mix(high, high_flux, high_wave, low, low_flux, low_wave)
        for v in range(5):
            flux_ref[2 * d, v] = low_flux[v]
            flux_ref[2 * d + 1, v] = high_flux[v]
            local_ref[d, v] = local[v]
        flux_ref[2 * d, 5] = low_wave
        flux_ref[2 * d + 1, 5] = high_wave
    to_slot = lanes_ref[...]
    rank = lax.broadcasted_iota(jnp.int32, (LANES, LANES), 0)
    lane = lax.broadcasted_iota(jnp.int32, (LANES, LANES), 1)
    index[...] = jnp.zeros_like(index)
    for k in range(6):
        order = (minus_ref, plus_ref)[k % 2][k // 2 : k // 2 + 1, :]
        order = lane_gather(jnp.broadcast_to(order, (8, LANES)), to_slot)
        index[k : k + 1, :] = order[0:1].astype(jnp.float32)
    turned = index[...].T.astype(jnp.int32)
    back_ref[...] = jnp.zeros_like(back_ref)
    for k in range(6):
        found = jnp.where(turned[:, k : k + 1] == lane, rank, 0)
        back_ref[k : k + 1, :] = jnp.sum(found, axis=0, keepdims=True)
    me = lax.axis_index("grid")
    points = recv_ref.shape[1] // 6
    where_ref[...] = jnp.zeros_like(where_ref)
    for k in range(6):
        slot = recv_ref[:, k * points : (k + 1) * points]
        device = ((slot.astype(jnp.float32) + 0.5) * (1.0 / count)).astype(jnp.int32)
        rest = slot - device * count
        grid = ((device.astype(jnp.float32) + 0.5) * (1.0 / parts)).astype(jnp.int32)
        step = jnp.zeros_like(grid)
        for g in range(grids):
            if grids & (grids - 1) == 0:
                away = me ^ g
            else:
                away = lax.rem(me + grids - g, grids)
            step = jnp.where(grid == g, away, step)
        where_ref[0, k : k + 1, :points] = device - grid * parts
        where_ref[1, k : k + 1, :points] = jnp.maximum(step - 1, 0) * count + rest


def finish_kernel(
    parts,
    capacity,
    rows,
    first,
    fringes,
    come_ref,
    slots_ref,
    flux_ref,
    local_ref,
    back_ref,
    where_ref,
    part_ref,
    size_ref,
    lift_ref,
    out_ref,
    turn,
    turned,
    wide,
):
    remote = parts * capacity
    row = lax.broadcasted_iota(jnp.int32, (ROWS, LANES), 0)
    lane = lax.broadcasted_iota(jnp.int32, (ROWS, LANES), 1)
    is_remote = (lane < remote) & (row < 25)
    is_outer = lane < remote + fringes
    spread = jnp.clip(jnp.minimum(row, 24) * fringes + lane - remote, 0, LANES - 1)
    source = where_ref[0]
    place = where_ref[1]
    fringe = []
    for v in range(5):
        sent = come_ref[pl.ds(first + v, parts, stride=rows), :]
        total = jnp.zeros((8, LANES), jnp.float32)
        for q in range(parts):
            picked = lane_gather(jnp.broadcast_to(sent[q : q + 1], (8, LANES)), place)
            total = jnp.where(source == q, picked, total)
        fringe.append(total)
    turn[...] = jnp.zeros_like(turn)
    turned[LANES:, :] = jnp.zeros((8, LANES), jnp.float32)
    for k in range(6):
        d = k // 2
        other = k ^ 1
        for s in range(capacity):
            turn[s * parts : (s + 1) * parts, :] = come_ref[
                pl.ds(other * capacity + s, parts, stride=rows), :
            ]
        turned[:LANES, :] = turn[...].T
        own = [slots_ref[k, v] for v in range(5)]
        theirs = []
        for v in range(5):
            outer = lane_gather(jnp.broadcast_to(fringe[v][k : k + 1], (ROWS, LANES)), spread)
            outer = jnp.where(is_outer, outer, slots_ref[other, v])
            theirs.append(jnp.where(is_remote, turned[25 * v : 25 * v + ROWS, :], outer))
        their_flux, their_wave = euler_wave(theirs, d)
        own_flux = [flux_ref[k, v] for v in range(5)]
        own_wave = flux_ref[k, 5]
        if k % 2:
            common = mix(own, own_flux, own_wave, theirs, their_flux, their_wave)
        else:
            common = mix(theirs, their_flux, their_wave, own, own_flux, own_wave)
        index = jnp.broadcast_to(back_ref[k : k + 1, :], (ROWS, LANES))
        scale = size_ref[d : d + 1, :]
        for v in range(5):
            value = jnp.where(is_outer, common[v], local_ref[d, v])
            wide[k * ROWS : (k + 1) * ROWS, v * LANES : (v + 1) * LANES] = (
                lane_gather(value, index) * scale
            )
    total = part_ref[...] + jnp.dot(
        lift_ref[...], wide[...], precision=precise, preferred_element_type=jnp.float32
    )
    for v in range(5):
        out_ref[v] = total[:, v * LANES : (v + 1) * LANES]


def call(kernel, name, out_shape, scratch, flops, size, *operands):
    return pl.pallas_call(
        kernel,
        name=name,
        out_shape=out_shape,
        scratch_shapes=scratch,
        compiler_params=pltpu.CompilerParams(vmem_limit_bytes=VMEM),
        cost_estimate=pl.CostEstimate(flops=flops, bytes_accessed=size, transcendentals=0),
    )(*operands)


def body(state, inv_size, plus_order, minus_order, donor_cell, donor_weights, recv_slot):
    columns = state.shape[-1]
    parts = lax.axis_size("dom")
    grids = lax.axis_size("grid")
    capacity = max(1, columns // (3 * parts))
    remote = parts * capacity
    fringes = recv_slot.shape[-1] // 150
    total = donor_cell.shape[-1]
    count = total // (grids * parts)
    padded = -(-total // LANES) * LANES
    first = -(-6 * capacity // 8) * 8
    rows = first + 8
    faces, volume, lift, expand = matrices()
    lanes = np.arange(LANES)
    lanes[:remote] = (lanes[:remote] % parts) * capacity + lanes[:remote] // parts
    lanes = np.ascontiguousarray(np.broadcast_to(lanes.astype(np.int32), (8, LANES)))
    f32 = functools.partial(jax.ShapeDtypeStruct, dtype=jnp.float32)
    i32 = functools.partial(jax.ShapeDtypeStruct, dtype=jnp.int32)

    sent = call(
        functools.partial(donor_kernel, grids, parts, count),
        "donors",
        tuple(f32((parts, 8, LANES)) for _ in range(grids - 1)),
        [
            pltpu.VMEM((8, padded), jnp.int32),
            pltpu.VMEM((16, padded), jnp.float32),
            pltpu.VMEM((8, padded), jnp.float32),
            pltpu.VMEM((8, LANES), jnp.float32),
        ],
        5_000_000,
        500_000,
        state,
        donor_cell,
        donor_weights.reshape(15, 1, total),
        expand,
    )
    arrived = [
        lax.ppermute(sent[step - 1], "grid", [(g, partner(g, step, grids)) for g in range(grids)])
        for step in range(1, grids)
    ]
    slots, pay = call(
        functools.partial(face_kernel, parts, capacity, rows),
        "faces",
        (f32((6, 5, ROWS, LANES)), f32((parts * rows, LANES))),
        [pltpu.VMEM((LANES, LANES), jnp.float32)],
        200_000_000,
        1_500_000,
        state,
        plus_order,
        minus_order,
        faces,
        lanes,
    )
    merged = arrived[0]
    for extra in arrived[1:]:
        merged = merged + extra
    pay = lax.dynamic_update_slice(pay.reshape(parts, rows, LANES), merged, (0, first, 0))
    come = lax.all_to_all(pay, "dom", split_axis=0, concat_axis=0, tiled=True)
    part, flux, local, back, where = call(
        functools.partial(volume_kernel, grids, parts, count),
        "volume",
        (
            f32((125, 5 * LANES)),
            f32((6, 6, ROWS, LANES)),
            f32((3, 5, ROWS, LANES)),
            i32((8, LANES)),
            i32((2, 8, LANES)),
        ),
        [pltpu.VMEM((3 * LANES, 5 * LANES), jnp.float32), pltpu.VMEM((LANES, LANES), jnp.float32)],
        400_000_000,
        3_000_000,
        state,
        inv_size,
        plus_order,
        minus_order,
        recv_slot,
        slots,
        volume,
        lanes,
    )
    return call(
        functools.partial(finish_kernel, parts, capacity, rows, first, fringes),
        "finish",
        f32((5, 125, columns)),
        [
            pltpu.VMEM((LANES, LANES), jnp.float32),
            pltpu.VMEM((LANES + 8, LANES), jnp.float32),
            pltpu.VMEM((6 * ROWS, 5 * LANES), jnp.float32),
        ],
        200_000_000,
        3_000_000,
        come.reshape(parts * rows, LANES),
        slots,
        flux,
        local,
        back,
        where,
        part,
        inv_size,
        lift,
    )


def solution(mesh):
    return jax.shard_map(
        body,
        mesh=mesh,
        in_specs=(
            P(None, None, ("grid", "dom")),
            P(None, ("grid", "dom")),
            P(None, ("grid", "dom")),
            P(None, ("grid", "dom")),
            P(("grid", "dom"), None),
            P(("grid", "dom"), None, None, None),
            P(("grid", "dom"), None),
        ),
        out_specs=P(None, None, ("grid", "dom")),
        check_vma=False,
    )
```

time: 174 us -> 28.7 us (0.16)
  local copies, waits for them, and re-layouts: 72.3 us -> 3.52 us
  other arithmetic: 50.5 us -> 0.62 us
  matrix products: 14.9 us -> 0 us
  starting transfers between devices: 23.3 us -> 9.12 us
  Pallas kernels: 0 us -> 6.49 us
  loops' own time: 3.06 us -> 0 us
  between operations: 2.57 us -> 0.09 us
  waiting for transfers between devices: 6.57 us -> 8.5 us
    gather x26 -> x0, local copies, waits for them, and re-layouts: 24 us -> none  [the longest x12 10.4 us: one_block(): jnp.take(state, block_cells, axis=2).reshape(5, 5, 5, 5, block_width)]
    all_to_all x4 -> x1, starting transfers between devices: 23.3 us -> 5.94 us  [body(): come = lax.all_to_all(pay, 'dom', split_axis=0, concat_axis=0, tiled=True)]
    dot_general x15 -> x0, matrix products: 14.9 us -> none  [the longest x3 3.65 us: divergence(): inner = jnp.einsum(volume_forms[direction], deriv, flux, precision=precise)]
    unnamed x256 -> x26, local copies, waits for them, and re-layouts: 16.2 us -> 3.52 us
    unnamed x89 -> x0, other arithmetic: 10.1 us -> none
    reduce_sum x18 -> x0, other arithmetic: 9.07 us -> none  [euler_flux(): jnp.sum(momenta * momenta, axis=0)]
    select_n x20 -> x0, other arithmetic: 6.57 us -> none  [the longest x6 2.36 us: assemble(): jnp.take(minus_slots, inverse_order(minus_rows[direction]), axis=2)]
    pallas_call x0 -> x4, Pallas kernels: none -> 6.49 us  [call(): pl.pallas_call(kernel, name=name, out_shape=out_shape, scratch_shapes=scr...]
  transfers between devices with their start and end apart: 4 -> 4, of which waited for: 1 -> 3; matrix products, arithmetic and copies ran while one was open for 54% -> 0% of each run, Pallas kernels for 0% -> 9%
where the time goes in v1:
time: 28.7 us; the launch traced here: 28.3 us
  starting transfers between devices  9.12 us (32%)
  waiting for transfers between devices  8.5 us (30%)
  Pallas kernels  6.49 us (23%)
  local copies, waits for them, and re-layouts  3.52 us (12%)
  other arithmetic  0.62 us (2%)
    all_to_all x1, waiting for transfers between devices, body(): come = lax.all_to_all(pay, 'dom', split_axis=0, concat_axis=0, tiled=True)  6.76 us
    pallas_call x4, Pallas kernels, call(): pl.pallas_call(kernel, name=name, out_shape=out_shape, scratch_shapes=scr...  6.49 us
    all_to_all x1, starting transfers between devices, body(): come = lax.all_to_all(pay, 'dom', split_axis=0, concat_axis=0, tiled=True)  5.94 us
    unnamed x26, local copies, waits for them, and re-layouts  3.52 us
    ppermute x3, starting transfers between devices, body(): lax.ppermute(sent[step - 1], 'grid', [(g, partner(g, step, grids)) for g...  3.18 us
    ppermute x3, waiting for transfers between devices, body(): lax.ppermute(sent[step - 1], 'grid', [(g, partner(g, step, grids)) for g...  1.74 us
    dynamic_update_slice x1, other arithmetic, body(): lax.dynamic_update_slice(pay.reshape(parts, rows, LANES), merged, (0, fir...  0.62 us
  transfers between devices with their start and end apart: 4, of which 3 were waited for; matrix products, arithmetic and copies ran while one was open for 0% of the time, Pallas kernels for 9%

profile of v1, /device:TPU:0, one launch (start us, length us, event | category | flops | bytes accessed | tf_op | source)
XLA Modules:
  0.0 28.3 jit_solution(679716786544091374)
XLA Ops:
  0.0 0.0 copy-start
  0.0 1.0 %copy-done = f32[5,125,128]{2,1,0:T(8,128)S(1)} copy-done((f32[5,125,128]{2,1,0:T(8,128)S(1)}, f32[5,125,128]{2,1,0:T(8,128)}, u32[]{:S(2)}) %copy-start) | copy-done | bytes 320024
  1.0 0.0 copy-start.2
  1.0 0.9 %copy-done.2 = f32[384,15]{1,0:T(8,128)S(1)} copy-done((f32[384,15]{1,0:T(8,128)S(1)}, f32[384,15]{1,0:T(8,128)}, u32[]{:S(2)}) %copy-start.2) | copy-done | bytes 23064
  1.9 0.0 copy-start.4
  1.9 0.9 %copy-done.4 = f32[1,3,5,1184]{3,0,2,1:T(1,128)S(1)} copy-done((f32[1,3,5,1184]{3,0,2,1:T(1,128)S(1)}, f32[1,3,5,1184]{3,0,2,1:T(1,128)}, u32[]{:S(2)}) %copy-start.4) | copy-done | bytes 71064
  2.8 0.0 copy-start.5
  2.8 0.7 %copy-done.5 = s32[1,1184]{1,0:T(1,128)S(1)} copy-done((s32[1,1184]{1,0:T(1,128)S(1)}, s32[1,1184]{1,0:T(1,128)}, u32[]{:S(2)}) %copy-start.5) | copy-done | bytes 4760
  3.5 0.0 copy-start.11
  3.5 0.0 copy-start.12
  3.5 2.0 %donors.1 = (f32[8,8,128]{2,1,0:T(8,128)S(1)}, f32[8,8,128]{2,1,0:T(8,128)S(1)}, f32[8,8,128]{2,1,0:T(8,128)S(1)}) custom-call(f32[5,125,128]{2,1,0:T(8,128)S(1)} %copy-done, s32[1,1184]{1,0:T(1,128)S(1)} %copy-done.5, f32[15,1,1184]{2,1,0:T(1,128)S(1)} %bitcast.4, f32[384,15]{1,0:T(8,128)S(1)} %copy-done.2), custom_call_target="tpu_custom_call" | custom-call | flops 5000000 | bytes 500000 | tf_op jit(solution)/shard_map/donors/pallas_call | solution.py:354
  5.5 0.0 copy-start.9
  5.5 0.0 copy-start.8
  5.5 0.5 %collective-permute-start = (f32[8,8,128]{2,1,0:T(8,128)S(1)}, f32[8,8,128]{2,1,0:T(8,128)S(1)}, u32[]{:S(2)}, u32[]{:S(2)}) collective-permute-start(f32[8,8,128]{2,1,0:T(8,128)S(1)} %get-tuple-element.16), channel_id=1, source_target_pairs={{0,8},{8,0},{16,24},{24,16},{1,9},{9,1},{17,25},{25,17},{2,10},{10... | collective-permute-start | bytes 98312 | tf_op jit(solution)/shard_map/ppermute | solution.py:401
  6.1 2.6 %collective-permute-start.1 = (f32[8,8,128]{2,1,0:T(8,128)S(1)}, f32[8,8,128]{2,1,0:T(8,128)S(1)}, u32[]{:S(2)}, u32[]{:S(2)}) collective-permute-start(f32[8,8,128]{2,1,0:T(8,128)S(1)} %get-tuple-element.17), channel_id=1, source_target_pairs={{0,16},{8,24},{16,0},{24,8},{1,17},{9,25},{17,1},{25,9},{2,18},{10... | collective-permute-start | bytes 98312 | tf_op jit(solution)/shard_map/ppermute | solution.py:401
  8.7 0.1 collective-permute-start.2
  8.7 0.0 copy-done.11
  8.7 0.0 copy-done.12
  8.7 0.0 copy-done.9
  8.7 0.0 copy-done.8
  8.7 0.0 copy-start.10
  8.7 1.5 %faces.1 = (f32[6,5,32,128]{3,2,1,0:T(8,128)S(1)}, f32[320,128]{1,0:T(8,128)}) custom-call(f32[5,125,128]{2,1,0:T(8,128)S(1)} %copy-done, s32[3,128]{1,0:T(4,128)S(1)} %copy-done.8, s32[3,128]{1,0:T(4,128)S(1)} %copy-done.9, f32[192,125]{1,0:T(8,128)S(1)} %copy-done.11, s32[8,128]{1,0:T(8,128)S(1)} %copy-done.12), custom_call_target="tpu_custom_call" | custom-call | flops 200000000 | bytes 1500000 | tf_op jit(solution)/shard_map/faces/pallas_call | solution.py:354
  10.3 0.0 copy-start.1
  10.3 0.0 collective-permute-done
  10.3 0.4 %collective-permute-done.1 = f32[8,8,128]{2,1,0:T(8,128)S(1)} collective-permute-done((f32[8,8,128]{2,1,0:T(8,128)S(1)}, f32[8,8,128]{2,1,0:T(8,128)S(1)}, u32[]{:S(2)}, u32[]{:S(2)}) %collective-permute-start.1) | collective-permute-done | bytes 32800 | tf_op jit(solution)/shard_map/ppermute | solution.py:401
  10.6 1.4 %collective-permute-done.2 = f32[8,8,128]{2,1,0:T(8,128)S(1)} collective-permute-done((f32[8,8,128]{2,1,0:T(8,128)S(1)}, f32[8,8,128]{2,1,0:T(8,128)S(1)}, u32[]{:S(2)}, u32[]{:S(2)}) %collective-permute-start.2) | collective-permute-done | bytes 32800 | tf_op jit(solution)/shard_map/ppermute | solution.py:401
  12.0 0.6 %add_dynamic-update-slice_fusion = f32[8,40,128]{2,1,0:T(8,128)} fusion(f32[8,40,128]{2,1,0:T(8,128)} %bitcast, f32[8,8,128]{2,1,0:T(8,128)S(1)} %collective-permute-done.2, f32[8,8,128]{2,1,0:T(8,128)S(1)} %collective-permute-done, f32[8,8,128]{2,1,0:T(8,128)S(1)} %collective-permute-done.1), kind=kLoop, calls=%fused_computation | loop fusion | flops 16384 | bytes 131072 | tf_op jit(solution)/shard_map/dynamic_update_slice | solution.py:420
  12.6 0.0 copy-start.6
  12.6 0.0 copy-start.7
  12.6 5.9 %all-to-all-start = ((f32[8,40,128]{2,1,0:T(8,128)}), f32[8,40,128]{2,1,0:T(8,128)S(1)}, u32[]{:S(2)}, u32[]{:S(2)}) async-start(f32[8,40,128]{2,1,0:T(8,128)} %add_dynamic-update-slice_fusion), calls=%async_computation | async-start | bytes 327680 | tf_op jit(solution)/shard_map/all_to_all | solution.py:421
  18.6 0.0 copy-done.10
  18.6 0.0 copy-done.1
  18.6 0.0 copy-done.6
  18.6 0.0 copy-done.7
  18.6 0.0 copy-start.3
  18.6 1.0 %volume.1 = (f32[125,640]{1,0:T(8,128)S(1)}, f32[6,6,32,128]{3,2,1,0:T(8,128)S(1)}, f32[3,5,32,128]{3,2,1,0:T(8,128)S(1)}, s32[8,128]{1,0:T(8,128)S(1)}, s32[2,8,128]{2,1,0:T(8,128)S(1)}) custom-call(f32[5,125,128]{2,1,0:T(8,128)S(1)} %copy-done.1, f32[3,128]{1,0:T(4,128)S(1)} %copy-done.6, s32[3,128]{1,0:T(4,128)S(1)} %copy-done.8, s32[3,128]{1,0:T(4,128)S(1)} %copy-done.9, ...), custom_call_target="tpu_custom_call" | custom-call | flops 400000000 | bytes 3000000 | tf_op jit(solution)/shard_map/volume/pallas_call | solution.py:354
  19.6 6.8 %all-to-all-done = f32[8,40,128]{2,1,0:T(8,128)S(1)} async-done(((f32[8,40,128]{2,1,0:T(8,128)}), f32[8,40,128]{2,1,0:T(8,128)S(1)}, u32[]{:S(2)}, u32[]{:S(2)}) %all-to-all-start) | async-done | bytes 163872 | tf_op jit(solution)/shard_map/all_to_all | solution.py:421
  26.4 0.0 copy-done.3
  26.4 2.0 %finish.1 = f32[5,125,128]{2,1,0:T(8,128)} custom-call(f32[320,128]{1,0:T(8,128)S(1)} %bitcast.3, f32[6,5,32,128]{3,2,1,0:T(8,128)S(1)} %get-tuple-element.19.slots_ref, f32[6,6,32,128]{3,2,1,0:T(8,128)S(1)} %get-tuple-element.20.flux_ref, f32[3,5,32,128]{3,2,1,0:T(8,128)S(1)} %get-tuple-element.21.local_ref, s32[8,128]{1,0:T(8,128)S(1)} %get-tuple-element.22.back_ref, ...), custom_call_target="tpu_custom_call" | custom-call | flops 200000000 | bytes 3000000 | tf_op jit(solution)/shard_map/finish/pallas_call | solution.py:354
Async XLA Ops:
  0.0 1.0 %copy-start = (f32[5,125,128]{2,1,0:T(8,128)S(1)}, f32[5,125,128]{2,1,0:T(8,128)}, u32[]{:S(2)}) copy-start(f32[5,125,128]{2,1,0:T(8,128)} %state_ref.5) | copy-start | bytes 960004
  1.0 0.9 %copy-start.2 = (f32[384,15]{1,0:T(8,128)S(1)}, f32[384,15]{1,0:T(8,128)}, u32[]{:S(2)}) copy-start(f32[384,15]{1,0:T(8,128)} %constant.14.clone.expand_ref) | copy-start | bytes 69124
  1.9 0.9 %copy-start.4 = (f32[1,3,5,1184]{3,0,2,1:T(1,128)S(1)}, f32[1,3,5,1184]{3,0,2,1:T(1,128)}, u32[]{:S(2)}) copy-start(f32[1,3,5,1184]{3,0,2,1:T(1,128)} %param.17) | copy-start | bytes 213124
  2.8 0.7 %copy-start.5 = (s32[1,1184]{1,0:T(1,128)S(1)}, s32[1,1184]{1,0:T(1,128)}, u32[]{:S(2)}) copy-start(s32[1,1184]{1,0:T(1,128)} %cell_ref.1) | copy-start | bytes 14212
  3.5 5.2 %copy-start.11 = (f32[192,125]{1,0:T(8,128)S(1)}, f32[192,125]{1,0:T(8,128)}, u32[]{:S(2)}) copy-start(f32[192,125]{1,0:T(8,128)} %constant.15.clone.faces_ref) | copy-start | bytes 288004
  3.5 5.2 %copy-start.12 = (s32[8,128]{1,0:T(8,128)S(1)}, s32[8,128]{1,0:T(8,128)}, u32[]{:S(2)}) copy-start(s32[8,128]{1,0:T(8,128)} %constant.16.clone.lanes_ref) | copy-start | bytes 12292
  5.5 3.2 %copy-start.9 = (s32[3,128]{1,0:T(4,128)S(1)}, s32[3,128]{1,0:T(4,128)}, u32[]{:S(2)}) copy-start(s32[3,128]{1,0:T(4,128)} %minus_ref.3) | copy-start | bytes 4612
  5.5 3.2 %copy-start.8 = (s32[3,128]{1,0:T(4,128)S(1)}, s32[3,128]{1,0:T(4,128)}, u32[]{:S(2)}) copy-start(s32[3,128]{1,0:T(4,128)} %plus_ref.3) | copy-start | bytes 4612
  5.5 4.7 %collective-permute-start = (f32[8,8,128]{2,1,0:T(8,128)S(1)}, f32[8,8,128]{2,1,0:T(8,128)S(1)}, u32[]{:S(2)}, u32[]{:S(2)}) collective-permute-start(f32[8,8,128]{2,1,0:T(8,128)S(1)} %get-tuple-element.16), channel_id=1, source_target_pairs={{0,8},{8,0},{16,24},{24,16},{1,9},{9,1},{17,25},{25,17},{2,10},{10... | collective-permute-start | bytes 98312 | tf_op jit(solution)/shard_map/ppermute | solution.py:401
  6.1 4.6 %collective-permute-start.1 = (f32[8,8,128]{2,1,0:T(8,128)S(1)}, f32[8,8,128]{2,1,0:T(8,128)S(1)}, u32[]{:S(2)}, u32[]{:S(2)}) collective-permute-start(f32[8,8,128]{2,1,0:T(8,128)S(1)} %get-tuple-element.17), channel_id=1, source_target_pairs={{0,16},{8,24},{16,0},{24,8},{1,17},{9,25},{17,1},{25,9},{2,18},{10... | collective-permute-start | bytes 98312 | tf_op jit(solution)/shard_map/ppermute | solution.py:401
  8.7 3.3 %collective-permute-start.2 = (f32[8,8,128]{2,1,0:T(8,128)S(1)}, f32[8,8,128]{2,1,0:T(8,128)S(1)}, u32[]{:S(2)}, u32[]{:S(2)}) collective-permute-start(f32[8,8,128]{2,1,0:T(8,128)S(1)} %get-tuple-element.18), channel_id=1, source_target_pairs={{0,24},{8,16},{16,8},{24,0},{1,25},{9,17},{17,9},{25,1},{2,26},{10... | collective-permute-start | bytes 98312 | tf_op jit(solution)/shard_map/ppermute | solution.py:401
  8.7 9.8 %copy-start.10 = (f32[125,384]{1,0:T(8,128)S(1)}, f32[125,384]{1,0:T(8,128)}, u32[]{:S(2)}) copy-start(f32[125,384]{1,0:T(8,128)} %constant.17.clone.volume_ref) | copy-start | bytes 576004
  10.3 8.3 %copy-start.1 = (f32[5,125,128]{2,1,0:T(8,128)S(1)}, f32[5,125,128]{2,1,0:T(8,128)}, u32[]{:S(2)}) copy-start(f32[5,125,128]{2,1,0:T(8,128)} %state_ref.5) | copy-start | bytes 960004
  12.6 6.0 %copy-start.6 = (f32[3,128]{1,0:T(4,128)S(1)}, f32[3,128]{1,0:T(4,128)}, u32[]{:S(2)}) copy-start(f32[3,128]{1,0:T(4,128)} %size_ref.3) | copy-start | bytes 4612
  12.6 6.0 %copy-start.7 = (s32[1,600]{1,0:T(1,128)S(1)}, s32[1,600]{1,0:T(1,128)}, u32[]{:S(2)}) copy-start(s32[1,600]{1,0:T(1,128)} %recv_ref.1) | copy-start | bytes 7204
  12.6 13.7 %all-to-all-start = ((f32[8,40,128]{2,1,0:T(8,128)}), f32[8,40,128]{2,1,0:T(8,128)S(1)}, u32[]{:S(2)}, u32[]{:S(2)}) async-start(f32[8,40,128]{2,1,0:T(8,128)} %add_dynamic-update-slice_fusion), calls=%async_computation | async-start | bytes 327680 | tf_op jit(solution)/shard_map/all_to_all | solution.py:421
  18.6 7.8 %copy-start.3 = (f32[125,192]{1,0:T(8,128)S(1)}, f32[125,192]{1,0:T(8,128)}, u32[]{:S(2)}) copy-start(f32[125,192]{1,0:T(8,128)} %constant.18.clone.lift_ref) | copy-start | bytes 288004

commit v2 on v1

v2 whole, which is shorter than its diff:
```python
import functools
import math

import jax
import jax.numpy as jnp
import numpy as np
from jax import lax
from jax.experimental import pallas as pl
from jax.experimental.pallas import tpu as pltpu
from jax.sharding import PartitionSpec as P

precise = lax.Precision.HIGHEST
closer = lax.Precision.HIGH
LANES = 128
ROWS = 32
VMEM = 48 * 1024 * 1024


def gauss_nodes():
    outer = math.sqrt(5.0 + 2.0 * math.sqrt(10.0 / 7.0)) / 3.0
    inner = math.sqrt(5.0 - 2.0 * math.sqrt(10.0 / 7.0)) / 3.0
    return [-outer, -inner, 0.0, inner, outer]


def basis_value(nodes, column, target):
    value = 1.0
    for other in range(5):
        if other != column:
            value = value * (target - nodes[other]) / (nodes[column] - nodes[other])
    return value


def basis_slope(nodes, column, target):
    total = 0.0
    for skipped in range(5):
        if skipped != column:
            value = 1.0 / (nodes[column] - nodes[skipped])
            for other in range(5):
                if other != column and other != skipped:
                    value = value * (target - nodes[other]) / (nodes[column] - nodes[other])
            total = total + value
    return total


def legendre_slopes(target):
    values = [1.0, target]
    slopes = [0.0, 1.0]
    for order in range(1, 5):
        values.append(
            ((2 * order + 1) * target * values[order] - order * values[order - 1]) / (order + 1)
        )
        slopes.append(slopes[order - 1] + (2 * order + 1) * values[order])
    return (slopes[4], slopes[5])


def tables():
    nodes = gauss_nodes()
    deriv = [[basis_slope(nodes, column, nodes[row]) for column in range(5)] for row in range(5)]
    lower = [basis_value(nodes, column, -1.0) for column in range(5)]
    upper = [basis_value(nodes, column, 1.0) for column in range(5)]
    lift_low = []
    lift_high = []
    for row in range(5):
        slope_four, slope_five = legendre_slopes(nodes[row])
        lift_low.append(-0.5 * (slope_five - slope_four))
        lift_high.append(0.5 * (slope_five + slope_four))
    return tuple(np.asarray(m, np.float64) for m in (deriv, lower, upper, lift_low, lift_high))


def split_point(point, direction):
    index = [point // 25, point // 5 % 5, point % 5]
    along = index.pop(direction)
    return along, 5 * index[0] + index[1]


def matrices():
    deriv, lower, upper, lift_low, lift_high = tables()
    faces = np.zeros((6 * ROWS, 125))
    volume = np.zeros((125, 3 * LANES))
    lift = np.zeros((125, 6 * ROWS))
    own = deriv - np.outer(lift_low, lower) - np.outer(lift_high, upper)
    for d in range(3):
        for p in range(125):
            i, t = split_point(p, d)
            faces[(2 * d) * ROWS + t, p] = lower[i]
            faces[(2 * d + 1) * ROWS + t, p] = upper[i]
            lift[p, (2 * d) * ROWS + t] = -lift_low[i]
            lift[p, (2 * d + 1) * ROWS + t] = -lift_high[i]
            for other in range(125):
                m, line = split_point(other, d)
                if line == t:
                    volume[p, d * LANES + other] = -own[i, m]
    for k in range(6):
        faces[k * ROWS + 25 : (k + 1) * ROWS] = faces[k * ROWS + 24]
    expand = np.zeros((3 * LANES, 48))
    for p in range(125):
        for axis, index in enumerate((p // 25, p // 5 % 5, p % 5)):
            for part in range(3):
                expand[axis * LANES + p, 16 * part + 5 * axis + index] = 1.0
    return tuple(m.astype(np.float32) for m in (faces, volume, lift, expand))


def slot_lanes(parts, capacity, fringes):
    remote = parts * capacity
    lanes = np.zeros((8, LANES), np.int32)
    for d in range(3):
        held = {}
        for lane in range(remote):
            held[d * remote + lane] = lane % parts * capacity + lane // parts
        for i in range(fringes):
            held[(3 * remote + d * fringes + i) % LANES] = remote + i
        free = iter(range(remote + fringes, LANES))
        for lane in range(LANES):
            lanes[d, lane] = held[lane] if lane in held else next(free)
    return lanes


def fringe_lanes(fringes):
    found = np.zeros((8, LANES), np.int32)
    for side in range(2):
        for t in range(ROWS):
            for d in range(3):
                for i in range(fringes):
                    point = ((2 * d + side) * 25 + min(t, 24)) * fringes + i
                    found[side * 4 + t // 8, (t % 8 * 3 + d) * fringes + i] = point
    return found


def partner(index, step, count):
    if count & (count - 1) == 0:
        return index ^ step
    return (index + step) % count


def lane_gather(values, index):
    return jnp.take_along_axis(values, index, axis=1, mode="promise_in_bounds")


def in_lanes(lane, start, width):
    start = start % LANES
    if start + width <= LANES:
        return (lane >= start) & (lane < start + width)
    return (lane >= start) | (lane < start + width - LANES)


def euler(state, choose, along):
    density, momenta, energy = state[0], state[1:4], state[4]
    inverse = 1.0 / density
    normal = choose(momenta)
    speed = normal * inverse
    squares = momenta[0] * momenta[0] + momenta[1] * momenta[1] + momenta[2] * momenta[2]
    pressure = 0.4 * (energy - 0.5 * squares * inverse)
    flux = [normal] + [m * speed for m in momenta] + [(energy + pressure) * speed]
    for d in range(3):
        flux[1 + d] = along(d, flux[1 + d], pressure - 1.0)
    return flux, speed, pressure, inverse


def euler_wave(state, choose, along):
    flux, speed, pressure, inverse = euler(state, choose, along)
    return flux, jnp.abs(speed) + jnp.sqrt(1.4 * pressure * inverse)


def fixed(direction):
    def choose(parts):
        return parts[direction]

    def along(d, flux, pressure):
        return flux + pressure if d == direction else flux

    return choose, along


def by_lane(first, second):
    def choose(parts):
        return jnp.where(first, parts[0], jnp.where(second, parts[1], parts[2]))

    third = ~(first | second)

    def along(d, flux, pressure):
        return flux + jnp.where((first, second, third)[d], pressure, 0.0)

    return choose, along


def mix(left, left_flux, left_wave, right, right_flux, right_wave):
    wave = 0.5 * jnp.maximum(left_wave, right_wave)
    return [
        0.5 * (left_flux[v] + right_flux[v]) - wave * (right[v] - left[v]) for v in range(5)
    ]


def donor_kernel(grids, parts, count, *refs):
    inputs = refs[:4]
    outs = refs[4 : 3 + grids]
    copies = refs[3 + grids : 7 + grids]
    cells, weights, values, done = refs[7 + grids :]
    moves = [
        pltpu.make_async_copy(source, target, done.at[k])
        for k, (source, target) in enumerate(zip(inputs, copies))
    ]
    for move in moves:
        move.start()
    state, cell, weight, expand = copies
    total = grids * parts * count
    padded = cells.shape[1]
    cells[...] = jnp.zeros_like(cells)
    weights[...] = jnp.zeros_like(weights)
    moves[1].wait()
    cells[0:1, :total] = cell[...]
    moves[2].wait()
    for k in range(15):
        weights[k : k + 1, :total] = weight[k]
    high = weights[...].astype(jnp.bfloat16)
    rest = weights[...] - high.astype(jnp.float32)
    middle = rest.astype(jnp.bfloat16)
    low = (rest - middle.astype(jnp.float32)).astype(jnp.bfloat16)
    pieces = jnp.concatenate([high, middle, low], axis=0)
    moves[3].wait()
    wide = jnp.dot(expand[...], pieces, preferred_element_type=jnp.float32)
    weight = (wide[:LANES] * wide[LANES : 2 * LANES] * wide[2 * LANES :])[:125]
    element = lax.broadcasted_iota(jnp.int32, (LANES, padded), 0)
    chosen = jnp.where(element == cells[0:1, :], 1.0, 0.0).astype(jnp.bfloat16)
    chosen = jnp.concatenate([chosen, chosen], axis=0)
    moves[0].wait()
    for v in range(5):
        shift = (1.0, 0.0, 0.0, 0.0, 2.5)[v]
        shifted = state[v] - shift
        high = shifted.astype(jnp.bfloat16)
        low = (shifted - high.astype(jnp.float32)).astype(jnp.bfloat16)
        halves = jnp.concatenate([high, low], axis=1)
        picked = jnp.dot(halves, chosen, preferred_element_type=jnp.float32)
        values[v : v + 1, :] = jnp.sum(picked * weight, axis=0, keepdims=True) + shift
    lane = lax.broadcasted_iota(jnp.int32, (8, LANES), 1)
    me = lax.axis_index("grid")
    for step in range(1, grids):
        wanted = in_lanes(lane, (step - 1) * count, count)
        for g in range(grids):

            @pl.when(partner(me, step, grids) == g)
            def _():
                for q in range(parts):
                    start = (g * parts + q) * count
                    block = start // LANES * LANES
                    width = min(2 * LANES, padded - block)
                    pair = values[:, block : block + width]
                    shift = ((step - 1) * count - (start - block)) % width
                    moved = pltpu.roll(pair, shift, 1)[:, :LANES] if shift else pair[:, :LANES]
                    outs[step - 1][q] = jnp.where(wanted, moved, 0.0)


def face_kernel(
    parts,
    capacity,
    rows,
    state_ref,
    plus_ref,
    minus_ref,
    faces_ref,
    lanes_ref,
    slots_ref,
    both_ref,
    pay_ref,
    turn,
):
    remote = parts * capacity
    wide = jnp.concatenate([state_ref[v] for v in range(5)], axis=1)
    face = jnp.dot(
        faces_ref[...], wide, precision=precise, preferred_element_type=jnp.float32
    )
    for side in range(2):
        order = (minus_ref, plus_ref)[side]
        for d in range(3):
            k = 2 * d + side
            index = lane_gather(
                jnp.broadcast_to(order[d : d + 1, :], (ROWS, LANES)),
                jnp.broadcast_to(lanes_ref[d : d + 1, :], (ROWS, LANES)),
            )
            for v in range(5):
                block = face[k * ROWS : (k + 1) * ROWS, v * LANES : (v + 1) * LANES]
                slots_ref[k, v] = lane_gather(block, index)
    lane = lax.broadcasted_iota(jnp.int32, (ROWS, LANES), 1)
    turn[:, 120:128, :] = jnp.zeros((2, 8, LANES), jnp.float32)
    for side in range(2):
        for v in range(5):
            both = jnp.where(
                lane < remote,
                slots_ref[side, v],
                jnp.where(lane < 2 * remote, slots_ref[2 + side, v], slots_ref[4 + side, v]),
            )
            both_ref[side, v] = both
            turn[side, 25 * v : 25 * v + 25, :] = both[:25]
        turned = turn[side].T
        for d in range(3):
            for s in range(capacity):
                start = d * remote + s * parts
                pay_ref[pl.ds((2 * d + side) * capacity + s, parts, stride=rows), :] = turned[
                    start : start + parts
                ]


def merge_kernel(parts, rows, first, pay_ref, *refs):
    out_ref = refs[-1]
    for q in range(parts):
        total = refs[0][q]
        for extra in refs[1:-1]:
            total = total + extra[q]
        out_ref[q * rows : q * rows + first, :] = pay_ref[q * rows : q * rows + first, :]
        out_ref[q * rows + first : q * rows + first + 8, :] = total


def volume_kernel(
    grids,
    parts,
    count,
    remote,
    fringes,
    state_ref,
    size_ref,
    plus_ref,
    minus_ref,
    recv_ref,
    slots_ref,
    both_ref,
    volume_ref,
    lanes_ref,
    points_ref,
    part_ref,
    flux_ref,
    edge_ref,
    local_ref,
    back_ref,
    where_ref,
    wide,
    index,
    received,
):
    state = [state_ref[v] for v in range(5)]
    for d in range(3):
        flux = euler(state, *fixed(d))[0]
        scale = size_ref[d : d + 1, :]
        wide[d * LANES + 120 : (d + 1) * LANES, :] = jnp.zeros((8, 5 * LANES), jnp.float32)
        for v in range(5):
            wide[d * LANES : d * LANES + 125, v * LANES : (v + 1) * LANES] = flux[v] * scale
    part_ref[...] = jnp.dot(
        volume_ref[...], wide[...], precision=closer, preferred_element_type=jnp.float32
    )
    for d in range(3):
        low = [slots_ref[2 * d, v] for v in range(5)]
        high = [slots_ref[2 * d + 1, v] for v in range(5)]
        low_flux, low_wave = euler_wave(low, *fixed(d))
        high_flux, high_wave = euler_wave(high, *fixed(d))
        local = mix(high, high_flux, high_wave, low, low_flux, low_wave)
        for v in range(5):
            local_ref[d, v] = local[v]
    lane = lax.broadcasted_iota(jnp.int32, (ROWS, LANES), 1)
    for side in range(2):
        own = [both_ref[side, v] for v in range(5)]
        flux, wave = euler_wave(own, *by_lane(lane < remote, in_lanes(lane, remote, remote)))
        for v in range(5):
            flux_ref[side, v] = flux[v]
        flux_ref[side, 5] = wave
        second = in_lanes(lane, 3 * remote + fringes, fringes)
        third = in_lanes(lane, 3 * remote + 2 * fringes, fringes)
        edge = [
            jnp.where(
                second,
                slots_ref[2 + side, v],
                jnp.where(third, slots_ref[4 + side, v], slots_ref[side, v]),
            )
            for v in range(5)
        ]
        flux, wave = euler_wave(edge, *by_lane(~(second | third), second))
        for v in range(5):
            edge_ref[side, v] = edge[v]
            edge_ref[side, 5 + v] = flux[v]
        edge_ref[side, 10] = wave
    rank = lax.broadcasted_iota(jnp.int32, (LANES, LANES), 0)
    column = lax.broadcasted_iota(jnp.int32, (LANES, LANES), 1)
    index[...] = jnp.zeros_like(index)
    for k in range(6):
        d = k // 2
        order = lane_gather(
            jnp.broadcast_to((minus_ref, plus_ref)[k % 2][d : d + 1, :], (8, LANES)),
            jnp.broadcast_to(lanes_ref[d : d + 1, :], (8, LANES)),
        )
        index[k : k + 1, :] = order[0:1].astype(jnp.float32)
    turned = index[...].T.astype(jnp.int32)
    back_ref[...] = jnp.zeros_like(back_ref)
    for k in range(6):
        found = jnp.where(turned[:, k : k + 1] == column, rank, 0)
        back_ref[k : k + 1, :] = jnp.sum(found, axis=0, keepdims=True)
    me = lax.axis_index("grid")
    received[...] = jnp.zeros_like(received)
    received[0:1, : recv_ref.shape[1]] = recv_ref[...]
    points = points_ref[...]
    slot = jnp.zeros((8, LANES), jnp.int32)
    for block in range(received.shape[1] // LANES):
        held = jnp.broadcast_to(received[0:1, block * LANES : (block + 1) * LANES], (8, LANES))
        inside = (points >= block * LANES) & (points < (block + 1) * LANES)
        picked = lane_gather(held, jnp.where(inside, points - block * LANES, 0))
        slot = jnp.where(inside, picked, slot)
    device = ((slot.astype(jnp.float32) + 0.5) * (1.0 / count)).astype(jnp.int32)
    rest = slot - device * count
    grid = ((device.astype(jnp.float32) + 0.5) * (1.0 / parts)).astype(jnp.int32)
    step = jnp.zeros_like(grid)
    for g in range(grids):
        if grids & (grids - 1) == 0:
            away = me ^ g
        else:
            away = lax.rem(me + grids - g, grids)
        step = jnp.where(grid == g, away, step)
    where_ref[0] = device - grid * parts
    where_ref[1] = jnp.maximum(step - 1, 0) * count + rest


def finish_kernel(
    parts,
    capacity,
    rows,
    first,
    fringes,
    come_ref,
    both_ref,
    flux_ref,
    edge_ref,
    local_ref,
    back_ref,
    where_ref,
    part_ref,
    size_ref,
    lift_ref,
    out_ref,
    turn,
    turned,
    wide,
):
    remote = parts * capacity
    row = lax.broadcasted_iota(jnp.int32, (ROWS, LANES), 0)
    lane = lax.broadcasted_iota(jnp.int32, (ROWS, LANES), 1)
    is_remote = [in_lanes(lane, d * remote, remote) for d in range(3)]
    is_fringe = [in_lanes(lane, 3 * remote + d * fringes, fringes) for d in range(3)]
    any_remote = (lane < 3 * remote) & (row < 25)
    any_fringe = is_fringe[0] | is_fringe[1] | is_fringe[2]
    spread = row[:8] * (3 * fringes) + ((lane[:8] - 3 * remote) & (LANES - 1))
    spread = jnp.where(any_fringe[:8], spread, 0)
    for side in range(2):
        for d in range(3):
            for s in range(capacity):
                start = d * remote + s * parts
                turn[side, start : start + parts, :] = come_ref[
                    pl.ds((2 * d + 1 - side) * capacity + s, parts, stride=rows), :
                ]
        turned[side, :LANES, :] = turn[side].T
    fringe = []
    for v in range(5):
        sent = come_ref[pl.ds(first + v, parts, stride=rows), :]
        total = jnp.zeros((8, LANES), jnp.float32)
        for q in range(parts):
            picked = lane_gather(jnp.broadcast_to(sent[q : q + 1], (8, LANES)), where_ref[1])
            total = jnp.where(where_ref[0] == q, picked, total)
        fringe.append(total)
    for side in range(2):
        own = [both_ref[side, v] for v in range(5)]
        theirs = [
            jnp.where(any_remote, turned[side, 25 * v : 25 * v + ROWS, :], own[v])
            for v in range(5)
        ]
        their = (theirs, *euler_wave(theirs, *by_lane(is_remote[0], is_remote[1])))
        mine = (own, [flux_ref[side, v] for v in range(5)], flux_ref[side, 5])
        common = mix(*mine, *their) if side else mix(*their, *mine)
        own = [edge_ref[side, v] for v in range(5)]
        theirs = []
        for v in range(5):
            pieces = [
                lane_gather(
                    jnp.broadcast_to(fringe[v][side * 4 + r : side * 4 + r + 1], (8, LANES)), spread
                )
                for r in range(4)
            ]
            theirs.append(jnp.where(any_fringe, jnp.concatenate(pieces, axis=0), own[v]))
        their = (theirs, *euler_wave(theirs, *by_lane(~(is_fringe[1] | is_fringe[2]), is_fringe[1])))
        mine = (own, [edge_ref[side, 5 + v] for v in range(5)], edge_ref[side, 10])
        outer = mix(*mine, *their) if side else mix(*their, *mine)
        for d in range(3):
            k = 2 * d + side
            index = jnp.broadcast_to(back_ref[k : k + 1, :], (ROWS, LANES))
            scale = size_ref[d : d + 1, :]
            for v in range(5):
                value = jnp.where(is_fringe[d], outer[v], local_ref[d, v])
                value = jnp.where(is_remote[d], common[v], value)
                wide[k * ROWS : (k + 1) * ROWS, v * LANES : (v + 1) * LANES] = (
                    lane_gather(value, index) * scale
                )
    total = part_ref[...] + jnp.dot(
        lift_ref[...], wide[...], precision=closer, preferred_element_type=jnp.float32
    )
    for v in range(5):
        out_ref[v] = total[:, v * LANES : (v + 1) * LANES]


def call(kernel, name, out_shape, scratch, flops, size, *operands, limit=VMEM, **more):
    return pl.pallas_call(
        kernel,
        name=name,
        out_shape=out_shape,
        scratch_shapes=scratch,
        compiler_params=pltpu.CompilerParams(vmem_limit_bytes=limit),
        cost_estimate=pl.CostEstimate(flops=flops, bytes_accessed=size, transcendentals=0),
        **more,
    )(*operands)


def body(state, inv_size, plus_order, minus_order, donor_cell, donor_weights, recv_slot):
    columns = state.shape[-1]
    parts = lax.axis_size("dom")
    grids = lax.axis_size("grid")
    capacity = max(1, columns // (3 * parts))
    remote = parts * capacity
    fringes = recv_slot.shape[-1] // 150
    total = donor_cell.shape[-1]
    count = total // (grids * parts)
    padded = -(-total // LANES) * LANES
    held = -(-recv_slot.shape[-1] // LANES) * LANES
    first = -(-6 * capacity // 8) * 8
    rows = first + 8
    faces, volume, lift, expand = matrices()
    expand = jnp.asarray(expand, jnp.bfloat16)
    lanes = slot_lanes(parts, capacity, fringes)
    points = fringe_lanes(fringes)
    f32 = functools.partial(jax.ShapeDtypeStruct, dtype=jnp.float32)
    i32 = functools.partial(jax.ShapeDtypeStruct, dtype=jnp.int32)
    memory = functools.partial(pltpu.VMEM, dtype=jnp.float32)

    sent = call(
        functools.partial(donor_kernel, grids, parts, count),
        "donors",
        tuple(f32((parts, 8, LANES)) for _ in range(grids - 1)),
        [
            memory(state.shape),
            pltpu.VMEM(donor_cell.shape, jnp.int32),
            memory((15, 1, total)),
            pltpu.VMEM(expand.shape, jnp.bfloat16),
            pltpu.VMEM((8, padded), jnp.int32),
            memory((16, padded)),
            memory((8, padded)),
            pltpu.SemaphoreType.DMA((4,)),
        ],
        5_000_000,
        500_000,
        state,
        donor_cell,
        donor_weights.reshape(15, 1, total),
        expand,
        in_specs=[pl.BlockSpec(memory_space=pl.ANY)] * 4,
        limit=60 * 1024 * 1024,
    )
    arrived = [
        lax.ppermute(sent[step - 1], "grid", [(g, partner(g, step, grids)) for g in range(grids)])
        for step in (*range(2, grids), 1)
    ]
    slots, both, pay = call(
        functools.partial(face_kernel, parts, capacity, rows),
        "faces",
        (
            f32((6, 5, ROWS, LANES)),
            f32((2, 5, ROWS, LANES)),
            f32((parts * rows, LANES)),
        ),
        [memory((2, LANES, LANES))],
        200_000_000,
        1_500_000,
        state,
        plus_order,
        minus_order,
        faces,
        lanes,
    )
    pay = call(
        functools.partial(merge_kernel, parts, rows, first),
        "merge",
        f32((parts * rows, LANES)),
        [],
        50_000,
        200_000,
        pay,
        *arrived,
    )
    come = lax.all_to_all(
        pay.reshape(parts, rows, LANES), "dom", split_axis=0, concat_axis=0, tiled=True
    )
    part, flux, edge, local, back, where = call(
        functools.partial(volume_kernel, grids, parts, count, remote, fringes),
        "volume",
        (
            f32((125, 5 * LANES)),
            f32((2, 6, ROWS, LANES)),
            f32((2, 11, ROWS, LANES)),
            f32((3, 5, ROWS, LANES)),
            i32((8, LANES)),
            i32((2, 8, LANES)),
        ),
        [
            memory((3 * LANES, 5 * LANES)),
            memory((LANES, LANES)),
            pltpu.VMEM((8, held), jnp.int32),
        ],
        400_000_000,
        3_000_000,
        state,
        inv_size,
        plus_order,
        minus_order,
        recv_slot,
        slots,
        both,
        volume,
        lanes,
        points,
    )
    return call(
        functools.partial(finish_kernel, parts, capacity, rows, first, fringes),
        "finish",
        f32((5, 125, columns)),
        [
            memory((2, LANES, LANES)),
            memory((2, LANES + 8, LANES)),
            memory((6 * ROWS, 5 * LANES)),
        ],
        200_000_000,
        3_000_000,
        come.reshape(parts * rows, LANES),
        both,
        flux,
        edge,
        local,
        back,
        where,
        part,
        inv_size,
        lift,
    )


def solution(mesh):
    return jax.shard_map(
        body,
        mesh=mesh,
        in_specs=(
            P(None, None, ("grid", "dom")),
            P(None, ("grid", "dom")),
            P(None, ("grid", "dom")),
            P(None, ("grid", "dom")),
            P(("grid", "dom"), None),
            P(("grid", "dom"), None, None, None),
            P(("grid", "dom"), None),
        ),
        out_specs=P(None, None, ("grid", "dom")),
        check_vma=False,
    )
```

time: 28.7 us -> 25.9 us (0.902)
  local copies, waits for them, and re-layouts: 3.52 us -> 0.69 us
  other arithmetic: 0.62 us -> 0 us
  Pallas kernels: 6.49 us -> 6.91 us
    unnamed x26 -> x20, local copies, waits for them, and re-layouts: 3.52 us -> 0.69 us
    ppermute x3, waiting for transfers between devices: 1.74 us -> 2.64 us  [body(): lax.ppermute(sent[step - 1], 'grid', [(g, partner(g, step, grids)) for g...]
    all_to_all x1, waiting for transfers between devices: 6.76 us -> 6.12 us  [body(): lax.all_to_all(pay.reshape(parts, rows, LANES), 'dom', split_axis=0, conc...]
    dynamic_update_slice x1 -> x0, other arithmetic: 0.62 us -> none  [body(): lax.dynamic_update_slice(pay.reshape(parts, rows, LANES), merged, (0, fir...]
    pallas_call x4 -> x5, Pallas kernels: 6.49 us -> 6.91 us  [call(): pl.pallas_call(kernel, name=name, out_shape=out_shape, scratch_shapes=scr...]
  transfers between devices with their start and end apart: 4 -> 4, of which waited for: 3 -> 3; matrix products, arithmetic and copies ran while one was open for 0% -> 0% of each run, Pallas kernels for 9% -> 6%
where the time goes in v2:
time: 25.9 us; the launch traced here: 25.6 us
  starting transfers between devices  9.16 us (35%)
  waiting for transfers between devices  8.76 us (34%)
  Pallas kernels  6.91 us (27%)
  local copies, waits for them, and re-layouts  0.69 us (3%)
    pallas_call x5, Pallas kernels, call(): pl.pallas_call(kernel, name=name, out_shape=out_shape, scratch_shapes=scr...  6.91 us
    all_to_all x1, waiting for transfers between devices, body(): lax.all_to_all(pay.reshape(parts, rows, LANES), 'dom', split_axis=0, conc...  6.12 us
    all_to_all x1, starting transfers between devices, body(): lax.all_to_all(pay.reshape(parts, rows, LANES), 'dom', split_axis=0, conc...  5.94 us
    ppermute x3, starting transfers between devices, body(): lax.ppermute(sent[step - 1], 'grid', [(g, partner(g, step, grids)) for g...  3.23 us
    ppermute x3, waiting for transfers between devices, body(): lax.ppermute(sent[step - 1], 'grid', [(g, partner(g, step, grids)) for g...  2.64 us
    unnamed x20, local copies, waits for them, and re-layouts  0.69 us
  transfers between devices with their start and end apart: 4, of which 3 were waited for; matrix products, arithmetic and copies ran while one was open for 0% of the time, Pallas kernels for 6%

profile of v2, /device:TPU:0, one launch (start us, length us, event | category | flops | bytes accessed | tf_op | source)
XLA Modules:
  0.0 25.6 jit_solution(130201871856162175)
XLA Ops:
  0.0 0.0 copy-start
  0.0 0.0 copy-start.7
  0.0 0.0 copy-start.8
  0.0 3.2 %donors.1 = (f32[8,8,128]{2,1,0:T(8,128)}, f32[8,8,128]{2,1,0:T(8,128)}, f32[8,8,128]{2,1,0:T(8,128)}) custom-call(f32[5,125,128]{2,1,0:T(8,128)} %state_ref.3, s32[1,1184]{1,0:T(1,128)} %refs_1_.1, f32[15,1,1184]{2,1,0:T(1,128)} %bitcast.4, bf16[384,48]{1,0:T(8,128)(2,1)} %constant.12.clone.refs_3_), custom_call_target="tpu_custom_call" | custom-call | flops 5000000 | bytes 500000 | tf_op jit(solution)/shard_map/donors/pallas_call | solution.py:503
  3.2 0.0 copy-start.5
  3.2 0.0 copy-start.4
  3.2 3.0 %collective-permute-start = (f32[8,8,128]{2,1,0:T(8,128)}, f32[8,8,128]{2,1,0:T(8,128)S(1)}, u32[]{:S(2)}, u32[]{:S(2)}) collective-permute-start(f32[8,8,128]{2,1,0:T(8,128)} %get-tuple-element.18), channel_id=1, source_target_pairs={{0,16},{8,24},{16,0},{24,8},{1,17},{9,25},{17,1},{25,9},{2,18},{10... | collective-permute-start | bytes 98312 | tf_op jit(solution)/shard_map/ppermute | solution.py:559
  6.2 0.0 collective-permute-start.1
  6.2 0.2 collective-permute-start.2
  6.4 0.0 copy-done
  6.4 0.0 copy-done.7
  6.4 0.0 copy-done.8
  6.4 0.0 copy-done.5
  6.5 0.0 copy-done.4
  6.5 0.8 %faces.1 = (f32[6,5,32,128]{3,2,1,0:T(8,128)S(1)}, f32[2,5,32,128]{3,2,1,0:T(8,128)S(1)}, f32[320,128]{1,0:T(8,128)S(1)}) custom-call(f32[5,125,128]{2,1,0:T(8,128)S(1)} %copy-done, s32[3,128]{1,0:T(4,128)S(1)} %copy-done.4, s32[3,128]{1,0:T(4,128)S(1)} %copy-done.5, f32[192,125]{1,0:T(8,128)S(1)} %copy-done.7, s32[8,128]{1,0:T(8,128)S(1)} %copy-done.8), custom_call_target="tpu_custom_call" | custom-call | flops 200000000 | bytes 1500000 | tf_op jit(solution)/shard_map/faces/pallas_call | solution.py:503
  7.2 1.1 %collective-permute-done.refs_0_ = f32[8,8,128]{2,1,0:T(8,128)S(1)} collective-permute-done((f32[8,8,128]{2,1,0:T(8,128)}, f32[8,8,128]{2,1,0:T(8,128)S(1)}, u32[]{:S(2)}, u32[]{:S(2)}) %collective-permute-start) | collective-permute-done | bytes 32800 | tf_op jit(solution)/shard_map/ppermute | solution.py:559
  8.4 1.5 %collective-permute-done.1.refs_1_ = f32[8,8,128]{2,1,0:T(8,128)S(1)} collective-permute-done((f32[8,8,128]{2,1,0:T(8,128)}, f32[8,8,128]{2,1,0:T(8,128)S(1)}, u32[]{:S(2)}, u32[]{:S(2)}) %collective-permute-start.1) | collective-permute-done | bytes 32800 | tf_op jit(solution)/shard_map/ppermute | solution.py:559
  9.9 0.0 collective-permute-done.2.refs_2_
  9.9 0.7 %merge.1 = f32[320,128]{1,0:T(8,128)} custom-call(f32[320,128]{1,0:T(8,128)S(1)} %get-tuple-element.17.pay_ref, f32[8,8,128]{2,1,0:T(8,128)S(1)} %collective-permute-done.refs_0_, f32[8,8,128]{2,1,0:T(8,128)S(1)} %collective-permute-done.1.refs_1_, f32[8,8,128]{2,1,0:T(8,128)S(1)} %collective-permute-done.2.refs_2_), custom_call_target="tpu_custom_call" | custom-call | flops 50000 | bytes 200000 | tf_op jit(solution)/shard_map/merge/pallas_call | solution.py:503
  10.6 0.0 copy-start.6
  10.6 0.0 copy-start.3
  10.6 0.0 copy-start.9
  10.6 5.9 %all-to-all-start = ((f32[8,40,128]{2,1,0:T(8,128)}), f32[8,40,128]{2,1,0:T(8,128)S(1)}, u32[]{:S(2)}, u32[]{:S(2)}) async-start(f32[8,40,128]{2,1,0:T(8,128)} %bitcast.1), calls=%async_computation | async-start | bytes 327680 | tf_op jit(solution)/shard_map/all_to_all | solution.py:589
  16.5 0.0 copy-start.2
  16.5 0.0 copy-done.6
  16.5 0.0 copy-done.3
  16.5 0.0 copy-done.9
  16.5 0.6 %copy-done.2 = f32[3,128]{1,0:T(4,128)S(1)} copy-done((f32[3,128]{1,0:T(4,128)S(1)}, f32[3,128]{1,0:T(4,128)}, u32[]{:S(2)}) %copy-start.2) | copy-done | bytes 1560
  17.2 0.0 copy-start.1
  17.2 0.8 %volume.1 = (f32[125,640]{1,0:T(8,128)S(1)}, f32[2,6,32,128]{3,2,1,0:T(8,128)S(1)}, f32[2,11,32,128]{3,2,1,0:T(8,128)S(1)}, f32[3,5,32,128]{3,2,1,0:T(8,128)S(1)...) custom-call(f32[5,125,128]{2,1,0:T(8,128)S(1)} %copy-done, f32[3,128]{1,0:T(4,128)S(1)} %copy-done.2, ...), custom_call_target="tpu_custom_call" | custom-call | flops 400000000 | bytes 3000000 | tf_op jit(solution)/shard_map/volume/pallas_call | solution.py:503
  18.0 6.1 %all-to-all-done = f32[8,40,128]{2,1,0:T(8,128)S(1)} async-done(((f32[8,40,128]{2,1,0:T(8,128)}), f32[8,40,128]{2,1,0:T(8,128)S(1)}, u32[]{:S(2)}, u32[]{:S(2)}) %all-to-all-start) | async-done | bytes 163872 | tf_op jit(solution)/shard_map/all_to_all | solution.py:589
  24.1 0.0 copy-done.1
  24.1 1.5 %finish.1 = f32[5,125,128]{2,1,0:T(8,128)} custom-call(f32[320,128]{1,0:T(8,128)S(1)} %bitcast.3, f32[2,5,32,128]{3,2,1,0:T(8,128)S(1)} %get-tuple-element.21.both_ref, f32[2,6,32,128]{3,2,1,0:T(8,128)S(1)} %get-tuple-element.23.flux_ref, f32[2,11,32,128]{3,2,1,0:T(8,128)S(1)} %get-tuple-element.24.edge_ref, ...), custom_call_target="tpu_custom_call" | custom-call | flops 200000000 | bytes 3000000 | tf_op jit(solution)/shard_map/finish/pallas_call | solution.py:503
Async XLA Ops:
  0.0 6.4 %copy-start = (f32[5,125,128]{2,1,0:T(8,128)S(1)}, f32[5,125,128]{2,1,0:T(8,128)}, u32[]{:S(2)}) copy-start(f32[5,125,128]{2,1,0:T(8,128)} %state_ref.3) | copy-start | bytes 960004
  0.0 6.4 %copy-start.7 = (f32[192,125]{1,0:T(8,128)S(1)}, f32[192,125]{1,0:T(8,128)}, u32[]{:S(2)}) copy-start(f32[192,125]{1,0:T(8,128)} %constant.13.clone.faces_ref) | copy-start | bytes 288004
  0.0 6.4 %copy-start.8 = (s32[8,128]{1,0:T(8,128)S(1)}, s32[8,128]{1,0:T(8,128)}, u32[]{:S(2)}) copy-start(s32[8,128]{1,0:T(8,128)} %constant.14.clone.lanes_ref) | copy-start | bytes 12292
  3.2 3.3 %copy-start.5 = (s32[3,128]{1,0:T(4,128)S(1)}, s32[3,128]{1,0:T(4,128)}, u32[]{:S(2)}) copy-start(s32[3,128]{1,0:T(4,128)} %minus_ref.3) | copy-start | bytes 4612
  3.2 3.3 %copy-start.4 = (s32[3,128]{1,0:T(4,128)S(1)}, s32[3,128]{1,0:T(4,128)}, u32[]{:S(2)}) copy-start(s32[3,128]{1,0:T(4,128)} %plus_ref.3) | copy-start | bytes 4612
  3.2 5.1 %collective-permute-start = (f32[8,8,128]{2,1,0:T(8,128)}, f32[8,8,128]{2,1,0:T(8,128)S(1)}, u32[]{:S(2)}, u32[]{:S(2)}) collective-permute-start(f32[8,8,128]{2,1,0:T(8,128)} %get-tuple-element.18), channel_id=1, source_target_pairs={{0,16},{8,24},{16,0},{24,8},{1,17},{9,25},{17,1},{25,9},{2,18},{10... | collective-permute-start | bytes 98312 | tf_op jit(solution)/shard_map/ppermute | solution.py:559
  6.2 3.6 %collective-permute-start.1 = (f32[8,8,128]{2,1,0:T(8,128)}, f32[8,8,128]{2,1,0:T(8,128)S(1)}, u32[]{:S(2)}, u32[]{:S(2)}) collective-permute-start(f32[8,8,128]{2,1,0:T(8,128)} %get-tuple-element.19), channel_id=1, source_target_pairs={{0,24},{8,16},{16,8},{24,0},{1,25},{9,17},{17,9},{25,1},{2,26},{10... | collective-permute-start | bytes 98312 | tf_op jit(solution)/shard_map/ppermute | solution.py:559
  6.2 3.6 %collective-permute-start.2 = (f32[8,8,128]{2,1,0:T(8,128)}, f32[8,8,128]{2,1,0:T(8,128)S(1)}, u32[]{:S(2)}, u32[]{:S(2)}) collective-permute-start(f32[8,8,128]{2,1,0:T(8,128)} %get-tuple-element.20), channel_id=1, source_target_pairs={{0,8},{8,0},{16,24},{24,16},{1,9},{9,1},{17,25},{25,17},{2,10},{10... | collective-permute-start | bytes 98312 | tf_op jit(solution)/shard_map/ppermute | solution.py:559
  10.6 6.0 %copy-start.6 = (f32[125,384]{1,0:T(8,128)S(1)}, f32[125,384]{1,0:T(8,128)}, u32[]{:S(2)}) copy-start(f32[125,384]{1,0:T(8,128)} %constant.15.clone.volume_ref) | copy-start | bytes 576004
  10.6 6.0 %copy-start.3 = (s32[1,600]{1,0:T(1,128)S(1)}, s32[1,600]{1,0:T(1,128)}, u32[]{:S(2)}) copy-start(s32[1,600]{1,0:T(1,128)} %recv_ref.1) | copy-start | bytes 7204
  10.6 6.0 %copy-start.9 = (s32[8,128]{1,0:T(8,128)S(1)}, s32[8,128]{1,0:T(8,128)}, u32[]{:S(2)}) copy-start(s32[8,128]{1,0:T(8,128)} %constant.16.clone.points_ref) | copy-start | bytes 12292
  10.6 13.5 %all-to-all-start = ((f32[8,40,128]{2,1,0:T(8,128)}), f32[8,40,128]{2,1,0:T(8,128)S(1)}, u32[]{:S(2)}, u32[]{:S(2)}) async-start(f32[8,40,128]{2,1,0:T(8,128)} %bitcast.1), calls=%async_computation | async-start | bytes 327680 | tf_op jit(solution)/shard_map/all_to_all | solution.py:589
  16.5 0.7 %copy-start.2 = (f32[3,128]{1,0:T(4,128)S(1)}, f32[3,128]{1,0:T(4,128)}, u32[]{:S(2)}) copy-start(f32[3,128]{1,0:T(4,128)} %size_ref.3) | copy-start | bytes 4612
  17.2 6.9 %copy-start.1 = (f32[125,192]{1,0:T(8,128)S(1)}, f32[125,192]{1,0:T(8,128)}, u32[]{:S(2)}) copy-start(f32[125,192]{1,0:T(8,128)} %constant.17.clone.lift_ref) | copy-start | bytes 288004

commit v3 on v2

--- a/solution.py
+++ b/solution.py
@@ -92,11 +92,11 @@
                     volume[p, d * LANES + other] = -own[i, m]
     for k in range(6):
         faces[k * ROWS + 25 : (k + 1) * ROWS] = faces[k * ROWS + 24]
-    expand = np.zeros((3 * LANES, 48))
-    for p in range(125):
-        for axis, index in enumerate((p // 25, p // 5 % 5, p % 5)):
-            for part in range(3):
-                expand[axis * LANES + p, 16 * part + 5 * axis + index] = 1.0
+    expand = np.zeros((2 * ROWS, 48))
+    for r in range(ROWS):
+        for part in range(3):
+            expand[r, 16 * part + 5 + r % 25 // 5] = 1.0
+            expand[ROWS + r, 16 * part + 10 + r % 5] = 1.0
     return tuple(m.astype(np.float32) for m in (faces, volume, lift, expand))
 
 
@@ -194,7 +194,7 @@
     inputs = refs[:4]
     outs = refs[4 : 3 + grids]
     copies = refs[3 + grids : 7 + grids]
-    cells, weights, values, done = refs[7 + grids :]
+    cells, weights, planes, values, done = refs[7 + grids :]
     moves = [
         pltpu.make_async_copy(source, target, done.at[k])
         for k, (source, target) in enumerate(zip(inputs, copies))
@@ -208,6 +208,9 @@
     weights[...] = jnp.zeros_like(weights)
     moves[1].wait()
     cells[0:1, :total] = cell[...]
+    element = lax.broadcasted_iota(jnp.int32, (LANES, padded), 0)
+    chosen = jnp.where(element == cells[0:1, :], 1.0, 0.0).astype(jnp.bfloat16)
+    chosen = jnp.concatenate([chosen, chosen], axis=0)
     moves[2].wait()
     for k in range(15):
         weights[k : k + 1, :total] = weight[k]
@@ -217,11 +220,18 @@
     low = (rest - middle.astype(jnp.float32)).astype(jnp.bfloat16)
     pieces = jnp.concatenate([high, middle, low], axis=0)
     moves[3].wait()
-    wide = jnp.dot(expand[...], pieces, preferred_element_type=jnp.float32)
-    weight = (wide[:LANES] * wide[LANES : 2 * LANES] * wide[2 * LANES :])[:125]
-    element = lax.broadcasted_iota(jnp.int32, (LANES, padded), 0)
-    chosen = jnp.where(element == cells[0:1, :], 1.0, 0.0).astype(jnp.bfloat16)
-    chosen = jnp.concatenate([chosen, chosen], axis=0)
+    plane = jnp.dot(expand[...], pieces, preferred_element_type=jnp.float32)
+    planes[...] = plane[:ROWS] * plane[ROWS:]
+    row = lax.broadcasted_iota(jnp.int32, (8, padded), 0)
+    tiles = []
+    for start in range(0, LANES, 8):
+        a = start // 25
+        outer = jnp.broadcast_to(weights[a : a + 1, :], (8, padded))
+        if start < 25 * (a + 1) < start + 8 and a < 4:
+            later = jnp.broadcast_to(weights[a + 1 : a + 2, :], (8, padded))
+            outer = jnp.where(row < 25 * (a + 1) - start, outer, later)
+        tiles.append(outer * planes[start % 25 : start % 25 + 8, :])
+    weight = jnp.concatenate(tiles, axis=0)[:125]
     moves[0].wait()
     for v in range(5):
         shift = (1.0, 0.0, 0.0, 0.0, 2.5)[v]
@@ -230,23 +240,21 @@
         low = (shifted - high.astype(jnp.float32)).astype(jnp.bfloat16)
         halves = jnp.concatenate([high, low], axis=1)
         picked = jnp.dot(halves, chosen, preferred_element_type=jnp.float32)
-        values[v : v + 1, :] = jnp.sum(picked * weight, axis=0, keepdims=True) + shift
+        total = jnp.sum(picked * weight, axis=0, keepdims=True) + shift
+        for block in range(padded // LANES):
+            values[block, v : v + 1, :] = total[:, block * LANES : (block + 1) * LANES]
     lane = lax.broadcasted_iota(jnp.int32, (8, LANES), 1)
     me = lax.axis_index("grid")
     for step in range(1, grids):
         wanted = in_lanes(lane, (step - 1) * count, count)
-        for g in range(grids):
-
-            @pl.when(partner(me, step, grids) == g)
-            def _():
-                for q in range(parts):
-                    start = (g * parts + q) * count
-                    block = start // LANES * LANES
-                    width = min(2 * LANES, padded - block)
-                    pair = values[:, block : block + width]
-                    shift = ((step - 1) * count - (start - block)) % width
-                    moved = pltpu.roll(pair, shift, 1)[:, :LANES] if shift else pair[:, :LANES]
-                    outs[step - 1][q] = jnp.where(wanted, moved, 0.0)
+        for q in range(parts):
+            start = (partner(me, step, grids) * parts + q) * count
+            block = start // LANES
+            index = lane + (start - block * LANES - (step - 1) * count)
+            inside = index & (LANES - 1)
+            near = lane_gather(values[block], inside)
+            far = lane_gather(values[block + 1], inside)
+            outs[step - 1][q] = jnp.where(wanted, jnp.where(index < LANES, near, far), 0.0)
 
 
 def face_kernel(
@@ -543,7 +551,8 @@
             pltpu.VMEM(expand.shape, jnp.bfloat16),
             pltpu.VMEM((8, padded), jnp.int32),
             memory((16, padded)),
-            memory((8, padded)),
+            memory((ROWS, padded)),
+            memory((padded // LANES + 1, 8, LANES)),
             pltpu.SemaphoreType.DMA((4,)),
         ],
         5_000_000,

time: 25.9 us -> 25.5 us (0.985)
  Pallas kernels: 6.91 us -> 6.54 us
    pallas_call x5, Pallas kernels: 6.91 us -> 6.54 us  [call(): pl.pallas_call(kernel, name=name, out_shape=out_shape, scratch_shapes=scr...]
where the time goes in v3:
time: 25.5 us; the launch traced here: 25.3 us
  starting transfers between devices  9.17 us (36%)
  waiting for transfers between devices  8.77 us (34%)
  Pallas kernels  6.54 us (26%)
  local copies, waits for them, and re-layouts  0.69 us (3%)
    pallas_call x5, Pallas kernels, call(): pl.pallas_call(kernel, name=name, out_shape=out_shape, scratch_shapes=scr...  6.54 us
    all_to_all x1, waiting for transfers between devices, body(): lax.all_to_all(pay.reshape(parts, rows, LANES), 'dom', split_axis=0, conc...  6.12 us
    all_to_all x1, starting transfers between devices, body(): lax.all_to_all(pay.reshape(parts, rows, LANES), 'dom', split_axis=0, conc...  5.94 us
    ppermute x3, starting transfers between devices, body(): lax.ppermute(sent[step - 1], 'grid', [(g, partner(g, step, grids)) for g...  3.23 us
    ppermute x3, waiting for transfers between devices, body(): lax.ppermute(sent[step - 1], 'grid', [(g, partner(g, step, grids)) for g...  2.65 us
    unnamed x20, local copies, waits for them, and re-layouts  0.69 us
  transfers between devices with their start and end apart: 4, of which 3 were waited for; matrix products, arithmetic and copies ran while one was open for 0% of the time, Pallas kernels for 6%

profile of v3, /device:TPU:0, one launch (start us, length us, event | category | flops | bytes accessed | tf_op | source)
XLA Modules:
  0.0 25.3 jit_solution(16866304730346035129)
XLA Ops:
  0.0 0.0 copy-start.8
  0.0 0.0 copy-start
  0.0 0.0 copy-start.7
  0.0 2.8 %donors.1 = (f32[8,8,128]{2,1,0:T(8,128)}, f32[8,8,128]{2,1,0:T(8,128)}, f32[8,8,128]{2,1,0:T(8,128)}) custom-call(f32[5,125,128]{2,1,0:T(8,128)} %state_ref.3, s32[1,1184]{1,0:T(1,128)} %refs_1_.1, f32[15,1,1184]{2,1,0:T(1,128)} %bitcast.4, bf16[64,48]{1,0:T(8,128)(2,1)} %constant.12.clone.refs_3_), custom_call_target="tpu_custom_call" | custom-call | flops 5000000 | bytes 500000 | tf_op jit(solution)/shard_map/donors/pallas_call | solution.py:511
  2.8 0.0 copy-start.5
  2.8 0.0 copy-start.4
  2.8 3.0 %collective-permute-start = (f32[8,8,128]{2,1,0:T(8,128)}, f32[8,8,128]{2,1,0:T(8,128)S(1)}, u32[]{:S(2)}, u32[]{:S(2)}) collective-permute-start(f32[8,8,128]{2,1,0:T(8,128)} %get-tuple-element.18), channel_id=1, source_target_pairs={{0,16},{8,24},{16,0},{24,8},{1,17},{9,25},{17,1},{25,9},{2,18},{10... | collective-permute-start | bytes 98312 | tf_op jit(solution)/shard_map/ppermute | solution.py:568
  5.9 0.0 collective-permute-start.1
  5.9 0.2 collective-permute-start.2
  6.1 0.0 copy-done.8
  6.1 0.0 copy-done
  6.1 0.0 copy-done.7
  6.1 0.0 copy-done.5
  6.1 0.0 copy-done.4
  6.1 0.8 %faces.1 = (f32[6,5,32,128]{3,2,1,0:T(8,128)S(1)}, f32[2,5,32,128]{3,2,1,0:T(8,128)S(1)}, f32[320,128]{1,0:T(8,128)S(1)}) custom-call(f32[5,125,128]{2,1,0:T(8,128)S(1)} %copy-done, s32[3,128]{1,0:T(4,128)S(1)} %copy-done.4, s32[3,128]{1,0:T(4,128)S(1)} %copy-done.5, f32[192,125]{1,0:T(8,128)S(1)} %copy-done.7, s32[8,128]{1,0:T(8,128)S(1)} %copy-done.8), custom_call_target="tpu_custom_call" | custom-call | flops 200000000 | bytes 1500000 | tf_op jit(solution)/shard_map/faces/pallas_call | solution.py:511
  6.9 1.1 %collective-permute-done.refs_0_ = f32[8,8,128]{2,1,0:T(8,128)S(1)} collective-permute-done((f32[8,8,128]{2,1,0:T(8,128)}, f32[8,8,128]{2,1,0:T(8,128)S(1)}, u32[]{:S(2)}, u32[]{:S(2)}) %collective-permute-start) | collective-permute-done | bytes 32800 | tf_op jit(solution)/shard_map/ppermute | solution.py:568
  8.0 1.5 %collective-permute-done.1.refs_1_ = f32[8,8,128]{2,1,0:T(8,128)S(1)} collective-permute-done((f32[8,8,128]{2,1,0:T(8,128)}, f32[8,8,128]{2,1,0:T(8,128)S(1)}, u32[]{:S(2)}, u32[]{:S(2)}) %collective-permute-start.1) | collective-permute-done | bytes 32800 | tf_op jit(solution)/shard_map/ppermute | solution.py:568
  9.5 0.0 collective-permute-done.2.refs_2_
  9.5 0.7 %merge.1 = f32[320,128]{1,0:T(8,128)} custom-call(f32[320,128]{1,0:T(8,128)S(1)} %get-tuple-element.17.pay_ref, f32[8,8,128]{2,1,0:T(8,128)S(1)} %collective-permute-done.refs_0_, f32[8,8,128]{2,1,0:T(8,128)S(1)} %collective-permute-done.1.refs_1_, f32[8,8,128]{2,1,0:T(8,128)S(1)} %collective-permute-done.2.refs_2_), custom_call_target="tpu_custom_call" | custom-call | flops 50000 | bytes 200000 | tf_op jit(solution)/shard_map/merge/pallas_call | solution.py:511
  10.2 0.0 copy-start.6
  10.2 0.0 copy-start.3
  10.2 0.0 copy-start.9
  10.2 5.9 %all-to-all-start = ((f32[8,40,128]{2,1,0:T(8,128)}), f32[8,40,128]{2,1,0:T(8,128)S(1)}, u32[]{:S(2)}, u32[]{:S(2)}) async-start(f32[8,40,128]{2,1,0:T(8,128)} %bitcast.1), calls=%async_computation | async-start | bytes 327680 | tf_op jit(solution)/shard_map/all_to_all | solution.py:598
  16.2 0.0 copy-start.2
  16.2 0.0 copy-done.6
  16.2 0.0 copy-done.3
  16.2 0.0 copy-done.9
  16.2 0.6 %copy-done.2 = f32[3,128]{1,0:T(4,128)S(1)} copy-done((f32[3,128]{1,0:T(4,128)S(1)}, f32[3,128]{1,0:T(4,128)}, u32[]{:S(2)}) %copy-start.2) | copy-done | bytes 1560
  16.8 0.0 copy-start.1
  16.8 0.8 %volume.1 = (f32[125,640]{1,0:T(8,128)S(1)}, f32[2,6,32,128]{3,2,1,0:T(8,128)S(1)}, f32[2,11,32,128]{3,2,1,0:T(8,128)S(1)}, f32[3,5,32,128]{3,2,1,0:T(8,128)S(1)...) custom-call(f32[5,125,128]{2,1,0:T(8,128)S(1)} %copy-done, f32[3,128]{1,0:T(4,128)S(1)} %copy-done.2, ...), custom_call_target="tpu_custom_call" | custom-call | flops 400000000 | bytes 3000000 | tf_op jit(solution)/shard_map/volume/pallas_call | solution.py:511
  17.6 6.1 %all-to-all-done = f32[8,40,128]{2,1,0:T(8,128)S(1)} async-done(((f32[8,40,128]{2,1,0:T(8,128)}), f32[8,40,128]{2,1,0:T(8,128)S(1)}, u32[]{:S(2)}, u32[]{:S(2)}) %all-to-all-start) | async-done | bytes 163872 | tf_op jit(solution)/shard_map/all_to_all | solution.py:598
  23.7 0.0 copy-done.1
  23.7 1.5 %finish.1 = f32[5,125,128]{2,1,0:T(8,128)} custom-call(f32[320,128]{1,0:T(8,128)S(1)} %bitcast.3, f32[2,5,32,128]{3,2,1,0:T(8,128)S(1)} %get-tuple-element.21.both_ref, f32[2,6,32,128]{3,2,1,0:T(8,128)S(1)} %get-tuple-element.23.flux_ref, f32[2,11,32,128]{3,2,1,0:T(8,128)S(1)} %get-tuple-element.24.edge_ref, ...), custom_call_target="tpu_custom_call" | custom-call | flops 200000000 | bytes 3000000 | tf_op jit(solution)/shard_map/finish/pallas_call | solution.py:511
Async XLA Ops:
  0.0 6.1 %copy-start.8 = (s32[8,128]{1,0:T(8,128)S(1)}, s32[8,128]{1,0:T(8,128)}, u32[]{:S(2)}) copy-start(s32[8,128]{1,0:T(8,128)} %constant.14.clone.lanes_ref) | copy-start | bytes 12292
  0.0 6.1 %copy-start = (f32[5,125,128]{2,1,0:T(8,128)S(1)}, f32[5,125,128]{2,1,0:T(8,128)}, u32[]{:S(2)}) copy-start(f32[5,125,128]{2,1,0:T(8,128)} %state_ref.3) | copy-start | bytes 960004
  0.0 6.1 %copy-start.7 = (f32[192,125]{1,0:T(8,128)S(1)}, f32[192,125]{1,0:T(8,128)}, u32[]{:S(2)}) copy-start(f32[192,125]{1,0:T(8,128)} %constant.13.clone.faces_ref) | copy-start | bytes 288004
  2.8 3.3 %copy-start.5 = (s32[3,128]{1,0:T(4,128)S(1)}, s32[3,128]{1,0:T(4,128)}, u32[]{:S(2)}) copy-start(s32[3,128]{1,0:T(4,128)} %minus_ref.3) | copy-start | bytes 4612
  2.8 3.3 %copy-start.4 = (s32[3,128]{1,0:T(4,128)S(1)}, s32[3,128]{1,0:T(4,128)}, u32[]{:S(2)}) copy-start(s32[3,128]{1,0:T(4,128)} %plus_ref.3) | copy-start | bytes 4612
  2.8 5.1 %collective-permute-start = (f32[8,8,128]{2,1,0:T(8,128)}, f32[8,8,128]{2,1,0:T(8,128)S(1)}, u32[]{:S(2)}, u32[]{:S(2)}) collective-permute-start(f32[8,8,128]{2,1,0:T(8,128)} %get-tuple-element.18), channel_id=1, source_target_pairs={{0,16},{8,24},{16,0},{24,8},{1,17},{9,25},{17,1},{25,9},{2,18},{10... | collective-permute-start | bytes 98312 | tf_op jit(solution)/shard_map/ppermute | solution.py:568
  5.9 3.6 %collective-permute-start.1 = (f32[8,8,128]{2,1,0:T(8,128)}, f32[8,8,128]{2,1,0:T(8,128)S(1)}, u32[]{:S(2)}, u32[]{:S(2)}) collective-permute-start(f32[8,8,128]{2,1,0:T(8,128)} %get-tuple-element.19), channel_id=1, source_target_pairs={{0,24},{8,16},{16,8},{24,0},{1,25},{9,17},{17,9},{25,1},{2,26},{10... | collective-permute-start | bytes 98312 | tf_op jit(solution)/shard_map/ppermute | solution.py:568
  5.9 3.6 %collective-permute-start.2 = (f32[8,8,128]{2,1,0:T(8,128)}, f32[8,8,128]{2,1,0:T(8,128)S(1)}, u32[]{:S(2)}, u32[]{:S(2)}) collective-permute-start(f32[8,8,128]{2,1,0:T(8,128)} %get-tuple-element.20), channel_id=1, source_target_pairs={{0,8},{8,0},{16,24},{24,16},{1,9},{9,1},{17,25},{25,17},{2,10},{10... | collective-permute-start | bytes 98312 | tf_op jit(solution)/shard_map/ppermute | solution.py:568
  10.2 6.0 %copy-start.6 = (f32[125,384]{1,0:T(8,128)S(1)}, f32[125,384]{1,0:T(8,128)}, u32[]{:S(2)}) copy-start(f32[125,384]{1,0:T(8,128)} %constant.15.clone.volume_ref) | copy-start | bytes 576004
  10.2 6.0 %copy-start.3 = (s32[1,600]{1,0:T(1,128)S(1)}, s32[1,600]{1,0:T(1,128)}, u32[]{:S(2)}) copy-start(s32[1,600]{1,0:T(1,128)} %recv_ref.1) | copy-start | bytes 7204
  10.2 6.0 %copy-start.9 = (s32[8,128]{1,0:T(8,128)S(1)}, s32[8,128]{1,0:T(8,128)}, u32[]{:S(2)}) copy-start(s32[8,128]{1,0:T(8,128)} %constant.16.clone.points_ref) | copy-start | bytes 12292
  10.2 13.5 %all-to-all-start = ((f32[8,40,128]{2,1,0:T(8,128)}), f32[8,40,128]{2,1,0:T(8,128)S(1)}, u32[]{:S(2)}, u32[]{:S(2)}) async-start(f32[8,40,128]{2,1,0:T(8,128)} %bitcast.1), calls=%async_computation | async-start | bytes 327680 | tf_op jit(solution)/shard_map/all_to_all | solution.py:598
  16.2 0.7 %copy-start.2 = (f32[3,128]{1,0:T(4,128)S(1)}, f32[3,128]{1,0:T(4,128)}, u32[]{:S(2)}) copy-start(f32[3,128]{1,0:T(4,128)} %size_ref.3) | copy-start | bytes 4612
  16.8 6.9 %copy-start.1 = (f32[125,192]{1,0:T(8,128)S(1)}, f32[125,192]{1,0:T(8,128)}, u32[]{:S(2)}) copy-start(f32[125,192]{1,0:T(8,128)} %constant.17.clone.lift_ref) | copy-start | bytes 288004

commit v4 on v2

--- a/solution.py
+++ b/solution.py
@@ -12,6 +12,7 @@
 precise = lax.Precision.HIGHEST
 closer = lax.Precision.HIGH
 LANES = 128
+SHIFT = (1.0, 0.0, 0.0, 0.0, 2.5)
 ROWS = 32
 VMEM = 48 * 1024 * 1024
 
@@ -92,12 +93,7 @@
                     volume[p, d * LANES + other] = -own[i, m]
     for k in range(6):
         faces[k * ROWS + 25 : (k + 1) * ROWS] = faces[k * ROWS + 24]
-    expand = np.zeros((3 * LANES, 48))
-    for p in range(125):
-        for axis, index in enumerate((p // 25, p // 5 % 5, p % 5)):
-            for part in range(3):
-                expand[axis * LANES + p, 16 * part + 5 * axis + index] = 1.0
-    return tuple(m.astype(np.float32) for m in (faces, volume, lift, expand))
+    return tuple(m.astype(np.float32) for m in (faces, volume, lift))
 
 
 def slot_lanes(parts, capacity, fringes):
@@ -126,10 +122,8 @@
     return found
 
 
-def partner(index, step, count):
-    if count & (count - 1) == 0:
-        return index ^ step
-    return (index + step) % count
+def partner(index, step):
+    return index ^ step
 
 
 def lane_gather(values, index):
@@ -190,63 +184,91 @@
     ]
 
 
+def table_kernel(out_ref):
+    row = lax.broadcasted_iota(jnp.int32, out_ref.shape, 0)
+    column = lax.broadcasted_iota(jnp.int32, out_ref.shape, 1) & 15
+    point = row & (ROWS - 1)
+    point = jnp.where(point >= 25, point - 25, point)
+    tens = ((point.astype(jnp.float32) + 0.5) * 0.2).astype(jnp.int32)
+    wanted = jnp.where(row < ROWS, 5 + tens, 10 + point - 5 * tens)
+    out_ref[...] = jnp.where(column == wanted, 1.0, 0.0).astype(jnp.bfloat16)
+
+
 def donor_kernel(grids, parts, count, *refs):
-    inputs = refs[:4]
-    outs = refs[4 : 3 + grids]
-    copies = refs[3 + grids : 7 + grids]
-    cells, weights, values, done = refs[7 + grids :]
-    moves = [
-        pltpu.make_async_copy(source, target, done.at[k])
-        for k, (source, target) in enumerate(zip(inputs, copies))
-    ]
-    for move in moves:
-        move.start()
-    state, cell, weight, expand = copies
-    total = grids * parts * count
-    padded = cells.shape[1]
+    states, cell_refs, weight_refs, expand_ref = refs[0:2], refs[2:4], refs[4:6], refs[6]
+    outs = refs[7 : 7 + grids // 2]
+    cells, weights, planes, values = refs[7 + grids // 2 :]
+    span = parts * count
+    total = grids * span
+    blocks = values.shape[1] - 1
+    width = blocks * LANES
     cells[...] = jnp.zeros_like(cells)
     weights[...] = jnp.zeros_like(weights)
-    moves[1].wait()
-    cells[0:1, :total] = cell[...]
-    moves[2].wait()
-    for k in range(15):
-        weights[k : k + 1, :total] = weight[k]
-    high = weights[...].astype(jnp.bfloat16)
-    rest = weights[...] - high.astype(jnp.float32)
-    middle = rest.astype(jnp.bfloat16)
-    low = (rest - middle.astype(jnp.float32)).astype(jnp.bfloat16)
-    pieces = jnp.concatenate([high, middle, low], axis=0)
-    moves[3].wait()
-    wide = jnp.dot(expand[...], pieces, preferred_element_type=jnp.float32)
-    weight = (wide[:LANES] * wide[LANES : 2 * LANES] * wide[2 * LANES :])[:125]
-    element = lax.broadcasted_iota(jnp.int32, (LANES, padded), 0)
-    chosen = jnp.where(element == cells[0:1, :], 1.0, 0.0).astype(jnp.bfloat16)
-    chosen = jnp.concatenate([chosen, chosen], axis=0)
-    moves[0].wait()
-    for v in range(5):
-        shift = (1.0, 0.0, 0.0, 0.0, 2.5)[v]
-        shifted = state[v] - shift
-        high = shifted.astype(jnp.bfloat16)
-        low = (shifted - high.astype(jnp.float32)).astype(jnp.bfloat16)
-        halves = jnp.concatenate([high, low], axis=1)
-        picked = jnp.dot(halves, chosen, preferred_element_type=jnp.float32)
-        values[v : v + 1, :] = jnp.sum(picked * weight, axis=0, keepdims=True) + shift
+    halves = []
+    for source in range(2):
+        for block in range(-(-total // LANES)):
+            lanes = slice(block * LANES, min((block + 1) * LANES, total))
+            held = lanes.stop - lanes.start
+            cells[source, block, 0:1, :held] = cell_refs[source][:, lanes]
+            for k in range(15):
+                weights[source, block, k : k + 1, :held] = weight_refs[source][k, :, lanes]
+        for v in range(5):
+            shifted = states[source][v] - SHIFT[v]
+            high = shifted.astype(jnp.bfloat16)
+            low = (shifted - high.astype(jnp.float32)).astype(jnp.bfloat16)
+            halves.append(jnp.concatenate([high, low], axis=1))
+    element = lax.broadcasted_iota(jnp.int32, (LANES, width), 0)
+    row = lax.broadcasted_iota(jnp.int32, (8, width), 0)
     lane = lax.broadcasted_iota(jnp.int32, (8, LANES), 1)
     me = lax.axis_index("grid")
-    for step in range(1, grids):
-        wanted = in_lanes(lane, (step - 1) * count, count)
-        for g in range(grids):
-
-            @pl.when(partner(me, step, grids) == g)
-            def _():
-                for q in range(parts):
-                    start = (g * parts + q) * count
-                    block = start // LANES * LANES
-                    width = min(2 * LANES, padded - block)
-                    pair = values[:, block : block + width]
-                    shift = ((step - 1) * count - (start - block)) % width
-                    moved = pltpu.roll(pair, shift, 1)[:, :LANES] if shift else pair[:, :LANES]
-                    outs[step - 1][q] = jnp.where(wanted, moved, 0.0)
+    number = 0
+    for step in range(0, grids, 2):
+        start = partner(me, step) * span
+        first = start // LANES
+        found = [jnp.zeros((8, LANES), jnp.float32)] * parts
+        for source in range(0 if step else 1, 2):
+            held = jnp.concatenate([cells[source, first + i] for i in range(blocks)], axis=1)
+            chosen = jnp.where(element == held[0:1], 1.0, 0.0).astype(jnp.bfloat16)
+            chosen = jnp.concatenate([chosen, chosen], axis=0)
+            held = jnp.concatenate([weights[source, first + i] for i in range(blocks)], axis=1)
+            high = held.astype(jnp.bfloat16)
+            rest = held - high.astype(jnp.float32)
+            middle = rest.astype(jnp.bfloat16)
+            low = (rest - middle.astype(jnp.float32)).astype(jnp.bfloat16)
+            pieces = jnp.concatenate([high, middle, low], axis=0)
+            plane = jnp.dot(expand_ref[...], pieces, preferred_element_type=jnp.float32)
+            planes[number] = plane[:ROWS] * plane[ROWS:]
+            tiles = []
+            for top in range(0, LANES, 8):
+                a = top // 25
+                outer = jnp.broadcast_to(held[a : a + 1], (8, width))
+                if top < 25 * (a + 1) < top + 8 and a < 4:
+                    later = jnp.broadcast_to(held[a + 1 : a + 2], (8, width))
+                    outer = jnp.where(row < 25 * (a + 1) - top, outer, later)
+                tiles.append(outer * planes[number, top % 25 : top % 25 + 8, :])
+            weight = jnp.concatenate(tiles, axis=0)[:125]
+            for v in range(5):
+                picked = jnp.dot(
+                    halves[5 * source + v], chosen, preferred_element_type=jnp.float32
+                )
+                value = jnp.sum(picked * weight, axis=0, keepdims=True) + SHIFT[v]
+                for block in range(blocks):
+                    values[number, block, v : v + 1, :] = value[
+                        :, block * LANES : (block + 1) * LANES
+                    ]
+            place = (step + source - 1) * count
+            wanted = in_lanes(lane, place, count)
+            for q in range(parts):
+                offset = start - first * LANES + q * count
+                block = offset // LANES
+                index = lane + (offset - block * LANES - place)
+                inside = index & (LANES - 1)
+                near = lane_gather(values[number, block], inside)
+                far = lane_gather(values[number, block + 1], inside)
+                found[q] = jnp.where(wanted, jnp.where(index < LANES, near, far), found[q])
+            number += 1
+        for q in range(parts):
+            outs[step // 2][q] = found[q]
 
 
 def face_kernel(
@@ -405,10 +427,7 @@
     grid = ((device.astype(jnp.float32) + 0.5) * (1.0 / parts)).astype(jnp.int32)
     step = jnp.zeros_like(grid)
     for g in range(grids):
-        if grids & (grids - 1) == 0:
-            away = me ^ g
-        else:
-            away = lax.rem(me + grids - g, grids)
+        away = partner(me, g)
         step = jnp.where(grid == g, away, step)
     where_ref[0] = device - grid * parts
     where_ref[1] = jnp.maximum(step - 1, 0) * count + rest
@@ -520,45 +539,54 @@
     fringes = recv_slot.shape[-1] // 150
     total = donor_cell.shape[-1]
     count = total // (grids * parts)
-    padded = -(-total // LANES) * LANES
     held = -(-recv_slot.shape[-1] // LANES) * LANES
     first = -(-6 * capacity // 8) * 8
     rows = first + 8
-    faces, volume, lift, expand = matrices()
-    expand = jnp.asarray(expand, jnp.bfloat16)
+    faces, volume, lift = matrices()
     lanes = slot_lanes(parts, capacity, fringes)
     points = fringe_lanes(fringes)
     f32 = functools.partial(jax.ShapeDtypeStruct, dtype=jnp.float32)
     i32 = functools.partial(jax.ShapeDtypeStruct, dtype=jnp.int32)
     memory = functools.partial(pltpu.VMEM, dtype=jnp.float32)
 
+    span = parts * count
+    blocks = (2 * (LANES - 1) + span) // LANES
+    sets = grids - 1
+    held_blocks = -(-total // LANES) + blocks
+
+    def exchange(values, step):
+        return lax.ppermute(values, "grid", [(g, partner(g, step)) for g in range(grids)])
+
+    expand = call(
+        table_kernel,
+        "tables",
+        jax.ShapeDtypeStruct((2 * ROWS, 48), jnp.bfloat16),
+        [],
+        400_000_000,
+        3_000_000,
+    )
+    weights = donor_weights.reshape(15, 1, total)
     sent = call(
         functools.partial(donor_kernel, grids, parts, count),
         "donors",
-        tuple(f32((parts, 8, LANES)) for _ in range(grids - 1)),
+        tuple(f32((parts, 8, LANES)) for _ in range(grids // 2)),
         [
-            memory(state.shape),
-            pltpu.VMEM(donor_cell.shape, jnp.int32),
-            memory((15, 1, total)),
-            pltpu.VMEM(expand.shape, jnp.bfloat16),
-            pltpu.VMEM((8, padded), jnp.int32),
-            memory((16, padded)),
-            memory((8, padded)),
-            pltpu.SemaphoreType.DMA((4,)),
+            pltpu.VMEM((2, held_blocks, 8, LANES), jnp.int32),
+            memory((2, held_blocks, 16, LANES)),
+            memory((sets, ROWS, blocks * LANES)),
+            memory((sets, blocks + 1, 8, LANES)),
         ],
         5_000_000,
         500_000,
         state,
+        exchange(state, 1),
         donor_cell,
-        donor_weights.reshape(15, 1, total),
+        exchange(donor_cell, 1),
+        weights,
+        exchange(weights, 1),
         expand,
-        in_specs=[pl.BlockSpec(memory_space=pl.ANY)] * 4,
-        limit=60 * 1024 * 1024,
-    )
-    arrived = [
-        lax.ppermute(sent[step - 1], "grid", [(g, partner(g, step, grids)) for g in range(grids)])
-        for step in (*range(2, grids), 1)
-    ]
+    )
+    arrived = [sent[0]] + [exchange(sent[k], 2 * k) for k in range(1, grids // 2)]
     slots, both, pay = call(
         functools.partial(face_kernel, parts, capacity, rows),
         "faces",

time: 25.9 us -> 24.6 us (0.950)
  Pallas kernels: 6.91 us -> 4.97 us
  starting transfers between devices: 9.16 us -> 10.3 us
  waiting for transfers between devices: 8.76 us -> 8.22 us
    pallas_call x5 -> x6, Pallas kernels: 6.91 us -> 4.97 us  [call(): pl.pallas_call(kernel, name=name, out_shape=out_shape, scratch_shapes=scr...]
    ppermute x3 -> x4, starting transfers between devices: 3.23 us -> 3.9 us  [exchange(): lax.ppermute(values, 'grid', [(g, partner(g, step)) for g in range(grids)])]
    ppermute x3 -> x4, waiting for transfers between devices: 2.64 us -> 2.1 us  [exchange(): lax.ppermute(values, 'grid', [(g, partner(g, step)) for g in range(grids)])]
    all_to_all x1, starting transfers between devices: 5.94 us -> 6.45 us  [body(): lax.all_to_all(pay.reshape(parts, rows, LANES), 'dom', split_axis=0, conc...]
    unnamed x20 -> x24, local copies, waits for them, and re-layouts: 0.69 us -> 0.7 us
  transfers between devices with their start and end apart: 4 -> 5, of which waited for: 3 -> 3; matrix products, arithmetic and copies ran while one was open for 0% -> 0% of each run, Pallas kernels for 6% -> 6%
where the time goes in v4:
time: 24.6 us; the launch traced here: 24.4 us
  starting transfers between devices  10.3 us (42%)
  waiting for transfers between devices  8.22 us (33%)
  Pallas kernels  4.97 us (20%)
  local copies, waits for them, and re-layouts  0.7 us (3%)
    all_to_all x1, starting transfers between devices, body(): lax.all_to_all(pay.reshape(parts, rows, LANES), 'dom', split_axis=0, conc...  6.45 us
    all_to_all x1, waiting for transfers between devices, body(): lax.all_to_all(pay.reshape(parts, rows, LANES), 'dom', split_axis=0, conc...  6.12 us
    pallas_call x6, Pallas kernels, call(): pl.pallas_call(kernel, name=name, out_shape=out_shape, scratch_shapes=scr...  4.97 us
    ppermute x4, starting transfers between devices, exchange(): lax.ppermute(values, 'grid', [(g, partner(g, step)) for g in range(grids)])  3.9 us
    ppermute x4, waiting for transfers between devices, exchange(): lax.ppermute(values, 'grid', [(g, partner(g, step)) for g in range(grids)])  2.1 us
    unnamed x24, local copies, waits for them, and re-layouts  0.7 us
  transfers between devices with their start and end apart: 5, of which 3 were waited for; matrix products, arithmetic and copies ran while one was open for 0% of the time, Pallas kernels for 6%

profile of v4, /device:TPU:0, one launch (start us, length us, event | category | flops | bytes accessed | tf_op | source)
XLA Modules:
  0.0 24.4 jit_solution(12931519364459803893)
XLA Ops:
  0.0 0.5 %collective-permute-start = (f32[5,125,128]{2,1,0:T(8,128)}, f32[5,125,128]{2,1,0:T(8,128)S(1)}, u32[]{:S(2)}, u32[]{:S(2)}) collective-permute-start(f32[5,125,128]{2,1,0:T(8,128)} %state_ref.3), channel_id=1, source_target_pairs={{0,8},{8,0},{16,24},{24,16},{1,9},{9,1},{17,25},{25,17},{2,10},{10... | collective-permute-start | bytes 960008 | tf_op jit(solution)/shard_map/ppermute | solution.py:558
  0.5 0.0 copy-start
  0.5 0.0 copy-start.2
  0.5 0.0 copy-start.3
  0.5 0.1 collective-permute-start.2
  0.5 0.4 %collective-permute-start.1 = (s32[1,1184]{1,0:T(1,128)}, s32[1,1184]{1,0:T(1,128)S(1)}, u32[]{:S(2)}, u32[]{:S(2)}) collective-permute-start(s32[1,1184]{1,0:T(1,128)} %refs_2_.1), channel_id=1, source_target_pairs={{0,8},{8,0},{16,24},{24,16},{1,9},{9,1},{17,25},{25,17},{2,10},{10... | collective-permute-start | bytes 14216 | tf_op jit(solution)/shard_map/ppermute | solution.py:558
  1.0 0.0 copy-start.6
  1.0 0.0 copy-start.7
  1.0 0.0 copy-start.9
  1.0 0.0 copy-start.10
  1.0 1.0 %collective-permute-done.1.refs_3_ = s32[1,1184]{1,0:T(1,128)S(1)} collective-permute-done((s32[1,1184]{1,0:T(1,128)}, s32[1,1184]{1,0:T(1,128)S(1)}, u32[]{:S(2)}, u32[]{:S(2)}) %collective-permute-start.1) | collective-permute-done | bytes 4768 | tf_op jit(solution)/shard_map/ppermute | solution.py:558
  2.0 0.0 collective-permute-done.2.refs_5_
  2.0 0.0 collective-permute-done.refs_1_
  2.0 0.0 copy-done
  2.0 0.0 copy-done.2
  2.1 0.0 copy-done.3
  2.1 1.2 %donors.1 = (f32[8,8,128]{2,1,0:T(8,128)S(1)}, f32[8,8,128]{2,1,0:T(8,128)S(1)}) custom-call(f32[5,125,128]{2,1,0:T(8,128)S(1)} %copy-done, f32[5,125,128]{2,1,0:T(8,128)S(1)} %collective-permute-done.refs_1_, s32[1,1184]{1,0:T(1,128)S(1)} %copy-done.3, s32[1,1184]{1,0:T(1,128)S(1)} %collective-permute-done.1.refs_3_, f32[15,1,1184]{2,1,0:T(1,128)S(1)} %bitcast.5, ...), custom_call_target="tpu_custom_call" | custom-call | flops 5000000 | bytes 500000 | tf_op jit(solution)/shard_map/donors/pallas_call | solution.py:522
  3.3 2.9 %collective-permute-start.3 = (f32[8,8,128]{2,1,0:T(8,128)S(1)}, f32[8,8,128]{2,1,0:T(8,128)S(1)}, u32[]{:S(2)}, u32[]{:S(2)}) collective-permute-start(f32[8,8,128]{2,1,0:T(8,128)S(1)} %get-tuple-element.18), channel_id=1, source_target_pairs={{0,16},{8,24},{16,0},{24,8},{1,17},{9,25},{17,1},{25,9},{2,18},{10... | collective-permute-start | bytes 98312 | tf_op jit(solution)/shard_map/ppermute | solution.py:558
  6.2 0.0 copy-done.6
  6.2 0.0 copy-done.7
  6.2 0.0 copy-done.9
  6.2 0.0 copy-done.10
  6.2 0.8 %faces.1 = (f32[6,5,32,128]{3,2,1,0:T(8,128)S(1)}, f32[2,5,32,128]{3,2,1,0:T(8,128)S(1)}, f32[320,128]{1,0:T(8,128)S(1)}) custom-call(f32[5,125,128]{2,1,0:T(8,128)S(1)} %copy-done, s32[3,128]{1,0:T(4,128)S(1)} %copy-done.6, s32[3,128]{1,0:T(4,128)S(1)} %copy-done.7, f32[192,125]{1,0:T(8,128)S(1)} %copy-done.9, s32[8,128]{1,0:T(8,128)S(1)} %copy-done.10), custom_call_target="tpu_custom_call" | custom-call | flops 200000000 | bytes 1500000 | tf_op jit(solution)/shard_map/faces/pallas_call | solution.py:522
  7.0 1.1 %collective-permute-done.3.refs_1_ = f32[8,8,128]{2,1,0:T(8,128)S(1)} collective-permute-done((f32[8,8,128]{2,1,0:T(8,128)S(1)}, f32[8,8,128]{2,1,0:T(8,128)S(1)}, u32[]{:S(2)}, u32[]{:S(2)}) %collective-permute-start.3) | collective-permute-done | bytes 32800 | tf_op jit(solution)/shard_map/ppermute | solution.py:558
  8.1 0.7 %merge.1 = f32[320,128]{1,0:T(8,128)} custom-call(f32[320,128]{1,0:T(8,128)S(1)} %get-tuple-element.16.pay_ref, f32[8,8,128]{2,1,0:T(8,128)S(1)} %get-tuple-element.17.refs_0_, f32[8,8,128]{2,1,0:T(8,128)S(1)} %collective-permute-done.3.refs_1_), custom_call_target="tpu_custom_call" | custom-call | flops 50000 | bytes 200000 | tf_op jit(solution)/shard_map/merge/pallas_call | solution.py:522
  8.8 0.0 copy-start.8
  8.8 0.0 copy-start.5
  8.8 0.0 copy-start.11
  8.8 6.4 %all-to-all-start = ((f32[8,40,128]{2,1,0:T(8,128)}), f32[8,40,128]{2,1,0:T(8,128)S(1)}, u32[]{:S(2)}, u32[]{:S(2)}) async-start(f32[8,40,128]{2,1,0:T(8,128)} %bitcast.1), calls=%async_computation | async-start | bytes 327680 | tf_op jit(solution)/shard_map/all_to_all | solution.py:617
  15.3 0.0 copy-start.4
  15.3 0.0 copy-done.8
  15.3 0.0 copy-done.5
  15.3 0.0 copy-done.11
  15.3 0.6 %copy-done.4 = f32[3,128]{1,0:T(4,128)S(1)} copy-done((f32[3,128]{1,0:T(4,128)S(1)}, f32[3,128]{1,0:T(4,128)}, u32[]{:S(2)}) %copy-start.4) | copy-done | bytes 1560
  15.9 0.0 copy-start.1
  15.9 0.8 %volume.1 = (f32[125,640]{1,0:T(8,128)S(1)}, f32[2,6,32,128]{3,2,1,0:T(8,128)S(1)}, f32[2,11,32,128]{3,2,1,0:T(8,128)S(1)}, f32[3,5,32,128]{3,2,1,0:T(8,128)S(1)...) custom-call(f32[5,125,128]{2,1,0:T(8,128)S(1)} %copy-done, f32[3,128]{1,0:T(4,128)S(1)} %copy-done.4, ...), custom_call_target="tpu_custom_call" | custom-call | flops 400000000 | bytes 3000000 | tf_op jit(solution)/shard_map/volume/pallas_call | solution.py:522
  16.7 6.1 %all-to-all-done = f32[8,40,128]{2,1,0:T(8,128)S(1)} async-done(((f32[8,40,128]{2,1,0:T(8,128)}), f32[8,40,128]{2,1,0:T(8,128)S(1)}, u32[]{:S(2)}, u32[]{:S(2)}) %all-to-all-start) | async-done | bytes 163872 | tf_op jit(solution)/shard_map/all_to_all | solution.py:617
  22.8 0.0 copy-done.1
  22.8 1.5 %finish.1 = f32[5,125,128]{2,1,0:T(8,128)} custom-call(f32[320,128]{1,0:T(8,128)S(1)} %bitcast.3, f32[2,5,32,128]{3,2,1,0:T(8,128)S(1)} %get-tuple-element.19.both_ref, f32[2,6,32,128]{3,2,1,0:T(8,128)S(1)} %get-tuple-element.21.flux_ref, f32[2,11,32,128]{3,2,1,0:T(8,128)S(1)} %get-tuple-element.22.edge_ref, ...), custom_call_target="tpu_custom_call" | custom-call | flops 200000000 | bytes 3000000 | tf_op jit(solution)/shard_map/finish/pallas_call | solution.py:522
  (1 shorter events, 0.0 us)
Async XLA Ops:
  0.0 2.0 %collective-permute-start = (f32[5,125,128]{2,1,0:T(8,128)}, f32[5,125,128]{2,1,0:T(8,128)S(1)}, u32[]{:S(2)}, u32[]{:S(2)}) collective-permute-start(f32[5,125,128]{2,1,0:T(8,128)} %state_ref.3), channel_id=1, source_target_pairs={{0,8},{8,0},{16,24},{24,16},{1,9},{9,1},{17,25},{25,17},{2,10},{10... | collective-permute-start | bytes 960008 | tf_op jit(solution)/shard_map/ppermute | solution.py:558
  0.5 1.6 %copy-start = (f32[5,125,128]{2,1,0:T(8,128)S(1)}, f32[5,125,128]{2,1,0:T(8,128)}, u32[]{:S(2)}) copy-start(f32[5,125,128]{2,1,0:T(8,128)} %state_ref.3) | copy-start | bytes 960004
  0.5 1.6 %copy-start.2 = (f32[1,3,5,1184]{3,0,2,1:T(1,128)S(1)}, f32[1,3,5,1184]{3,0,2,1:T(1,128)}, u32[]{:S(2)}) copy-start(f32[1,3,5,1184]{3,0,2,1:T(1,128)} %param.17) | copy-start | bytes 213124
  0.5 1.6 %copy-start.3 = (s32[1,1184]{1,0:T(1,128)S(1)}, s32[1,1184]{1,0:T(1,128)}, u32[]{:S(2)}) copy-start(s32[1,1184]{1,0:T(1,128)} %refs_2_.1) | copy-start | bytes 14212
  0.5 1.6 %collective-permute-start.2 = (f32[15,1,1184]{2,1,0:T(1,128)}, f32[15,1,1184]{2,1,0:T(1,128)S(1)}, u32[]{:S(2)}, u32[]{:S(2)}) collective-permute-start(f32[15,1,1184]{2,1,0:T(1,128)} %bitcast.4), channel_id=1, source_target_pairs={{0,8},{8,0},{16,24},{24,16},{1,9},{9,1},{17,25},{25,17},{2,10},{10... | collective-permute-start | bytes 213128 | tf_op jit(solution)/shard_map/ppermute | solution.py:558
  0.5 1.5 %collective-permute-start.1 = (s32[1,1184]{1,0:T(1,128)}, s32[1,1184]{1,0:T(1,128)S(1)}, u32[]{:S(2)}, u32[]{:S(2)}) collective-permute-start(s32[1,1184]{1,0:T(1,128)} %refs_2_.1), channel_id=1, source_target_pairs={{0,8},{8,0},{16,24},{24,16},{1,9},{9,1},{17,25},{25,17},{2,10},{10... | collective-permute-start | bytes 14216 | tf_op jit(solution)/shard_map/ppermute | solution.py:558
  1.0 5.2 %copy-start.6 = (s32[3,128]{1,0:T(4,128)S(1)}, s32[3,128]{1,0:T(4,128)}, u32[]{:S(2)}) copy-start(s32[3,128]{1,0:T(4,128)} %plus_ref.3) | copy-start | bytes 4612
  1.0 5.2 %copy-start.7 = (s32[3,128]{1,0:T(4,128)S(1)}, s32[3,128]{1,0:T(4,128)}, u32[]{:S(2)}) copy-start(s32[3,128]{1,0:T(4,128)} %minus_ref.3) | copy-start | bytes 4612
  1.0 5.2 %copy-start.9 = (f32[192,125]{1,0:T(8,128)S(1)}, f32[192,125]{1,0:T(8,128)}, u32[]{:S(2)}) copy-start(f32[192,125]{1,0:T(8,128)} %constant.10.clone.faces_ref) | copy-start | bytes 288004
  1.0 5.2 %copy-start.10 = (s32[8,128]{1,0:T(8,128)S(1)}, s32[8,128]{1,0:T(8,128)}, u32[]{:S(2)}) copy-start(s32[8,128]{1,0:T(8,128)} %constant.11.clone.lanes_ref) | copy-start | bytes 12292
  3.3 4.8 %collective-permute-start.3 = (f32[8,8,128]{2,1,0:T(8,128)S(1)}, f32[8,8,128]{2,1,0:T(8,128)S(1)}, u32[]{:S(2)}, u32[]{:S(2)}) collective-permute-start(f32[8,8,128]{2,1,0:T(8,128)S(1)} %get-tuple-element.18), channel_id=1, source_target_pairs={{0,16},{8,24},{16,0},{24,8},{1,17},{9,25},{17,1},{25,9},{2,18},{10... | collective-permute-start | bytes 98312 | tf_op jit(solution)/shard_map/ppermute | solution.py:558
  8.8 6.5 %copy-start.8 = (f32[125,384]{1,0:T(8,128)S(1)}, f32[125,384]{1,0:T(8,128)}, u32[]{:S(2)}) copy-start(f32[125,384]{1,0:T(8,128)} %constant.12.clone.volume_ref) | copy-start | bytes 576004
  8.8 6.5 %copy-start.5 = (s32[1,600]{1,0:T(1,128)S(1)}, s32[1,600]{1,0:T(1,128)}, u32[]{:S(2)}) copy-start(s32[1,600]{1,0:T(1,128)} %recv_ref.1) | copy-start | bytes 7204
  8.8 6.5 %copy-start.11 = (s32[8,128]{1,0:T(8,128)S(1)}, s32[8,128]{1,0:T(8,128)}, u32[]{:S(2)}) copy-start(s32[8,128]{1,0:T(8,128)} %constant.13.clone.points_ref) | copy-start | bytes 12292
  8.8 14.0 %all-to-all-start = ((f32[8,40,128]{2,1,0:T(8,128)}), f32[8,40,128]{2,1,0:T(8,128)S(1)}, u32[]{:S(2)}, u32[]{:S(2)}) async-start(f32[8,40,128]{2,1,0:T(8,128)} %bitcast.1), calls=%async_computation | async-start | bytes 327680 | tf_op jit(solution)/shard_map/all_to_all | solution.py:617
  15.3 0.7 %copy-start.4 = (f32[3,128]{1,0:T(4,128)S(1)}, f32[3,128]{1,0:T(4,128)}, u32[]{:S(2)}) copy-start(f32[3,128]{1,0:T(4,128)} %size_ref.3) | copy-start | bytes 4612
  15.9 6.9 %copy-start.1 = (f32[125,192]{1,0:T(8,128)S(1)}, f32[125,192]{1,0:T(8,128)}, u32[]{:S(2)}) copy-start(f32[125,192]{1,0:T(8,128)} %constant.14.clone.lift_ref) | copy-start | bytes 288004

commit v5 on v4

--- a/solution.py
+++ b/solution.py
@@ -96,21 +96,6 @@
     return tuple(m.astype(np.float32) for m in (faces, volume, lift))
 
 
-def slot_lanes(parts, capacity, fringes):
-    remote = parts * capacity
-    lanes = np.zeros((8, LANES), np.int32)
-    for d in range(3):
-        held = {}
-        for lane in range(remote):
-            held[d * remote + lane] = lane % parts * capacity + lane // parts
-        for i in range(fringes):
-            held[(3 * remote + d * fringes + i) % LANES] = remote + i
-        free = iter(range(remote + fringes, LANES))
-        for lane in range(LANES):
-            lanes[d, lane] = held[lane] if lane in held else next(free)
-    return lanes
-
-
 def fringe_lanes(fringes):
     found = np.zeros((8, LANES), np.int32)
     for side in range(2):
@@ -184,20 +169,51 @@
     ]
 
 
-def table_kernel(out_ref):
-    row = lax.broadcasted_iota(jnp.int32, out_ref.shape, 0)
-    column = lax.broadcasted_iota(jnp.int32, out_ref.shape, 1) & 15
+def floor_divide(values, divisor):
+    return ((values.astype(jnp.float32) + 0.5) * (1.0 / divisor)).astype(jnp.int32)
+
+
+def table_kernel(parts, capacity, fringes, expand_ref, lanes_ref):
+    row = lax.broadcasted_iota(jnp.int32, expand_ref.shape, 0)
+    column = lax.broadcasted_iota(jnp.int32, expand_ref.shape, 1) & 15
     point = row & (ROWS - 1)
     point = jnp.where(point >= 25, point - 25, point)
-    tens = ((point.astype(jnp.float32) + 0.5) * 0.2).astype(jnp.int32)
+    tens = floor_divide(point, 5)
     wanted = jnp.where(row < ROWS, 5 + tens, 10 + point - 5 * tens)
-    out_ref[...] = jnp.where(column == wanted, 1.0, 0.0).astype(jnp.bfloat16)
-
-
-def donor_kernel(grids, parts, count, *refs):
-    states, cell_refs, weight_refs, expand_ref = refs[0:2], refs[2:4], refs[4:6], refs[6]
-    outs = refs[7 : 7 + grids // 2]
-    cells, weights, planes, values = refs[7 + grids // 2 :]
+    expand_ref[...] = jnp.where(column == wanted, 1.0, 0.0).astype(jnp.bfloat16)
+    me = lax.axis_index("dom")
+    remote = parts * capacity
+    row = lax.broadcasted_iota(jnp.int32, (8, LANES), 0)
+    lane = lax.broadcasted_iota(jnp.int32, (8, LANES), 1)
+    total = jnp.zeros((8, LANES), jnp.int32)
+    for d in range(3):
+        near = jnp.clip(lane - d * remote, 0, remote - 1)
+        away = floor_divide(near, capacity)
+        slot = (away ^ me) * capacity + near - away * capacity
+        edge = (lane - 3 * remote - d * fringes) & (LANES - 1)
+        start = (3 * remote + d * fringes) % LANES
+        taken = jnp.clip(lane - d * remote, 0, remote) + jnp.clip(
+            lane - start, 0, min(fringes, LANES - start)
+        )
+        if start + fringes > LANES:
+            taken = taken + jnp.clip(lane, 0, start + fringes - LANES)
+        other = remote + fringes + lane - taken
+        slot = jnp.where(
+            in_lanes(lane, d * remote, remote),
+            slot,
+            jnp.where(edge < fringes, remote + edge, other),
+        )
+        total = jnp.where(row == d, slot, total)
+    lanes_ref[...] = total
+
+
+def donor_kernel(grids, parts, count, height, *refs):
+    states, cell_refs, weight_refs, expand_ref, pay_ref = *(refs[k : k + 2] for k in (0, 2, 4)), *refs[6:8]
+    keep_ref, side_ref = refs[8:10]
+    outs = refs[10 : 8 + grids]
+    cells, weights, planes, values = refs[8 + grids :]
+    outer = parts // 2
+    side_ref[: outer * height, :] = pay_ref[outer * height :, :]
     span = parts * count
     total = grids * span
     blocks = values.shape[1] - 1
@@ -221,6 +237,7 @@
     row = lax.broadcasted_iota(jnp.int32, (8, width), 0)
     lane = lax.broadcasted_iota(jnp.int32, (8, LANES), 1)
     me = lax.axis_index("grid")
+    here = lax.axis_index("dom")
     number = 0
     for step in range(0, grids, 2):
         start = partner(me, step) * span
@@ -241,11 +258,11 @@
             tiles = []
             for top in range(0, LANES, 8):
                 a = top // 25
-                outer = jnp.broadcast_to(held[a : a + 1], (8, width))
+                factor = jnp.broadcast_to(held[a : a + 1], (8, width))
                 if top < 25 * (a + 1) < top + 8 and a < 4:
                     later = jnp.broadcast_to(held[a + 1 : a + 2], (8, width))
-                    outer = jnp.where(row < 25 * (a + 1) - top, outer, later)
-                tiles.append(outer * planes[number, top % 25 : top % 25 + 8, :])
+                    factor = jnp.where(row < 25 * (a + 1) - top, factor, later)
+                tiles.append(factor * planes[number, top % 25 : top % 25 + 8, :])
             weight = jnp.concatenate(tiles, axis=0)[:125]
             for v in range(5):
                 picked = jnp.dot(
@@ -259,7 +276,7 @@
             place = (step + source - 1) * count
             wanted = in_lanes(lane, place, count)
             for q in range(parts):
-                offset = start - first * LANES + q * count
+                offset = start - first * LANES + partner(here, q) * count
                 block = offset // LANES
                 index = lane + (offset - block * LANES - place)
                 inside = index & (LANES - 1)
@@ -267,14 +284,19 @@
                 far = lane_gather(values[number, block + 1], inside)
                 found[q] = jnp.where(wanted, jnp.where(index < LANES, near, far), found[q])
             number += 1
-        for q in range(parts):
-            outs[step // 2][q] = found[q]
+        for z in range(outer):
+            if step:
+                outs[step - 2][z] = found[2 * z]
+                outs[step - 1][z] = found[2 * z + 1]
+            else:
+                keep_ref[z] = found[2 * z]
+                side_ref[outer * height + 8 * z : outer * height + 8 * z + 8, :] = found[2 * z + 1]
 
 
 def face_kernel(
     parts,
     capacity,
-    rows,
+    height,
     state_ref,
     plus_ref,
     minus_ref,
@@ -314,21 +336,26 @@
             turn[side, 25 * v : 25 * v + 25, :] = both[:25]
         turned = turn[side].T
         for d in range(3):
-            for s in range(capacity):
-                start = d * remote + s * parts
-                pay_ref[pl.ds((2 * d + side) * capacity + s, parts, stride=rows), :] = turned[
-                    start : start + parts
-                ]
-
-
-def merge_kernel(parts, rows, first, pay_ref, *refs):
-    out_ref = refs[-1]
-    for q in range(parts):
-        total = refs[0][q]
-        for extra in refs[1:-1]:
-            total = total + extra[q]
-        out_ref[q * rows : q * rows + first, :] = pay_ref[q * rows : q * rows + first, :]
-        out_ref[q * rows + first : q * rows + first + 8, :] = total
+            for q in range(parts):
+                start = d * remote + q * capacity
+                place = (q % 2 * (parts // 2) + q // 2) * height + (2 * d + side) * capacity
+                pay_ref[place : place + capacity, :] = turned[start : start + capacity]
+
+
+def repack_kernel(outer, height, pay_ref, keep_ref, side_ref, *refs):
+    pairs = (len(refs) - outer) // 2
+    across, straight, outs = refs[:pairs], refs[pairs : 2 * pairs], refs[2 * pairs :]
+    for z in range(outer):
+        outs[z][:height, :] = pay_ref[z * height : (z + 1) * height, :]
+        outs[z][height : 2 * height, :] = side_ref[z * height : (z + 1) * height, :]
+        total = keep_ref[z]
+        for extra in straight:
+            total = total + extra[z]
+        outs[z][2 * height : 2 * height + 8, :] = total
+        total = side_ref[outer * height + 8 * z : outer * height + 8 * z + 8, :]
+        for extra in across:
+            total = total + extra[z]
+        outs[z][2 * height + 8 : 2 * height + 16, :] = total
 
 
 def volume_kernel(
@@ -422,38 +449,27 @@
         inside = (points >= block * LANES) & (points < (block + 1) * LANES)
         picked = lane_gather(held, jnp.where(inside, points - block * LANES, 0))
         slot = jnp.where(inside, picked, slot)
-    device = ((slot.astype(jnp.float32) + 0.5) * (1.0 / count)).astype(jnp.int32)
+    device = floor_divide(slot, count)
     rest = slot - device * count
-    grid = ((device.astype(jnp.float32) + 0.5) * (1.0 / parts)).astype(jnp.int32)
+    grid = floor_divide(device, parts)
     step = jnp.zeros_like(grid)
     for g in range(grids):
         away = partner(me, g)
         step = jnp.where(grid == g, away, step)
-    where_ref[0] = device - grid * parts
+    where_ref[0] = (device - grid * parts) ^ lax.axis_index("dom")
     where_ref[1] = jnp.maximum(step - 1, 0) * count + rest
 
 
-def finish_kernel(
-    parts,
-    capacity,
-    rows,
-    first,
-    fringes,
-    come_ref,
-    both_ref,
-    flux_ref,
-    edge_ref,
-    local_ref,
-    back_ref,
-    where_ref,
-    part_ref,
-    size_ref,
-    lift_ref,
-    out_ref,
-    turn,
-    turned,
-    wide,
-):
+def distances(outer):
+    return [0, outer - 1, *range(1, outer - 1)]
+
+
+def finish_kernel(parts, capacity, height, fringes, *refs):
+    come = dict(zip(distances(parts // 2), refs[: parts // 2]))
+    both_ref, flux_ref, edge_ref, local_ref, back_ref, where_ref, part_ref, size_ref, lift_ref = refs[
+        parts // 2 : parts // 2 + 9
+    ]
+    out_ref, turn, turned, wide = refs[parts // 2 + 9 :]
     remote = parts * capacity
     row = lax.broadcasted_iota(jnp.int32, (ROWS, LANES), 0)
     lane = lax.broadcasted_iota(jnp.int32, (ROWS, LANES), 1)
@@ -465,18 +481,18 @@
     spread = jnp.where(any_fringe[:8], spread, 0)
     for side in range(2):
         for d in range(3):
-            for s in range(capacity):
-                start = d * remote + s * parts
-                turn[side, start : start + parts, :] = come_ref[
-                    pl.ds((2 * d + 1 - side) * capacity + s, parts, stride=rows), :
-                ]
+            for q in range(parts):
+                start = d * remote + q * capacity
+                place = q % 2 * height + (2 * d + 1 - side) * capacity
+                turn[side, start : start + capacity, :] = come[q // 2][place : place + capacity, :]
         turned[side, :LANES, :] = turn[side].T
     fringe = []
     for v in range(5):
-        sent = come_ref[pl.ds(first + v, parts, stride=rows), :]
         total = jnp.zeros((8, LANES), jnp.float32)
         for q in range(parts):
-            picked = lane_gather(jnp.broadcast_to(sent[q : q + 1], (8, LANES)), where_ref[1])
+            place = 2 * height + q % 2 * 8 + v
+            sent = come[q // 2][place : place + 1, :]
+            picked = lane_gather(jnp.broadcast_to(sent, (8, LANES)), where_ref[1])
             total = jnp.where(where_ref[0] == q, picked, total)
         fringe.append(total)
     for side in range(2):
@@ -540,36 +556,61 @@
     total = donor_cell.shape[-1]
     count = total // (grids * parts)
     held = -(-recv_slot.shape[-1] // LANES) * LANES
-    first = -(-6 * capacity // 8) * 8
-    rows = first + 8
+    outer = parts // 2
+    height = -(-6 * capacity // 8) * 8
+    span = parts * count
+    blocks = (2 * (LANES - 1) + span) // LANES
+    sets = grids - 1
+    held_blocks = -(-total // LANES) + blocks
     faces, volume, lift = matrices()
-    lanes = slot_lanes(parts, capacity, fringes)
     points = fringe_lanes(fringes)
     f32 = functools.partial(jax.ShapeDtypeStruct, dtype=jnp.float32)
     i32 = functools.partial(jax.ShapeDtypeStruct, dtype=jnp.int32)
     memory = functools.partial(pltpu.VMEM, dtype=jnp.float32)
 
-    span = parts * count
-    blocks = (2 * (LANES - 1) + span) // LANES
-    sets = grids - 1
-    held_blocks = -(-total // LANES) + blocks
-
-    def exchange(values, step):
-        return lax.ppermute(values, "grid", [(g, partner(g, step)) for g in range(grids)])
-
-    expand = call(
-        table_kernel,
+    def exchange(values, step, move):
+        pairs = [
+            (g * parts + q, partner(g, step) * parts + partner(q, move))
+            for g in range(grids)
+            for q in range(parts)
+        ]
+        return lax.ppermute(values, ("grid", "dom"), pairs)
+
+    weights = donor_weights.reshape(15, 1, total)
+    mates = [exchange(values, 1, 0) for values in (state, donor_cell, weights)]
+    expand, lanes = call(
+        functools.partial(table_kernel, parts, capacity, fringes),
         "tables",
-        jax.ShapeDtypeStruct((2 * ROWS, 48), jnp.bfloat16),
+        (jax.ShapeDtypeStruct((2 * ROWS, 48), jnp.bfloat16), i32((8, LANES))),
         [],
         400_000_000,
         3_000_000,
     )
-    weights = donor_weights.reshape(15, 1, total)
-    sent = call(
-        functools.partial(donor_kernel, grids, parts, count),
+    slots, both, pay = call(
+        functools.partial(face_kernel, parts, capacity, height),
+        "faces",
+        (
+            f32((6, 5, ROWS, LANES)),
+            f32((2, 5, ROWS, LANES)),
+            f32((parts * height, LANES)),
+        ),
+        [memory((2, LANES, LANES))],
+        200_000_000,
+        1_500_000,
+        state,
+        plus_order,
+        minus_order,
+        faces,
+        lanes,
+    )
+    keep, side, *sent = call(
+        functools.partial(donor_kernel, grids, parts, count, height),
         "donors",
-        tuple(f32((parts, 8, LANES)) for _ in range(grids // 2)),
+        (
+            f32((outer, 8, LANES)),
+            f32((outer * (height + 8), LANES)),
+            *(f32((outer, 8, LANES)) for _ in range(grids - 2)),
+        ),
         [
             pltpu.VMEM((2, held_blocks, 8, LANES), jnp.int32),
             memory((2, held_blocks, 16, LANES)),
@@ -579,44 +620,31 @@
         5_000_000,
         500_000,
         state,
-        exchange(state, 1),
+        mates[0],
         donor_cell,
-        exchange(donor_cell, 1),
+        mates[1],
         weights,
-        exchange(weights, 1),
+        mates[2],
         expand,
-    )
-    arrived = [sent[0]] + [exchange(sent[k], 2 * k) for k in range(1, grids // 2)]
-    slots, both, pay = call(
-        functools.partial(face_kernel, parts, capacity, rows),
-        "faces",
-        (
-            f32((6, 5, ROWS, LANES)),
-            f32((2, 5, ROWS, LANES)),
-            f32((parts * rows, LANES)),
-        ),
-        [memory((2, LANES, LANES))],
-        200_000_000,
-        1_500_000,
-        state,
-        plus_order,
-        minus_order,
-        faces,
-        lanes,
-    )
-    pay = call(
-        functools.partial(merge_kernel, parts, rows, first),
-        "merge",
-        f32((parts * rows, LANES)),
+        pay,
+    )
+    side = exchange(side, 0, 1)
+    across = [exchange(sent[k + 1], k + 2, 1) for k in range(0, grids - 2, 2)]
+    straight = [exchange(sent[k], k + 2, 0) for k in range(0, grids - 2, 2)]
+    packed = call(
+        functools.partial(repack_kernel, outer, height),
+        "repack",
+        tuple(f32((2 * height + 16, LANES)) for _ in range(outer)),
         [],
         50_000,
         200_000,
         pay,
-        *arrived,
-    )
-    come = lax.all_to_all(
-        pay.reshape(parts, rows, LANES), "dom", split_axis=0, concat_axis=0, tiled=True
-    )
+        keep,
+        side,
+        *across,
+        *straight,
+    )
+    come = [exchange(packed[z], 0, 2 * z) if z else packed[z] for z in distances(outer)]
     part, flux, edge, local, back, where = call(
         functools.partial(volume_kernel, grids, parts, count, remote, fringes),
         "volume",
@@ -647,7 +675,7 @@
         points,
     )
     return call(
-        functools.partial(finish_kernel, parts, capacity, rows, first, fringes),
+        functools.partial(finish_kernel, parts, capacity, height, fringes),
         "finish",
         f32((5, 125, columns)),
         [
@@ -657,7 +685,7 @@
         ],
         200_000_000,
         3_000_000,
-        come.reshape(parts * rows, LANES),
+        *come,
         both,
         flux,
         edge,

time: 24.6 us -> 21.8 us (0.89)
  waiting for transfers between devices: 8.22 us -> 7.02 us
  starting transfers between devices: 10.3 us -> 9.65 us
  Pallas kernels: 4.97 us -> 4.36 us
    all_to_all x1 -> x0, starting transfers between devices: 6.45 us -> none  [body(): lax.all_to_all(pay.reshape(parts, rows, LANES), 'dom', split_axis=0, conc...]
    all_to_all x1 -> x0, waiting for transfers between devices: 6.12 us -> none  [body(): lax.all_to_all(pay.reshape(parts, rows, LANES), 'dom', split_axis=0, conc...]
    ppermute x4 -> x9, starting transfers between devices: 3.9 us -> 9.65 us  [exchange(): return lax.ppermute(values, ('grid', 'dom'), pairs)]
    ppermute x4 -> x9, waiting for transfers between devices: 2.1 us -> 7.02 us  [exchange(): return lax.ppermute(values, ('grid', 'dom'), pairs)]
    pallas_call x6, Pallas kernels: 4.97 us -> 4.36 us  [call(): pl.pallas_call(kernel, name=name, out_shape=out_shape, scratch_shapes=scr...]
    unnamed x24 -> x22, local copies, waits for them, and re-layouts: 0.7 us -> 0.51 us
  transfers between devices with their start and end apart: 5 -> 9, of which waited for: 3 -> 5; matrix products, arithmetic and copies ran while one was open for 0% -> 0% of each run, Pallas kernels for 6% -> 7%
where the time goes in v5:
time: 21.8 us; the launch traced here: 21.6 us
  starting transfers between devices  9.65 us (44%)
  waiting for transfers between devices  7.02 us (32%)
  Pallas kernels  4.36 us (20%)
  local copies, waits for them, and re-layouts  0.51 us (2%)
    ppermute x9, starting transfers between devices, exchange(): return lax.ppermute(values, ('grid', 'dom'), pairs)  9.65 us
    ppermute x9, waiting for transfers between devices, exchange(): return lax.ppermute(values, ('grid', 'dom'), pairs)  7.02 us
    pallas_call x6, Pallas kernels, call(): pl.pallas_call(kernel, name=name, out_shape=out_shape, scratch_shapes=scr...  4.36 us
    unnamed x22, local copies, waits for them, and re-layouts  0.51 us
  transfers between devices with their start and end apart: 9, of which 5 were waited for; matrix products, arithmetic and copies ran while one was open for 0% of the time, Pallas kernels for 7%

profile of v5, /device:TPU:0, one launch (start us, length us, event | category | flops | bytes accessed | tf_op | source)
XLA Modules:
  0.0 21.6 jit_solution(2285437235872873604)
XLA Ops:
  0.0 0.5 %collective-permute-start = (f32[5,125,128]{2,1,0:T(8,128)}, f32[5,125,128]{2,1,0:T(8,128)S(1)}, u32[]{:S(2)}, u32[]{:S(2)}) collective-permute-start(f32[5,125,128]{2,1,0:T(8,128)} %state_ref.3), channel_id=1, source_target_pairs={{0,8},{1,9},{2,10},{3,11},{4,12},{5,13},{6,14},{7,15},{8,0},{9,1},... | collective-permute-start | bytes 960008 | tf_op jit(solution)/shard_map/ppermute | solution.py:577
  0.5 0.0 copy-start
  0.5 0.0 copy-start.6
  0.5 0.0 copy-start.7
  0.5 0.0 copy-start.9
  0.5 0.1 collective-permute-start.2
  0.6 0.5 %collective-permute-start.1 = (s32[1,1184]{1,0:T(1,128)}, s32[1,1184]{1,0:T(1,128)S(1)}, u32[]{:S(2)}, u32[]{:S(2)}) collective-permute-start(s32[1,1184]{1,0:T(1,128)} %refs_2_.1), channel_id=1, source_target_pairs={{0,8},{1,9},{2,10},{3,11},{4,12},{5,13},{6,14},{7,15},{8,0},{9,1},... | collective-permute-start | bytes 14216 | tf_op jit(solution)/shard_map/ppermute | solution.py:577
  1.1 0.3 %copy-done = f32[5,125,128]{2,1,0:T(8,128)S(1)} copy-done((f32[5,125,128]{2,1,0:T(8,128)S(1)}, f32[5,125,128]{2,1,0:T(8,128)}, u32[]{:S(2)}) %copy-start) | copy-done | bytes 320024
  1.4 0.0 copy-done.6
  1.4 0.0 copy-done.7
  1.4 0.0 copy-done.9
  1.5 0.0 copy-start.2
  1.5 0.0 copy-start.3
  1.5 0.8 %faces.1 = (f32[6,5,32,128]{3,2,1,0:T(8,128)S(1)}, f32[2,5,32,128]{3,2,1,0:T(8,128)S(1)}, f32[256,128]{1,0:T(8,128)S(1)}) custom-call(f32[5,125,128]{2,1,0:T(8,128)S(1)} %copy-done, s32[3,128]{1,0:T(4,128)S(1)} %copy-done.6, s32[3,128]{1,0:T(4,128)S(1)} %copy-done.7, f32[192,125]{1,0:T(8,128)S(1)} %copy-done.9, s32[8,128]{1,0:T(8,128)S(1)} %get-tuple-element.24.lanes_ref), custom_call_target="tpu_custom_call" | custom-call | flops 200000000 | bytes 1500000 | tf_op jit(solution)/shard_map/faces/pallas_call | solution.py:538
  2.3 0.0 collective-permute-done.1.refs_3_
  2.3 0.0 collective-permute-done.2.refs_5_
  2.3 0.0 collective-permute-done.refs_1_
  2.3 0.1 copy-done.2
  2.4 0.0 copy-done.3
  2.4 1.2 %donors.1 = (f32[4,8,128]{2,1,0:T(8,128)S(1)}, f32[160,128]{1,0:T(8,128)S(1)}, f32[4,8,128]{2,1,0:T(8,128)S(1)}, f32[4,8,128]{2,1,0:T(8,128)S(1)}) custom-call(f32[5,125,128]{2,1,0:T(8,128)S(1)} %copy-done, f32[5,125,128]{2,1,0:T(8,128)S(1)} %collective-permute-done.refs_1_, s32[1,1184]{1,0:T(1,128)S(1)} %copy-done.3, ...), custom_call_target="tpu_custom_call" | custom-call | flops 5000000 | bytes 500000 | tf_op jit(solution)/shard_map/donors/pallas_call | solution.py:538
  3.6 0.0 copy-start.8
  3.6 2.6 %collective-permute-start.3 = (f32[160,128]{1,0:T(8,128)S(1)}, f32[160,128]{1,0:T(8,128)S(1)}, u32[]{:S(2)}, u32[]{:S(2)}) collective-permute-start(f32[160,128]{1,0:T(8,128)S(1)} %get-tuple-element.28), channel_id=1, source_target_pairs={{0,1},{1,0},{2,3},{3,2},{4,5},{5,4},{6,7},{7,6},{8,9},{9,8},{10,11... | collective-permute-start | bytes 245768 | tf_op jit(solution)/shard_map/ppermute | solution.py:577
  6.2 1.5 %collective-permute-start.4 = (f32[4,8,128]{2,1,0:T(8,128)S(1)}, f32[4,8,128]{2,1,0:T(8,128)S(1)}, u32[]{:S(2)}, u32[]{:S(2)}) collective-permute-start(f32[4,8,128]{2,1,0:T(8,128)S(1)} %get-tuple-element.29), channel_id=1, source_target_pairs={{0,17},{1,16},{2,19},{3,18},{4,21},{5,20},{6,23},{7,22},{8,25},{9,... | collective-permute-start | bytes 49160 | tf_op jit(solution)/shard_map/ppermute | solution.py:577
  7.7 0.0 collective-permute-start.5
  7.8 3.1 %collective-permute-done.4.refs_0_ = f32[4,8,128]{2,1,0:T(8,128)S(1)} collective-permute-done((f32[4,8,128]{2,1,0:T(8,128)S(1)}, f32[4,8,128]{2,1,0:T(8,128)S(1)}, u32[]{:S(2)}, u32[]{:S(2)}) %collective-permute-start.4) | collective-permute-done | bytes 16416 | tf_op jit(solution)/shard_map/ppermute | solution.py:577
  10.9 0.6 %collective-permute-done.5.refs_1_ = f32[4,8,128]{2,1,0:T(8,128)S(1)} collective-permute-done((f32[4,8,128]{2,1,0:T(8,128)S(1)}, f32[4,8,128]{2,1,0:T(8,128)S(1)}, u32[]{:S(2)}, u32[]{:S(2)}) %collective-permute-start.5) | collective-permute-done | bytes 16416 | tf_op jit(solution)/shard_map/ppermute | solution.py:577
  11.5 0.0 collective-permute-done.3.side_ref
  11.5 0.0 copy-start.10
  11.5 3.7 %collective-permute-start.6 = (f32[80,128]{1,0:T(8,128)S(1)}, f32[80,128]{1,0:T(8,128)S(1)}, u32[]{:S(2)}, u32[]{:S(2)}) collective-permute-start(f32[80,128]{1,0:T(8,128)S(1)} %get-tuple-element.32), channel_id=1, source_target_pairs={{0,6},{1,7},{2,4},{3,5},{4,2},{5,3},{6,0},{7,1},{8,14},{9,15},{10,... | collective-permute-start | bytes 122888 | tf_op jit(solution)/shard_map/ppermute | solution.py:577
  15.2 0.0 copy-start.5
  15.2 0.0 collective-permute-start.7
  15.2 0.0 copy-start.4
  15.2 0.8 %collective-permute-start.8 = (f32[80,128]{1,0:T(8,128)S(1)}, f32[80,128]{1,0:T(8,128)S(1)}, u32[]{:S(2)}, u32[]{:S(2)}) collective-permute-start(f32[80,128]{1,0:T(8,128)S(1)} %get-tuple-element.34), channel_id=1, source_target_pairs={{0,4},{1,5},{2,6},{3,7},{4,0},{5,1},{6,2},{7,3},{8,12},{9,13},{10,... | collective-permute-start | bytes 122888 | tf_op jit(solution)/shard_map/ppermute | solution.py:577
  16.0 0.0 copy-done.8
  16.0 0.0 copy-done.10
  16.0 0.0 copy-done.5
  16.0 0.0 copy-done.4
  16.0 0.0 copy-start.1
  16.0 0.8 %volume.1 = (f32[125,640]{1,0:T(8,128)S(1)}, f32[2,6,32,128]{3,2,1,0:T(8,128)S(1)}, f32[2,11,32,128]{3,2,1,0:T(8,128)S(1)}, f32[3,5,32,128]{3,2,1,0:T(8,128)S(1)...) custom-call(f32[5,125,128]{2,1,0:T(8,128)S(1)} %copy-done, f32[3,128]{1,0:T(4,128)S(1)} %copy-done.4, ...), custom_call_target="tpu_custom_call" | custom-call | flops 400000000 | bytes 3000000 | tf_op jit(solution)/shard_map/volume/pallas_call | solution.py:538
  16.8 0.7 %collective-permute-done.6.refs_1_ = f32[80,128]{1,0:T(8,128)S(1)} collective-permute-done((f32[80,128]{1,0:T(8,128)S(1)}, f32[80,128]{1,0:T(8,128)S(1)}, u32[]{:S(2)}, u32[]{:S(2)}) %collective-permute-start.6) | collective-permute-done | bytes 40992 | tf_op jit(solution)/shard_map/ppermute | solution.py:577
  17.5 1.7 %collective-permute-done.7.refs_2_ = f32[80,128]{1,0:T(8,128)S(1)} collective-permute-done((f32[80,128]{1,0:T(8,128)S(1)}, f32[80,128]{1,0:T(8,128)S(1)}, u32[]{:S(2)}, u32[]{:S(2)}) %collective-permute-start.7) | collective-permute-done | bytes 40992 | tf_op jit(solution)/shard_map/ppermute | solution.py:577
  19.2 0.9 %collective-permute-done.8.refs_3_ = f32[80,128]{1,0:T(8,128)S(1)} collective-permute-done((f32[80,128]{1,0:T(8,128)S(1)}, f32[80,128]{1,0:T(8,128)S(1)}, u32[]{:S(2)}, u32[]{:S(2)}) %collective-permute-start.8) | collective-permute-done | bytes 40992 | tf_op jit(solution)/shard_map/ppermute | solution.py:577
  20.1 0.0 copy-done.1
  20.1 1.6 %finish.1 = f32[5,125,128]{2,1,0:T(8,128)} custom-call(f32[80,128]{1,0:T(8,128)S(1)} %get-tuple-element.31.refs_0_, f32[80,128]{1,0:T(8,128)S(1)} %collective-permute-done.6.refs_1_, f32[80,128]{1,0:T(8,128)S(1)} %collective-permute-done.7.refs_2_, f32[80,128]{1,0:T(8,128)S(1)} %collective-permute-done.8.refs_3_, ...), custom_call_target="tpu_custom_call" | custom-call | flops 200000000 | bytes 3000000 | tf_op jit(solution)/shard_map/finish/pallas_call | solution.py:538
  (2 shorter events, 0.1 us)
Async XLA Ops:
  0.0 2.3 %collective-permute-start = (f32[5,125,128]{2,1,0:T(8,128)}, f32[5,125,128]{2,1,0:T(8,128)S(1)}, u32[]{:S(2)}, u32[]{:S(2)}) collective-permute-start(f32[5,125,128]{2,1,0:T(8,128)} %state_ref.3), channel_id=1, source_target_pairs={{0,8},{1,9},{2,10},{3,11},{4,12},{5,13},{6,14},{7,15},{8,0},{9,1},... | collective-permute-start | bytes 960008 | tf_op jit(solution)/shard_map/ppermute | solution.py:577
  0.5 1.0 %copy-start = (f32[5,125,128]{2,1,0:T(8,128)S(1)}, f32[5,125,128]{2,1,0:T(8,128)}, u32[]{:S(2)}) copy-start(f32[5,125,128]{2,1,0:T(8,128)} %state_ref.3) | copy-start | bytes 960004
  0.5 1.0 %copy-start.6 = (s32[3,128]{1,0:T(4,128)S(1)}, s32[3,128]{1,0:T(4,128)}, u32[]{:S(2)}) copy-start(s32[3,128]{1,0:T(4,128)} %plus_ref.3) | copy-start | bytes 4612
  0.5 1.0 %copy-start.7 = (s32[3,128]{1,0:T(4,128)S(1)}, s32[3,128]{1,0:T(4,128)}, u32[]{:S(2)}) copy-start(s32[3,128]{1,0:T(4,128)} %minus_ref.3) | copy-start | bytes 4612
  0.5 1.0 %copy-start.9 = (f32[192,125]{1,0:T(8,128)S(1)}, f32[192,125]{1,0:T(8,128)}, u32[]{:S(2)}) copy-start(f32[192,125]{1,0:T(8,128)} %constant.8.clone.faces_ref) | copy-start | bytes 288004
  0.5 1.8 %collective-permute-start.2 = (f32[15,1,1184]{2,1,0:T(1,128)}, f32[15,1,1184]{2,1,0:T(1,128)S(1)}, u32[]{:S(2)}, u32[]{:S(2)}) collective-permute-start(f32[15,1,1184]{2,1,0:T(1,128)} %bitcast.1), channel_id=1, source_target_pairs={{0,8},{1,9},{2,10},{3,11},{4,12},{5,13},{6,14},{7,15},{8,0},{9,1},... | collective-permute-start | bytes 213128 | tf_op jit(solution)/shard_map/ppermute | solution.py:577
  0.6 1.7 %collective-permute-start.1 = (s32[1,1184]{1,0:T(1,128)}, s32[1,1184]{1,0:T(1,128)S(1)}, u32[]{:S(2)}, u32[]{:S(2)}) collective-permute-start(s32[1,1184]{1,0:T(1,128)} %refs_2_.1), channel_id=1, source_target_pairs={{0,8},{1,9},{2,10},{3,11},{4,12},{5,13},{6,14},{7,15},{8,0},{9,1},... | collective-permute-start | bytes 14216 | tf_op jit(solution)/shard_map/ppermute | solution.py:577
  1.5 0.9 %copy-start.2 = (f32[1,3,5,1184]{3,0,2,1:T(1,128)S(1)}, f32[1,3,5,1184]{3,0,2,1:T(1,128)}, u32[]{:S(2)}) copy-start(f32[1,3,5,1184]{3,0,2,1:T(1,128)} %param.16) | copy-start | bytes 213124
  1.5 0.9 %copy-start.3 = (s32[1,1184]{1,0:T(1,128)S(1)}, s32[1,1184]{1,0:T(1,128)}, u32[]{:S(2)}) copy-start(s32[1,1184]{1,0:T(1,128)} %refs_2_.1) | copy-start | bytes 14212
  3.6 12.4 %copy-start.8 = (f32[125,384]{1,0:T(8,128)S(1)}, f32[125,384]{1,0:T(8,128)}, u32[]{:S(2)}) copy-start(f32[125,384]{1,0:T(8,128)} %constant.9.clone.volume_ref) | copy-start | bytes 576004
  3.6 7.9 %collective-permute-start.3 = (f32[160,128]{1,0:T(8,128)S(1)}, f32[160,128]{1,0:T(8,128)S(1)}, u32[]{:S(2)}, u32[]{:S(2)}) collective-permute-start(f32[160,128]{1,0:T(8,128)S(1)} %get-tuple-element.28), channel_id=1, source_target_pairs={{0,1},{1,0},{2,3},{3,2},{4,5},{5,4},{6,7},{7,6},{8,9},{9,8},{10,11... | collective-permute-start | bytes 245768 | tf_op jit(solution)/shard_map/ppermute | solution.py:577
  6.2 4.6 %collective-permute-start.4 = (f32[4,8,128]{2,1,0:T(8,128)S(1)}, f32[4,8,128]{2,1,0:T(8,128)S(1)}, u32[]{:S(2)}, u32[]{:S(2)}) collective-permute-start(f32[4,8,128]{2,1,0:T(8,128)S(1)} %get-tuple-element.29), channel_id=1, source_target_pairs={{0,17},{1,16},{2,19},{3,18},{4,21},{5,20},{6,23},{7,22},{8,25},{9,... | collective-permute-start | bytes 49160 | tf_op jit(solution)/shard_map/ppermute | solution.py:577
  7.7 3.7 %collective-permute-start.5 = (f32[4,8,128]{2,1,0:T(8,128)S(1)}, f32[4,8,128]{2,1,0:T(8,128)S(1)}, u32[]{:S(2)}, u32[]{:S(2)}) collective-permute-start(f32[4,8,128]{2,1,0:T(8,128)S(1)} %get-tuple-element.30), channel_id=1, source_target_pairs={{0,16},{1,17},{2,18},{3,19},{4,20},{5,21},{6,22},{7,23},{8,24},{9,... | collective-permute-start | bytes 49160 | tf_op jit(solution)/shard_map/ppermute | solution.py:577
  11.5 4.5 %copy-start.10 = (s32[8,128]{1,0:T(8,128)S(1)}, s32[8,128]{1,0:T(8,128)}, u32[]{:S(2)}) copy-start(s32[8,128]{1,0:T(8,128)} %constant.10.clone.points_ref) | copy-start | bytes 12292
  11.5 6.0 %collective-permute-start.6 = (f32[80,128]{1,0:T(8,128)S(1)}, f32[80,128]{1,0:T(8,128)S(1)}, u32[]{:S(2)}, u32[]{:S(2)}) collective-permute-start(f32[80,128]{1,0:T(8,128)S(1)} %get-tuple-element.32), channel_id=1, source_target_pairs={{0,6},{1,7},{2,4},{3,5},{4,2},{5,3},{6,0},{7,1},{8,14},{9,15},{10,... | collective-permute-start | bytes 122888 | tf_op jit(solution)/shard_map/ppermute | solution.py:577
  15.2 0.8 %copy-start.5 = (s32[1,600]{1,0:T(1,128)S(1)}, s32[1,600]{1,0:T(1,128)}, u32[]{:S(2)}) copy-start(s32[1,600]{1,0:T(1,128)} %recv_ref.1) | copy-start | bytes 7204
  15.2 4.0 %collective-permute-start.7 = (f32[80,128]{1,0:T(8,128)S(1)}, f32[80,128]{1,0:T(8,128)S(1)}, u32[]{:S(2)}, u32[]{:S(2)}) collective-permute-start(f32[80,128]{1,0:T(8,128)S(1)} %get-tuple-element.33), channel_id=1, source_target_pairs={{0,2},{1,3},{2,0},{3,1},{4,6},{5,7},{6,4},{7,5},{8,10},{9,11},{10,... | collective-permute-start | bytes 122888 | tf_op jit(solution)/shard_map/ppermute | solution.py:577
  15.2 0.8 %copy-start.4 = (f32[3,128]{1,0:T(4,128)S(1)}, f32[3,128]{1,0:T(4,128)}, u32[]{:S(2)}) copy-start(f32[3,128]{1,0:T(4,128)} %refs_11_.1) | copy-start | bytes 4612
  15.2 4.9 %collective-permute-start.8 = (f32[80,128]{1,0:T(8,128)S(1)}, f32[80,128]{1,0:T(8,128)S(1)}, u32[]{:S(2)}, u32[]{:S(2)}) collective-permute-start(f32[80,128]{1,0:T(8,128)S(1)} %get-tuple-element.34), channel_id=1, source_target_pairs={{0,4},{1,5},{2,6},{3,7},{4,0},{5,1},{6,2},{7,3},{8,12},{9,13},{10,... | collective-permute-start | bytes 122888 | tf_op jit(solution)/shard_map/ppermute | solution.py:577
  16.0 4.1 %copy-start.1 = (f32[125,192]{1,0:T(8,128)S(1)}, f32[125,192]{1,0:T(8,128)}, u32[]{:S(2)}) copy-start(f32[125,192]{1,0:T(8,128)} %constant.11.clone.refs_12_) | copy-start | bytes 288004

commit v6 on v5

--- a/solution.py
+++ b/solution.py
@@ -3,13 +3,13 @@
 
 import jax
 import jax.numpy as jnp
+import ml_dtypes
 import numpy as np
 from jax import lax
 from jax.experimental import pallas as pl
 from jax.experimental.pallas import tpu as pltpu
 from jax.sharding import PartitionSpec as P
 
-precise = lax.Precision.HIGHEST
 closer = lax.Precision.HIGH
 LANES = 128
 SHIFT = (1.0, 0.0, 0.0, 0.0, 2.5)
@@ -308,9 +308,9 @@
     turn,
 ):
     remote = parts * capacity
-    wide = jnp.concatenate([state_ref[v] for v in range(5)], axis=1)
+    wide = jnp.concatenate([state_ref[v] - SHIFT[v] for v in range(5)], axis=1)
     face = jnp.dot(
-        faces_ref[...], wide, precision=precise, preferred_element_type=jnp.float32
+        faces_ref[...], wide, precision=closer, preferred_element_type=jnp.float32
     )
     for side in range(2):
         order = (minus_ref, plus_ref)[side]
@@ -322,7 +322,7 @@
             )
             for v in range(5):
                 block = face[k * ROWS : (k + 1) * ROWS, v * LANES : (v + 1) * LANES]
-                slots_ref[k, v] = lane_gather(block, index)
+                slots_ref[k, v] = lane_gather(block, index) + SHIFT[v]
     lane = lax.broadcasted_iota(jnp.int32, (ROWS, LANES), 1)
     turn[:, 120:128, :] = jnp.zeros((2, 8, LANES), jnp.float32)
     for side in range(2):
@@ -527,9 +527,12 @@
                 wide[k * ROWS : (k + 1) * ROWS, v * LANES : (v + 1) * LANES] = (
                     lane_gather(value, index) * scale
                 )
-    total = part_ref[...] + jnp.dot(
-        lift_ref[...], wide[...], precision=closer, preferred_element_type=jnp.float32
-    )
+    values = wide[...]
+    high = values.astype(jnp.bfloat16)
+    low = (values - high.astype(jnp.float32)).astype(jnp.bfloat16)
+    first = jnp.dot(lift_ref[...], high, preferred_element_type=jnp.float32)
+    second = jnp.dot(lift_ref[:LANES], low, preferred_element_type=jnp.float32)
+    total = part_ref[...] + (first[:125] + (first[LANES : LANES + 125] + second[:125]))
     for v in range(5):
         out_ref[v] = total[:, v * LANES : (v + 1) * LANES]
 
@@ -563,6 +566,9 @@
     sets = grids - 1
     held_blocks = -(-total // LANES) + blocks
     faces, volume, lift = matrices()
+    lift = np.pad(lift, ((0, LANES - 125), (0, 0)))
+    high = lift.astype(ml_dtypes.bfloat16)
+    lift = np.concatenate([high, (lift - high.astype(np.float32)).astype(ml_dtypes.bfloat16)])
     points = fringe_lanes(fringes)
     f32 = functools.partial(jax.ShapeDtypeStruct, dtype=jnp.float32)
     i32 = functools.partial(jax.ShapeDtypeStruct, dtype=jnp.int32)

time: 21.8 us -> 21.8 us (level)
  transfers between devices with their start and end apart: 9 -> 9, of which waited for: 5 -> 5; matrix products, arithmetic and copies ran while one was open for 0% -> 0% of each run, Pallas kernels for 7% -> 6%
where the time goes in v6:
time: 21.8 us; the launch traced here: 21.6 us
  starting transfers between devices  9.65 us (44%)
  waiting for transfers between devices  7.04 us (32%)
  Pallas kernels  4.15 us (19%)
  local copies, waits for them, and re-layouts  0.71 us (3%)
    ppermute x9, starting transfers between devices, exchange(): return lax.ppermute(values, ('grid', 'dom'), pairs)  9.65 us
    ppermute x9, waiting for transfers between devices, exchange(): return lax.ppermute(values, ('grid', 'dom'), pairs)  7.04 us
    pallas_call x6, Pallas kernels, call(): pl.pallas_call(kernel, name=name, out_shape=out_shape, scratch_shapes=scr...  4.15 us
    unnamed x22, local copies, waits for them, and re-layouts  0.71 us
  transfers between devices with their start and end apart: 9, of which 5 were waited for; matrix products, arithmetic and copies ran while one was open for 0% of the time, Pallas kernels for 6%

profile of v6, /device:TPU:0, one launch (start us, length us, event | category | flops | bytes accessed | tf_op | source)
XLA Modules:
  0.0 21.6 jit_solution(13667183578451317546)
XLA Ops:
  0.0 0.5 %collective-permute-start = (f32[5,125,128]{2,1,0:T(8,128)}, f32[5,125,128]{2,1,0:T(8,128)S(1)}, u32[]{:S(2)}, u32[]{:S(2)}) collective-permute-start(f32[5,125,128]{2,1,0:T(8,128)} %state_ref.3), channel_id=1, source_target_pairs={{0,8},{1,9},{2,10},{3,11},{4,12},{5,13},{6,14},{7,15},{8,0},{9,1},... | collective-permute-start | bytes 960008 | tf_op jit(solution)/shard_map/ppermute | solution.py:583
  0.5 0.0 copy-start
  0.5 0.0 copy-start.6
  0.5 0.0 copy-start.7
  0.5 0.0 copy-start.9
  0.5 0.1 collective-permute-start.2
  0.6 0.5 %collective-permute-start.1 = (s32[1,1184]{1,0:T(1,128)}, s32[1,1184]{1,0:T(1,128)S(1)}, u32[]{:S(2)}, u32[]{:S(2)}) collective-permute-start(s32[1,1184]{1,0:T(1,128)} %refs_2_.1), channel_id=1, source_target_pairs={{0,8},{1,9},{2,10},{3,11},{4,12},{5,13},{6,14},{7,15},{8,0},{9,1},... | collective-permute-start | bytes 14216 | tf_op jit(solution)/shard_map/ppermute | solution.py:583
  1.1 0.3 %copy-done = f32[5,125,128]{2,1,0:T(8,128)S(1)} copy-done((f32[5,125,128]{2,1,0:T(8,128)S(1)}, f32[5,125,128]{2,1,0:T(8,128)}, u32[]{:S(2)}) %copy-start) | copy-done | bytes 320024
  1.4 0.0 copy-done.6
  1.4 0.0 copy-done.7
  1.4 0.0 copy-done.9
  1.5 0.0 copy-start.2
  1.5 0.0 copy-start.3
  1.5 0.6 %faces.1 = (f32[6,5,32,128]{3,2,1,0:T(8,128)S(1)}, f32[2,5,32,128]{3,2,1,0:T(8,128)S(1)}, f32[256,128]{1,0:T(8,128)S(1)}) custom-call(f32[5,125,128]{2,1,0:T(8,128)S(1)} %copy-done, s32[3,128]{1,0:T(4,128)S(1)} %copy-done.6, s32[3,128]{1,0:T(4,128)S(1)} %copy-done.7, f32[192,125]{1,0:T(8,128)S(1)} %copy-done.9, s32[8,128]{1,0:T(8,128)S(1)} %get-tuple-element.24.lanes_ref), custom_call_target="tpu_custom_call" | custom-call | flops 200000000 | bytes 1500000 | tf_op jit(solution)/shard_map/faces/pallas_call | solution.py:541
  2.1 0.0 collective-permute-done.1.refs_3_
  2.1 0.0 collective-permute-done.2.refs_5_
  2.1 0.0 collective-permute-done.refs_1_
  2.1 0.3 %copy-done.2 = f32[1,3,5,1184]{3,0,2,1:T(1,128)S(1)} copy-done((f32[1,3,5,1184]{3,0,2,1:T(1,128)S(1)}, f32[1,3,5,1184]{3,0,2,1:T(1,128)}, u32[]{:S(2)}) %copy-start.2) | copy-done | bytes 71064
  2.4 0.0 copy-done.3
  2.4 1.2 %donors.1 = (f32[4,8,128]{2,1,0:T(8,128)S(1)}, f32[160,128]{1,0:T(8,128)S(1)}, f32[4,8,128]{2,1,0:T(8,128)S(1)}, f32[4,8,128]{2,1,0:T(8,128)S(1)}) custom-call(f32[5,125,128]{2,1,0:T(8,128)S(1)} %copy-done, f32[5,125,128]{2,1,0:T(8,128)S(1)} %collective-permute-done.refs_1_, s32[1,1184]{1,0:T(1,128)S(1)} %copy-done.3, ...), custom_call_target="tpu_custom_call" | custom-call | flops 5000000 | bytes 500000 | tf_op jit(solution)/shard_map/donors/pallas_call | solution.py:541
  3.6 0.0 copy-start.8
  3.6 2.6 %collective-permute-start.3 = (f32[160,128]{1,0:T(8,128)S(1)}, f32[160,128]{1,0:T(8,128)S(1)}, u32[]{:S(2)}, u32[]{:S(2)}) collective-permute-start(f32[160,128]{1,0:T(8,128)S(1)} %get-tuple-element.28), channel_id=1, source_target_pairs={{0,1},{1,0},{2,3},{3,2},{4,5},{5,4},{6,7},{7,6},{8,9},{9,8},{10,11... | collective-permute-start | bytes 245768 | tf_op jit(solution)/shard_map/ppermute | solution.py:583
  6.2 1.5 %collective-permute-start.4 = (f32[4,8,128]{2,1,0:T(8,128)S(1)}, f32[4,8,128]{2,1,0:T(8,128)S(1)}, u32[]{:S(2)}, u32[]{:S(2)}) collective-permute-start(f32[4,8,128]{2,1,0:T(8,128)S(1)} %get-tuple-element.29), channel_id=1, source_target_pairs={{0,17},{1,16},{2,19},{3,18},{4,21},{5,20},{6,23},{7,22},{8,25},{9,... | collective-permute-start | bytes 49160 | tf_op jit(solution)/shard_map/ppermute | solution.py:583
  7.7 0.0 collective-permute-start.5
  7.8 3.1 %collective-permute-done.4.refs_0_ = f32[4,8,128]{2,1,0:T(8,128)S(1)} collective-permute-done((f32[4,8,128]{2,1,0:T(8,128)S(1)}, f32[4,8,128]{2,1,0:T(8,128)S(1)}, u32[]{:S(2)}, u32[]{:S(2)}) %collective-permute-start.4) | collective-permute-done | bytes 16416 | tf_op jit(solution)/shard_map/ppermute | solution.py:583
  10.9 0.6 %collective-permute-done.5.refs_1_ = f32[4,8,128]{2,1,0:T(8,128)S(1)} collective-permute-done((f32[4,8,128]{2,1,0:T(8,128)S(1)}, f32[4,8,128]{2,1,0:T(8,128)S(1)}, u32[]{:S(2)}, u32[]{:S(2)}) %collective-permute-start.5) | collective-permute-done | bytes 16416 | tf_op jit(solution)/shard_map/ppermute | solution.py:583
  11.5 0.0 collective-permute-done.3.side_ref
  11.5 0.0 copy-start.10
  11.5 3.7 %collective-permute-start.6 = (f32[80,128]{1,0:T(8,128)S(1)}, f32[80,128]{1,0:T(8,128)S(1)}, u32[]{:S(2)}, u32[]{:S(2)}) collective-permute-start(f32[80,128]{1,0:T(8,128)S(1)} %get-tuple-element.32), channel_id=1, source_target_pairs={{0,6},{1,7},{2,4},{3,5},{4,2},{5,3},{6,0},{7,1},{8,14},{9,15},{10,... | collective-permute-start | bytes 122888 | tf_op jit(solution)/shard_map/ppermute | solution.py:583
  15.2 0.0 copy-start.5
  15.2 0.0 collective-permute-start.7
  15.2 0.0 copy-start.4
  15.2 0.8 %collective-permute-start.8 = (f32[80,128]{1,0:T(8,128)S(1)}, f32[80,128]{1,0:T(8,128)S(1)}, u32[]{:S(2)}, u32[]{:S(2)}) collective-permute-start(f32[80,128]{1,0:T(8,128)S(1)} %get-tuple-element.34), channel_id=1, source_target_pairs={{0,4},{1,5},{2,6},{3,7},{4,0},{5,1},{6,2},{7,3},{8,12},{9,13},{10,... | collective-permute-start | bytes 122888 | tf_op jit(solution)/shard_map/ppermute | solution.py:583
  16.0 0.0 copy-done.8
  16.0 0.0 copy-done.10
  16.0 0.0 copy-done.5
  16.0 0.0 copy-done.4
  16.0 0.0 copy-start.1
  16.0 0.8 %volume.1 = (f32[125,640]{1,0:T(8,128)S(1)}, f32[2,6,32,128]{3,2,1,0:T(8,128)S(1)}, f32[2,11,32,128]{3,2,1,0:T(8,128)S(1)}, f32[3,5,32,128]{3,2,1,0:T(8,128)S(1)...) custom-call(f32[5,125,128]{2,1,0:T(8,128)S(1)} %copy-done, f32[3,128]{1,0:T(4,128)S(1)} %copy-done.4, ...), custom_call_target="tpu_custom_call" | custom-call | flops 400000000 | bytes 3000000 | tf_op jit(solution)/shard_map/volume/pallas_call | solution.py:541
  16.8 0.7 %collective-permute-done.6.refs_1_ = f32[80,128]{1,0:T(8,128)S(1)} collective-permute-done((f32[80,128]{1,0:T(8,128)S(1)}, f32[80,128]{1,0:T(8,128)S(1)}, u32[]{:S(2)}, u32[]{:S(2)}) %collective-permute-start.6) | collective-permute-done | bytes 40992 | tf_op jit(solution)/shard_map/ppermute | solution.py:583
  17.5 1.7 %collective-permute-done.7.refs_2_ = f32[80,128]{1,0:T(8,128)S(1)} collective-permute-done((f32[80,128]{1,0:T(8,128)S(1)}, f32[80,128]{1,0:T(8,128)S(1)}, u32[]{:S(2)}, u32[]{:S(2)}) %collective-permute-start.7) | collective-permute-done | bytes 40992 | tf_op jit(solution)/shard_map/ppermute | solution.py:583
  19.2 0.9 %collective-permute-done.8.refs_3_ = f32[80,128]{1,0:T(8,128)S(1)} collective-permute-done((f32[80,128]{1,0:T(8,128)S(1)}, f32[80,128]{1,0:T(8,128)S(1)}, u32[]{:S(2)}, u32[]{:S(2)}) %collective-permute-start.8) | collective-permute-done | bytes 40992 | tf_op jit(solution)/shard_map/ppermute | solution.py:583
  20.1 0.0 copy-done.1
  20.1 1.5 %finish.1 = f32[5,125,128]{2,1,0:T(8,128)} custom-call(f32[80,128]{1,0:T(8,128)S(1)} %get-tuple-element.31.refs_0_, f32[80,128]{1,0:T(8,128)S(1)} %collective-permute-done.6.refs_1_, f32[80,128]{1,0:T(8,128)S(1)} %collective-permute-done.7.refs_2_, f32[80,128]{1,0:T(8,128)S(1)} %collective-permute-done.8.refs_3_, ...), custom_call_target="tpu_custom_call" | custom-call | flops 200000000 | bytes 3000000 | tf_op jit(solution)/shard_map/finish/pallas_call | solution.py:541
  (2 shorter events, 0.1 us)
Async XLA Ops:
  0.0 2.1 %collective-permute-start = (f32[5,125,128]{2,1,0:T(8,128)}, f32[5,125,128]{2,1,0:T(8,128)S(1)}, u32[]{:S(2)}, u32[]{:S(2)}) collective-permute-start(f32[5,125,128]{2,1,0:T(8,128)} %state_ref.3), channel_id=1, source_target_pairs={{0,8},{1,9},{2,10},{3,11},{4,12},{5,13},{6,14},{7,15},{8,0},{9,1},... | collective-permute-start | bytes 960008 | tf_op jit(solution)/shard_map/ppermute | solution.py:583
  0.5 1.0 %copy-start = (f32[5,125,128]{2,1,0:T(8,128)S(1)}, f32[5,125,128]{2,1,0:T(8,128)}, u32[]{:S(2)}) copy-start(f32[5,125,128]{2,1,0:T(8,128)} %state_ref.3) | copy-start | bytes 960004
  0.5 1.0 %copy-start.6 = (s32[3,128]{1,0:T(4,128)S(1)}, s32[3,128]{1,0:T(4,128)}, u32[]{:S(2)}) copy-start(s32[3,128]{1,0:T(4,128)} %plus_ref.3) | copy-start | bytes 4612
  0.5 1.0 %copy-start.7 = (s32[3,128]{1,0:T(4,128)S(1)}, s32[3,128]{1,0:T(4,128)}, u32[]{:S(2)}) copy-start(s32[3,128]{1,0:T(4,128)} %minus_ref.3) | copy-start | bytes 4612
  0.5 1.0 %copy-start.9 = (f32[192,125]{1,0:T(8,128)S(1)}, f32[192,125]{1,0:T(8,128)}, u32[]{:S(2)}) copy-start(f32[192,125]{1,0:T(8,128)} %constant.8.clone.faces_ref) | copy-start | bytes 288004
  0.5 1.6 %collective-permute-start.2 = (f32[15,1,1184]{2,1,0:T(1,128)}, f32[15,1,1184]{2,1,0:T(1,128)S(1)}, u32[]{:S(2)}, u32[]{:S(2)}) collective-permute-start(f32[15,1,1184]{2,1,0:T(1,128)} %bitcast.1), channel_id=1, source_target_pairs={{0,8},{1,9},{2,10},{3,11},{4,12},{5,13},{6,14},{7,15},{8,0},{9,1},... | collective-permute-start | bytes 213128 | tf_op jit(solution)/shard_map/ppermute | solution.py:583
  0.6 1.5 %collective-permute-start.1 = (s32[1,1184]{1,0:T(1,128)}, s32[1,1184]{1,0:T(1,128)S(1)}, u32[]{:S(2)}, u32[]{:S(2)}) collective-permute-start(s32[1,1184]{1,0:T(1,128)} %refs_2_.1), channel_id=1, source_target_pairs={{0,8},{1,9},{2,10},{3,11},{4,12},{5,13},{6,14},{7,15},{8,0},{9,1},... | collective-permute-start | bytes 14216 | tf_op jit(solution)/shard_map/ppermute | solution.py:583
  1.5 0.9 %copy-start.2 = (f32[1,3,5,1184]{3,0,2,1:T(1,128)S(1)}, f32[1,3,5,1184]{3,0,2,1:T(1,128)}, u32[]{:S(2)}) copy-start(f32[1,3,5,1184]{3,0,2,1:T(1,128)} %param.16) | copy-start | bytes 213124
  1.5 0.9 %copy-start.3 = (s32[1,1184]{1,0:T(1,128)S(1)}, s32[1,1184]{1,0:T(1,128)}, u32[]{:S(2)}) copy-start(s32[1,1184]{1,0:T(1,128)} %refs_2_.1) | copy-start | bytes 14212
  3.6 12.4 %copy-start.8 = (f32[125,384]{1,0:T(8,128)S(1)}, f32[125,384]{1,0:T(8,128)}, u32[]{:S(2)}) copy-start(f32[125,384]{1,0:T(8,128)} %constant.9.clone.volume_ref) | copy-start | bytes 576004
  3.6 7.9 %collective-permute-start.3 = (f32[160,128]{1,0:T(8,128)S(1)}, f32[160,128]{1,0:T(8,128)S(1)}, u32[]{:S(2)}, u32[]{:S(2)}) collective-permute-start(f32[160,128]{1,0:T(8,128)S(1)} %get-tuple-element.28), channel_id=1, source_target_pairs={{0,1},{1,0},{2,3},{3,2},{4,5},{5,4},{6,7},{7,6},{8,9},{9,8},{10,11... | collective-permute-start | bytes 245768 | tf_op jit(solution)/shard_map/ppermute | solution.py:583
  6.2 4.6 %collective-permute-start.4 = (f32[4,8,128]{2,1,0:T(8,128)S(1)}, f32[4,8,128]{2,1,0:T(8,128)S(1)}, u32[]{:S(2)}, u32[]{:S(2)}) collective-permute-start(f32[4,8,128]{2,1,0:T(8,128)S(1)} %get-tuple-element.29), channel_id=1, source_target_pairs={{0,17},{1,16},{2,19},{3,18},{4,21},{5,20},{6,23},{7,22},{8,25},{9,... | collective-permute-start | bytes 49160 | tf_op jit(solution)/shard_map/ppermute | solution.py:583
  7.7 3.7 %collective-permute-start.5 = (f32[4,8,128]{2,1,0:T(8,128)S(1)}, f32[4,8,128]{2,1,0:T(8,128)S(1)}, u32[]{:S(2)}, u32[]{:S(2)}) collective-permute-start(f32[4,8,128]{2,1,0:T(8,128)S(1)} %get-tuple-element.30), channel_id=1, source_target_pairs={{0,16},{1,17},{2,18},{3,19},{4,20},{5,21},{6,22},{7,23},{8,24},{9,... | collective-permute-start | bytes 49160 | tf_op jit(solution)/shard_map/ppermute | solution.py:583
  11.5 4.5 %copy-start.10 = (s32[8,128]{1,0:T(8,128)S(1)}, s32[8,128]{1,0:T(8,128)}, u32[]{:S(2)}) copy-start(s32[8,128]{1,0:T(8,128)} %constant.10.clone.points_ref) | copy-start | bytes 12292
  11.5 6.0 %collective-permute-start.6 = (f32[80,128]{1,0:T(8,128)S(1)}, f32[80,128]{1,0:T(8,128)S(1)}, u32[]{:S(2)}, u32[]{:S(2)}) collective-permute-start(f32[80,128]{1,0:T(8,128)S(1)} %get-tuple-element.32), channel_id=1, source_target_pairs={{0,6},{1,7},{2,4},{3,5},{4,2},{5,3},{6,0},{7,1},{8,14},{9,15},{10,... | collective-permute-start | bytes 122888 | tf_op jit(solution)/shard_map/ppermute | solution.py:583
  15.2 0.8 %copy-start.5 = (s32[1,600]{1,0:T(1,128)S(1)}, s32[1,600]{1,0:T(1,128)}, u32[]{:S(2)}) copy-start(s32[1,600]{1,0:T(1,128)} %recv_ref.1) | copy-start | bytes 7204
  15.2 4.0 %collective-permute-start.7 = (f32[80,128]{1,0:T(8,128)S(1)}, f32[80,128]{1,0:T(8,128)S(1)}, u32[]{:S(2)}, u32[]{:S(2)}) collective-permute-start(f32[80,128]{1,0:T(8,128)S(1)} %get-tuple-element.33), channel_id=1, source_target_pairs={{0,2},{1,3},{2,0},{3,1},{4,6},{5,7},{6,4},{7,5},{8,10},{9,11},{10,... | collective-permute-start | bytes 122888 | tf_op jit(solution)/shard_map/ppermute | solution.py:583
  15.2 0.8 %copy-start.4 = (f32[3,128]{1,0:T(4,128)S(1)}, f32[3,128]{1,0:T(4,128)}, u32[]{:S(2)}) copy-start(f32[3,128]{1,0:T(4,128)} %refs_11_.1) | copy-start | bytes 4612
  15.2 4.9 %collective-permute-start.8 = (f32[80,128]{1,0:T(8,128)S(1)}, f32[80,128]{1,0:T(8,128)S(1)}, u32[]{:S(2)}, u32[]{:S(2)}) collective-permute-start(f32[80,128]{1,0:T(8,128)S(1)} %get-tuple-element.34), channel_id=1, source_target_pairs={{0,4},{1,5},{2,6},{3,7},{4,0},{5,1},{6,2},{7,3},{8,12},{9,13},{10,... | collective-permute-start | bytes 122888 | tf_op jit(solution)/shard_map/ppermute | solution.py:583
  16.0 4.1 %copy-start.1 = (bf16[256,192]{1,0:T(8,128)(2,1)S(1)}, bf16[256,192]{1,0:T(8,128)(2,1)}, u32[]{:S(2)}) copy-start(bf16[256,192]{1,0:T(8,128)(2,1)} %constant.11.clone.refs_12_) | copy-start | bytes 294916

commit v7 on v6

--- a/solution.py
+++ b/solution.py
@@ -342,9 +342,9 @@
                 pay_ref[place : place + capacity, :] = turned[start : start + capacity]
 
 
-def repack_kernel(outer, height, pay_ref, keep_ref, side_ref, *refs):
-    pairs = (len(refs) - outer) // 2
-    across, straight, outs = refs[:pairs], refs[pairs : 2 * pairs], refs[2 * pairs :]
+def repack_kernel(outer, height, pay_ref, keep_ref, *refs):
+    pairs = (len(refs) - outer - 1) // 2
+    across, side_ref, straight, outs = refs[:pairs], refs[pairs], refs[pairs + 1 : 2 * pairs + 1], refs[2 * pairs + 1 :]
     for z in range(outer):
         outs[z][:height, :] = pay_ref[z * height : (z + 1) * height, :]
         outs[z][height : 2 * height, :] = side_ref[z * height : (z + 1) * height, :]
@@ -461,7 +461,7 @@
 
 
 def distances(outer):
-    return [0, outer - 1, *range(1, outer - 1)]
+    return [0, *sorted(range(1, outer), key=lambda z: (z ^ (outer // 2)) % outer)]
 
 
 def finish_kernel(parts, capacity, height, fringes, *refs):
@@ -646,8 +646,8 @@
         200_000,
         pay,
         keep,
+        *across,
         side,
-        *across,
         *straight,
     )
     come = [exchange(packed[z], 0, 2 * z) if z else packed[z] for z in distances(outer)]

time: 21.8 us -> 21.7 us (level)
  local copies, waits for them, and re-layouts: 0.71 us -> 1.14 us
  waiting for transfers between devices: 7.04 us -> 6.72 us
  starting transfers between devices: 9.65 us -> 9.43 us
    unnamed x22, local copies, waits for them, and re-layouts: 0.71 us -> 1.14 us
    ppermute x9, waiting for transfers between devices: 7.04 us -> 6.72 us  [exchange(): return lax.ppermute(values, ('grid', 'dom'), pairs)]
  transfers between devices with their start and end apart: 9 -> 9, of which waited for: 5 -> 3; matrix products, arithmetic and copies ran while one was open for 0% -> 0% of each run, Pallas kernels for 6% -> 6%
where the time goes in v7:
time: 21.7 us; the launch traced here: 21.5 us
  starting transfers between devices  9.43 us (43%)
  waiting for transfers between devices  6.72 us (31%)
  Pallas kernels  4.14 us (19%)
  local copies, waits for them, and re-layouts  1.14 us (5%)
    ppermute x9, starting transfers between devices, exchange(): return lax.ppermute(values, ('grid', 'dom'), pairs)  9.43 us
    ppermute x9, waiting for transfers between devices, exchange(): return lax.ppermute(values, ('grid', 'dom'), pairs)  6.72 us
    pallas_call x6, Pallas kernels, call(): pl.pallas_call(kernel, name=name, out_shape=out_shape, scratch_shapes=scr...  4.14 us
    unnamed x22, local copies, waits for them, and re-layouts  1.14 us
  transfers between devices with their start and end apart: 9, of which 3 were waited for; matrix products, arithmetic and copies ran while one was open for 0% of the time, Pallas kernels for 6%

profile of v7, /device:TPU:0, one launch (start us, length us, event | category | flops | bytes accessed | tf_op | source)
XLA Modules:
  0.0 21.5 jit_solution(14845408073050341719)
XLA Ops:
  0.0 0.5 %collective-permute-start = (f32[5,125,128]{2,1,0:T(8,128)}, f32[5,125,128]{2,1,0:T(8,128)S(1)}, u32[]{:S(2)}, u32[]{:S(2)}) collective-permute-start(f32[5,125,128]{2,1,0:T(8,128)} %state_ref.3), channel_id=1, source_target_pairs={{0,8},{1,9},{2,10},{3,11},{4,12},{5,13},{6,14},{7,15},{8,0},{9,1},... | collective-permute-start | bytes 960008 | tf_op jit(solution)/shard_map/ppermute | solution.py:583
  0.5 0.0 copy-start
  0.5 0.0 copy-start.6
  0.5 0.0 copy-start.7
  0.5 0.0 copy-start.9
  0.5 0.1 collective-permute-start.2
  0.6 0.5 %collective-permute-start.1 = (s32[1,1184]{1,0:T(1,128)}, s32[1,1184]{1,0:T(1,128)S(1)}, u32[]{:S(2)}, u32[]{:S(2)}) collective-permute-start(s32[1,1184]{1,0:T(1,128)} %refs_2_.1), channel_id=1, source_target_pairs={{0,8},{1,9},{2,10},{3,11},{4,12},{5,13},{6,14},{7,15},{8,0},{9,1},... | collective-permute-start | bytes 14216 | tf_op jit(solution)/shard_map/ppermute | solution.py:583
  1.1 0.3 %copy-done = f32[5,125,128]{2,1,0:T(8,128)S(1)} copy-done((f32[5,125,128]{2,1,0:T(8,128)S(1)}, f32[5,125,128]{2,1,0:T(8,128)}, u32[]{:S(2)}) %copy-start) | copy-done | bytes 320024
  1.4 0.0 copy-done.6
  1.4 0.0 copy-done.7
  1.4 0.0 copy-done.9
  1.5 0.0 copy-start.2
  1.5 0.0 copy-start.3
  1.5 0.6 %faces.1 = (f32[6,5,32,128]{3,2,1,0:T(8,128)S(1)}, f32[2,5,32,128]{3,2,1,0:T(8,128)S(1)}, f32[256,128]{1,0:T(8,128)S(1)}) custom-call(f32[5,125,128]{2,1,0:T(8,128)S(1)} %copy-done, s32[3,128]{1,0:T(4,128)S(1)} %copy-done.6, s32[3,128]{1,0:T(4,128)S(1)} %copy-done.7, f32[192,125]{1,0:T(8,128)S(1)} %copy-done.9, s32[8,128]{1,0:T(8,128)S(1)} %get-tuple-element.24.lanes_ref), custom_call_target="tpu_custom_call" | custom-call | flops 200000000 | bytes 1500000 | tf_op jit(solution)/shard_map/faces/pallas_call | solution.py:541
  2.1 0.0 collective-permute-done.1.refs_3_
  2.1 0.0 collective-permute-done.2.refs_5_
  2.1 0.0 collective-permute-done.refs_1_
  2.1 0.3 %copy-done.2 = f32[1,3,5,1184]{3,0,2,1:T(1,128)S(1)} copy-done((f32[1,3,5,1184]{3,0,2,1:T(1,128)S(1)}, f32[1,3,5,1184]{3,0,2,1:T(1,128)}, u32[]{:S(2)}) %copy-start.2) | copy-done | bytes 71064
  2.4 0.0 copy-done.3
  2.4 1.2 %donors.1 = (f32[4,8,128]{2,1,0:T(8,128)S(1)}, f32[160,128]{1,0:T(8,128)S(1)}, f32[4,8,128]{2,1,0:T(8,128)S(1)}, f32[4,8,128]{2,1,0:T(8,128)S(1)}) custom-call(f32[5,125,128]{2,1,0:T(8,128)S(1)} %copy-done, f32[5,125,128]{2,1,0:T(8,128)S(1)} %collective-permute-done.refs_1_, s32[1,1184]{1,0:T(1,128)S(1)} %copy-done.3, ...), custom_call_target="tpu_custom_call" | custom-call | flops 5000000 | bytes 500000 | tf_op jit(solution)/shard_map/donors/pallas_call | solution.py:541
  3.6 0.0 copy-start.8
  3.6 2.6 %collective-permute-start.4 = (f32[160,128]{1,0:T(8,128)S(1)}, f32[160,128]{1,0:T(8,128)S(1)}, u32[]{:S(2)}, u32[]{:S(2)}) collective-permute-start(f32[160,128]{1,0:T(8,128)S(1)} %get-tuple-element.29), channel_id=1, source_target_pairs={{0,1},{1,0},{2,3},{3,2},{4,5},{5,4},{6,7},{7,6},{8,9},{9,8},{10,11... | collective-permute-start | bytes 245768 | tf_op jit(solution)/shard_map/ppermute | solution.py:583
  6.2 1.5 %collective-permute-start.3 = (f32[4,8,128]{2,1,0:T(8,128)S(1)}, f32[4,8,128]{2,1,0:T(8,128)S(1)}, u32[]{:S(2)}, u32[]{:S(2)}) collective-permute-start(f32[4,8,128]{2,1,0:T(8,128)S(1)} %get-tuple-element.28), channel_id=1, source_target_pairs={{0,17},{1,16},{2,19},{3,18},{4,21},{5,20},{6,23},{7,22},{8,25},{9,... | collective-permute-start | bytes 49160 | tf_op jit(solution)/shard_map/ppermute | solution.py:583
  7.7 0.0 collective-permute-start.5
  7.8 3.1 %collective-permute-done.3.refs_0_ = f32[4,8,128]{2,1,0:T(8,128)S(1)} collective-permute-done((f32[4,8,128]{2,1,0:T(8,128)S(1)}, f32[4,8,128]{2,1,0:T(8,128)S(1)}, u32[]{:S(2)}, u32[]{:S(2)}) %collective-permute-start.3) | collective-permute-done | bytes 16416 | tf_op jit(solution)/shard_map/ppermute | solution.py:583
  10.9 0.6 %collective-permute-done.5.refs_2_ = f32[4,8,128]{2,1,0:T(8,128)S(1)} collective-permute-done((f32[4,8,128]{2,1,0:T(8,128)S(1)}, f32[4,8,128]{2,1,0:T(8,128)S(1)}, u32[]{:S(2)}, u32[]{:S(2)}) %collective-permute-start.5) | collective-permute-done | bytes 16416 | tf_op jit(solution)/shard_map/ppermute | solution.py:583
  11.5 0.0 collective-permute-done.4.refs_1_
  11.5 0.0 copy-start.10
  11.5 2.6 %collective-permute-start.6 = (f32[80,128]{1,0:T(8,128)S(1)}, f32[80,128]{1,0:T(8,128)S(1)}, u32[]{:S(2)}, u32[]{:S(2)}) collective-permute-start(f32[80,128]{1,0:T(8,128)S(1)} %get-tuple-element.32), channel_id=1, source_target_pairs={{0,4},{1,5},{2,6},{3,7},{4,0},{5,1},{6,2},{7,3},{8,12},{9,13},{10,... | collective-permute-start | bytes 122888 | tf_op jit(solution)/shard_map/ppermute | solution.py:583
  14.1 0.0 copy-start.5
  14.1 1.3 %collective-permute-start.7 = (f32[80,128]{1,0:T(8,128)S(1)}, f32[80,128]{1,0:T(8,128)S(1)}, u32[]{:S(2)}, u32[]{:S(2)}) collective-permute-start(f32[80,128]{1,0:T(8,128)S(1)} %get-tuple-element.33), channel_id=1, source_target_pairs={{0,6},{1,7},{2,4},{3,5},{4,2},{5,3},{6,0},{7,1},{8,14},{9,15},{10,... | collective-permute-start | bytes 122888 | tf_op jit(solution)/shard_map/ppermute | solution.py:583
  15.5 0.0 copy-start.4
  15.5 0.2 %collective-permute-start.8 = (f32[80,128]{1,0:T(8,128)S(1)}, f32[80,128]{1,0:T(8,128)S(1)}, u32[]{:S(2)}, u32[]{:S(2)}) collective-permute-start(f32[80,128]{1,0:T(8,128)S(1)} %get-tuple-element.34), channel_id=1, source_target_pairs={{0,2},{1,3},{2,0},{3,1},{4,6},{5,7},{6,4},{7,5},{8,10},{9,11},{10,... | collective-permute-start | bytes 122888 | tf_op jit(solution)/shard_map/ppermute | solution.py:583
  15.7 0.0 copy-done.8
  15.7 0.0 copy-done.10
  15.7 0.0 copy-done.5
  15.7 0.4 %copy-done.4 = f32[3,128]{1,0:T(4,128)S(1)} copy-done((f32[3,128]{1,0:T(4,128)S(1)}, f32[3,128]{1,0:T(4,128)}, u32[]{:S(2)}) %copy-start.4) | copy-done | bytes 1560
  16.2 0.0 copy-start.1
  16.2 0.8 %volume.1 = (f32[125,640]{1,0:T(8,128)S(1)}, f32[2,6,32,128]{3,2,1,0:T(8,128)S(1)}, f32[2,11,32,128]{3,2,1,0:T(8,128)S(1)}, f32[3,5,32,128]{3,2,1,0:T(8,128)S(1)...) custom-call(f32[5,125,128]{2,1,0:T(8,128)S(1)} %copy-done, f32[3,128]{1,0:T(4,128)S(1)} %copy-done.4, ...), custom_call_target="tpu_custom_call" | custom-call | flops 400000000 | bytes 3000000 | tf_op jit(solution)/shard_map/volume/pallas_call | solution.py:541
  16.9 0.0 collective-permute-done.6.refs_1_
  17.0 3.0 %collective-permute-done.7.refs_2_ = f32[80,128]{1,0:T(8,128)S(1)} collective-permute-done((f32[80,128]{1,0:T(8,128)S(1)}, f32[80,128]{1,0:T(8,128)S(1)}, u32[]{:S(2)}, u32[]{:S(2)}) %collective-permute-start.7) | collective-permute-done | bytes 40992 | tf_op jit(solution)/shard_map/ppermute | solution.py:583
  19.9 0.0 collective-permute-done.8.refs_3_
  19.9 0.0 copy-done.1
  20.0 1.5 %finish.1 = f32[5,125,128]{2,1,0:T(8,128)} custom-call(f32[80,128]{1,0:T(8,128)S(1)} %get-tuple-element.31.refs_0_, f32[80,128]{1,0:T(8,128)S(1)} %collective-permute-done.6.refs_1_, f32[80,128]{1,0:T(8,128)S(1)} %collective-permute-done.7.refs_2_, f32[80,128]{1,0:T(8,128)S(1)} %collective-permute-done.8.refs_3_, ...), custom_call_target="tpu_custom_call" | custom-call | flops 200000000 | bytes 3000000 | tf_op jit(solution)/shard_map/finish/pallas_call | solution.py:541
  (2 shorter events, 0.1 us)
Async XLA Ops:
  0.0 2.1 %collective-permute-start = (f32[5,125,128]{2,1,0:T(8,128)}, f32[5,125,128]{2,1,0:T(8,128)S(1)}, u32[]{:S(2)}, u32[]{:S(2)}) collective-permute-start(f32[5,125,128]{2,1,0:T(8,128)} %state_ref.3), channel_id=1, source_target_pairs={{0,8},{1,9},{2,10},{3,11},{4,12},{5,13},{6,14},{7,15},{8,0},{9,1},... | collective-permute-start | bytes 960008 | tf_op jit(solution)/shard_map/ppermute | solution.py:583
  0.5 1.0 %copy-start = (f32[5,125,128]{2,1,0:T(8,128)S(1)}, f32[5,125,128]{2,1,0:T(8,128)}, u32[]{:S(2)}) copy-start(f32[5,125,128]{2,1,0:T(8,128)} %state_ref.3) | copy-start | bytes 960004
  0.5 1.0 %copy-start.6 = (s32[3,128]{1,0:T(4,128)S(1)}, s32[3,128]{1,0:T(4,128)}, u32[]{:S(2)}) copy-start(s32[3,128]{1,0:T(4,128)} %plus_ref.3) | copy-start | bytes 4612
  0.5 1.0 %copy-start.7 = (s32[3,128]{1,0:T(4,128)S(1)}, s32[3,128]{1,0:T(4,128)}, u32[]{:S(2)}) copy-start(s32[3,128]{1,0:T(4,128)} %minus_ref.3) | copy-start | bytes 4612
  0.5 1.0 %copy-start.9 = (f32[192,125]{1,0:T(8,128)S(1)}, f32[192,125]{1,0:T(8,128)}, u32[]{:S(2)}) copy-start(f32[192,125]{1,0:T(8,128)} %constant.8.clone.faces_ref) | copy-start | bytes 288004
  0.5 1.6 %collective-permute-start.2 = (f32[15,1,1184]{2,1,0:T(1,128)}, f32[15,1,1184]{2,1,0:T(1,128)S(1)}, u32[]{:S(2)}, u32[]{:S(2)}) collective-permute-start(f32[15,1,1184]{2,1,0:T(1,128)} %bitcast.1), channel_id=1, source_target_pairs={{0,8},{1,9},{2,10},{3,11},{4,12},{5,13},{6,14},{7,15},{8,0},{9,1},... | collective-permute-start | bytes 213128 | tf_op jit(solution)/shard_map/ppermute | solution.py:583
  0.6 1.5 %collective-permute-start.1 = (s32[1,1184]{1,0:T(1,128)}, s32[1,1184]{1,0:T(1,128)S(1)}, u32[]{:S(2)}, u32[]{:S(2)}) collective-permute-start(s32[1,1184]{1,0:T(1,128)} %refs_2_.1), channel_id=1, source_target_pairs={{0,8},{1,9},{2,10},{3,11},{4,12},{5,13},{6,14},{7,15},{8,0},{9,1},... | collective-permute-start | bytes 14216 | tf_op jit(solution)/shard_map/ppermute | solution.py:583
  1.5 0.9 %copy-start.2 = (f32[1,3,5,1184]{3,0,2,1:T(1,128)S(1)}, f32[1,3,5,1184]{3,0,2,1:T(1,128)}, u32[]{:S(2)}) copy-start(f32[1,3,5,1184]{3,0,2,1:T(1,128)} %param.16) | copy-start | bytes 213124
  1.5 0.9 %copy-start.3 = (s32[1,1184]{1,0:T(1,128)S(1)}, s32[1,1184]{1,0:T(1,128)}, u32[]{:S(2)}) copy-start(s32[1,1184]{1,0:T(1,128)} %refs_2_.1) | copy-start | bytes 14212
  3.6 12.2 %copy-start.8 = (f32[125,384]{1,0:T(8,128)S(1)}, f32[125,384]{1,0:T(8,128)}, u32[]{:S(2)}) copy-start(f32[125,384]{1,0:T(8,128)} %constant.9.clone.volume_ref) | copy-start | bytes 576004
  3.6 7.9 %collective-permute-start.4 = (f32[160,128]{1,0:T(8,128)S(1)}, f32[160,128]{1,0:T(8,128)S(1)}, u32[]{:S(2)}, u32[]{:S(2)}) collective-permute-start(f32[160,128]{1,0:T(8,128)S(1)} %get-tuple-element.29), channel_id=1, source_target_pairs={{0,1},{1,0},{2,3},{3,2},{4,5},{5,4},{6,7},{7,6},{8,9},{9,8},{10,11... | collective-permute-start | bytes 245768 | tf_op jit(solution)/shard_map/ppermute | solution.py:583
  6.2 4.6 %collective-permute-start.3 = (f32[4,8,128]{2,1,0:T(8,128)S(1)}, f32[4,8,128]{2,1,0:T(8,128)S(1)}, u32[]{:S(2)}, u32[]{:S(2)}) collective-permute-start(f32[4,8,128]{2,1,0:T(8,128)S(1)} %get-tuple-element.28), channel_id=1, source_target_pairs={{0,17},{1,16},{2,19},{3,18},{4,21},{5,20},{6,23},{7,22},{8,25},{9,... | collective-permute-start | bytes 49160 | tf_op jit(solution)/shard_map/ppermute | solution.py:583
  7.7 3.7 %collective-permute-start.5 = (f32[4,8,128]{2,1,0:T(8,128)S(1)}, f32[4,8,128]{2,1,0:T(8,128)S(1)}, u32[]{:S(2)}, u32[]{:S(2)}) collective-permute-start(f32[4,8,128]{2,1,0:T(8,128)S(1)} %get-tuple-element.30), channel_id=1, source_target_pairs={{0,16},{1,17},{2,18},{3,19},{4,20},{5,21},{6,22},{7,23},{8,24},{9,... | collective-permute-start | bytes 49160 | tf_op jit(solution)/shard_map/ppermute | solution.py:583
  11.5 4.3 %copy-start.10 = (s32[8,128]{1,0:T(8,128)S(1)}, s32[8,128]{1,0:T(8,128)}, u32[]{:S(2)}) copy-start(s32[8,128]{1,0:T(8,128)} %constant.10.clone.points_ref) | copy-start | bytes 12292
  11.5 5.5 %collective-permute-start.6 = (f32[80,128]{1,0:T(8,128)S(1)}, f32[80,128]{1,0:T(8,128)S(1)}, u32[]{:S(2)}, u32[]{:S(2)}) collective-permute-start(f32[80,128]{1,0:T(8,128)S(1)} %get-tuple-element.32), channel_id=1, source_target_pairs={{0,4},{1,5},{2,6},{3,7},{4,0},{5,1},{6,2},{7,3},{8,12},{9,13},{10,... | collective-permute-start | bytes 122888 | tf_op jit(solution)/shard_map/ppermute | solution.py:583
  14.1 1.6 %copy-start.5 = (s32[1,600]{1,0:T(1,128)S(1)}, s32[1,600]{1,0:T(1,128)}, u32[]{:S(2)}) copy-start(s32[1,600]{1,0:T(1,128)} %recv_ref.1) | copy-start | bytes 7204
  14.1 5.8 %collective-permute-start.7 = (f32[80,128]{1,0:T(8,128)S(1)}, f32[80,128]{1,0:T(8,128)S(1)}, u32[]{:S(2)}, u32[]{:S(2)}) collective-permute-start(f32[80,128]{1,0:T(8,128)S(1)} %get-tuple-element.33), channel_id=1, source_target_pairs={{0,6},{1,7},{2,4},{3,5},{4,2},{5,3},{6,0},{7,1},{8,14},{9,15},{10,... | collective-permute-start | bytes 122888 | tf_op jit(solution)/shard_map/ppermute | solution.py:583
  15.5 0.7 %copy-start.4 = (f32[3,128]{1,0:T(4,128)S(1)}, f32[3,128]{1,0:T(4,128)}, u32[]{:S(2)}) copy-start(f32[3,128]{1,0:T(4,128)} %refs_11_.1) | copy-start | bytes 4612
  15.5 4.5 %collective-permute-start.8 = (f32[80,128]{1,0:T(8,128)S(1)}, f32[80,128]{1,0:T(8,128)S(1)}, u32[]{:S(2)}, u32[]{:S(2)}) collective-permute-start(f32[80,128]{1,0:T(8,128)S(1)} %get-tuple-element.34), channel_id=1, source_target_pairs={{0,2},{1,3},{2,0},{3,1},{4,6},{5,7},{6,4},{7,5},{8,10},{9,11},{10,... | collective-permute-start | bytes 122888 | tf_op jit(solution)/shard_map/ppermute | solution.py:583
  16.2 3.8 %copy-start.1 = (bf16[256,192]{1,0:T(8,128)(2,1)S(1)}, bf16[256,192]{1,0:T(8,128)(2,1)}, u32[]{:S(2)}) copy-start(bf16[256,192]{1,0:T(8,128)(2,1)} %constant.11.clone.refs_12_) | copy-start | bytes 294916

commit v8 on v7

--- a/solution.py
+++ b/solution.py
@@ -208,19 +208,21 @@
 
 
 def donor_kernel(grids, parts, count, height, *refs):
-    states, cell_refs, weight_refs, expand_ref, pay_ref = *(refs[k : k + 2] for k in (0, 2, 4)), *refs[6:8]
-    keep_ref, side_ref = refs[8:10]
+    states, cell_refs, weight_refs = (refs[k : k + 2] for k in (0, 2, 4))
+    expand_ref, pay_ref, keep_ref, side_ref = refs[6:10]
     outs = refs[10 : 8 + grids]
-    cells, weights, planes, values = refs[8 + grids :]
+    cells, weights, padded, planes, values = refs[8 + grids :]
     outer = parts // 2
     side_ref[: outer * height, :] = pay_ref[outer * height :, :]
     span = parts * count
     total = grids * span
     blocks = values.shape[1] - 1
-    width = blocks * LANES
     cells[...] = jnp.zeros_like(cells)
     weights[...] = jnp.zeros_like(weights)
-    halves = []
+    me = lax.axis_index("grid")
+    here = lax.axis_index("dom")
+    number = 0
+    places = []
     for source in range(2):
         for block in range(-(-total // LANES)):
             lanes = slice(block * LANES, min((block + 1) * LANES, total))
@@ -228,69 +230,71 @@
             cells[source, block, 0:1, :held] = cell_refs[source][:, lanes]
             for k in range(15):
                 weights[source, block, k : k + 1, :held] = weight_refs[source][k, :, lanes]
+        halves = []
         for v in range(5):
-            shifted = states[source][v] - SHIFT[v]
+            padded[source, v, 120:128, :] = jnp.zeros((8, LANES), jnp.float32)
+            padded[source, v, :125, :] = states[source][v] - SHIFT[v]
+            shifted = padded[source, v]
             high = shifted.astype(jnp.bfloat16)
             low = (shifted - high.astype(jnp.float32)).astype(jnp.bfloat16)
             halves.append(jnp.concatenate([high, low], axis=1))
-    element = lax.broadcasted_iota(jnp.int32, (LANES, width), 0)
-    row = lax.broadcasted_iota(jnp.int32, (8, width), 0)
+        halves = jnp.concatenate(halves, axis=0)
+        steps = range(0 if source else 2, grids, 2)
+        starts = [partner(me, step) * span for step in steps]
+        firsts = [start // LANES for start in starts]
+        width = len(steps) * blocks * LANES
+        pick = [(source, first + i) for first in firsts for i in range(blocks)]
+        held = jnp.concatenate([cells[at] for at in pick], axis=1)
+        element = lax.broadcasted_iota(jnp.int32, (LANES, width), 0)
+        chosen = jnp.where(element == held[0:1], 1.0, 0.0).astype(jnp.bfloat16)
+        chosen = jnp.concatenate([chosen, chosen], axis=0)
+        held = jnp.concatenate([weights[at] for at in pick], axis=1)
+        high = held.astype(jnp.bfloat16)
+        rest = held - high.astype(jnp.float32)
+        middle = rest.astype(jnp.bfloat16)
+        low = (rest - middle.astype(jnp.float32)).astype(jnp.bfloat16)
+        pieces = jnp.concatenate([high, middle, low], axis=0)
+        plane = jnp.dot(expand_ref[...], pieces, preferred_element_type=jnp.float32)
+        planes[source, :, :width] = plane[:ROWS] * plane[ROWS:]
+        row = lax.broadcasted_iota(jnp.int32, (8, width), 0)
+        tiles = []
+        for top in range(0, LANES, 8):
+            a = top // 25
+            factor = jnp.broadcast_to(held[a : a + 1], (8, width))
+            if a < 4 and 25 * (a + 1) < top + 8:
+                later = jnp.broadcast_to(held[a + 1 : a + 2], (8, width))
+                factor = jnp.where(row < 25 * (a + 1) - top, factor, later)
+            tiles.append(factor * planes[source, top % 25 : top % 25 + 8, :width])
+        weight = jnp.concatenate(tiles, axis=0)
+        picked = jnp.dot(halves, chosen, preferred_element_type=jnp.float32)
+        for v in range(5):
+            value = jnp.sum(picked[v * LANES : (v + 1) * LANES] * weight, axis=0, keepdims=True)
+            for k in range(len(steps) * blocks):
+                values[number + k // blocks, k % blocks, v : v + 1, :] = (
+                    value[:, k * LANES : (k + 1) * LANES] + SHIFT[v]
+                )
+        for step, start, first in zip(steps, starts, firsts):
+            places.append((number, step, (step + source - 1) * count, start - first * LANES))
+            number += 1
     lane = lax.broadcasted_iota(jnp.int32, (8, LANES), 1)
-    me = lax.axis_index("grid")
-    here = lax.axis_index("dom")
-    number = 0
-    for step in range(0, grids, 2):
-        start = partner(me, step) * span
-        first = start // LANES
-        found = [jnp.zeros((8, LANES), jnp.float32)] * parts
-        for source in range(0 if step else 1, 2):
-            held = jnp.concatenate([cells[source, first + i] for i in range(blocks)], axis=1)
-            chosen = jnp.where(element == held[0:1], 1.0, 0.0).astype(jnp.bfloat16)
-            chosen = jnp.concatenate([chosen, chosen], axis=0)
-            held = jnp.concatenate([weights[source, first + i] for i in range(blocks)], axis=1)
-            high = held.astype(jnp.bfloat16)
-            rest = held - high.astype(jnp.float32)
-            middle = rest.astype(jnp.bfloat16)
-            low = (rest - middle.astype(jnp.float32)).astype(jnp.bfloat16)
-            pieces = jnp.concatenate([high, middle, low], axis=0)
-            plane = jnp.dot(expand_ref[...], pieces, preferred_element_type=jnp.float32)
-            planes[number] = plane[:ROWS] * plane[ROWS:]
-            tiles = []
-            for top in range(0, LANES, 8):
-                a = top // 25
-                factor = jnp.broadcast_to(held[a : a + 1], (8, width))
-                if top < 25 * (a + 1) < top + 8 and a < 4:
-                    later = jnp.broadcast_to(held[a + 1 : a + 2], (8, width))
-                    factor = jnp.where(row < 25 * (a + 1) - top, factor, later)
-                tiles.append(factor * planes[number, top % 25 : top % 25 + 8, :])
-            weight = jnp.concatenate(tiles, axis=0)[:125]
-            for v in range(5):
-                picked = jnp.dot(
-                    halves[5 * source + v], chosen, preferred_element_type=jnp.float32
-                )
-                value = jnp.sum(picked * weight, axis=0, keepdims=True) + SHIFT[v]
-                for block in range(blocks):
-                    values[number, block, v : v + 1, :] = value[
-                        :, block * LANES : (block + 1) * LANES
-                    ]
-            place = (step + source - 1) * count
-            wanted = in_lanes(lane, place, count)
-            for q in range(parts):
-                offset = start - first * LANES + partner(here, q) * count
-                block = offset // LANES
-                index = lane + (offset - block * LANES - place)
-                inside = index & (LANES - 1)
-                near = lane_gather(values[number, block], inside)
-                far = lane_gather(values[number, block + 1], inside)
-                found[q] = jnp.where(wanted, jnp.where(index < LANES, near, far), found[q])
-            number += 1
-        for z in range(outer):
-            if step:
-                outs[step - 2][z] = found[2 * z]
-                outs[step - 1][z] = found[2 * z + 1]
-            else:
-                keep_ref[z] = found[2 * z]
-                side_ref[outer * height + 8 * z : outer * height + 8 * z + 8, :] = found[2 * z + 1]
+    found = {}
+    for number, step, place, start in places:
+        wanted = in_lanes(lane, place, count)
+        for q in range(parts):
+            offset = start + partner(here, q) * count
+            block = offset // LANES
+            index = lane + (offset - block * LANES - place)
+            inside = index & (LANES - 1)
+            near = lane_gather(values[number, block], inside)
+            far = lane_gather(values[number, block + 1], inside)
+            value = jnp.where(wanted, jnp.where(index < LANES, near, far), 0.0)
+            found[step, q] = found[step, q] + value if (step, q) in found else value
+    for z in range(outer):
+        for step in range(2, grids, 2):
+            outs[step - 2][z] = found[step, 2 * z]
+            outs[step - 1][z] = found[step, 2 * z + 1]
+        keep_ref[z] = found[0, 2 * z]
+        side_ref[outer * height + 8 * z : outer * height + 8 * z + 8, :] = found[0, 2 * z + 1]
 
 
 def face_kernel(
@@ -563,7 +567,6 @@
     height = -(-6 * capacity // 8) * 8
     span = parts * count
     blocks = (2 * (LANES - 1) + span) // LANES
-    sets = grids - 1
     held_blocks = -(-total // LANES) + blocks
     faces, volume, lift = matrices()
     lift = np.pad(lift, ((0, LANES - 125), (0, 0)))
@@ -620,8 +623,9 @@
         [
             pltpu.VMEM((2, held_blocks, 8, LANES), jnp.int32),
             memory((2, held_blocks, 16, LANES)),
-            memory((sets, ROWS, blocks * LANES)),
-            memory((sets, blocks + 1, 8, LANES)),
+            memory((2, 5, LANES, LANES)),
+            memory((2, ROWS, grids // 2 * blocks * LANES)),
+            memory((grids - 1, blocks + 1, 8, LANES)),
         ],
         5_000_000,
         500_000,

time: 21.7 us -> 21.6 us (level)
  no operation moved by 1% of the time
where the time goes in v8:
time: 21.6 us; the launch traced here: 21.5 us
  starting transfers between devices  9.43 us (44%)
  waiting for transfers between devices  6.71 us (31%)
  Pallas kernels  4.09 us (19%)
  local copies, waits for them, and re-layouts  1.15 us (5%)
    ppermute x9, starting transfers between devices, exchange(): return lax.ppermute(values, ('grid', 'dom'), pairs)  9.43 us
    ppermute x9, waiting for transfers between devices, exchange(): return lax.ppermute(values, ('grid', 'dom'), pairs)  6.71 us
    pallas_call x6, Pallas kernels, call(): pl.pallas_call(kernel, name=name, out_shape=out_shape, scratch_shapes=scr...  4.09 us
    unnamed x22, local copies, waits for them, and re-layouts  1.15 us
  transfers between devices with their start and end apart: 9, of which 3 were waited for; matrix products, arithmetic and copies ran while one was open for 0% of the time, Pallas kernels for 6%

profile of v8, /device:TPU:0, one launch (start us, length us, event | category | flops | bytes accessed | tf_op | source)
XLA Modules:
  0.0 21.5 jit_solution(6178723700525052575)
XLA Ops:
  0.0 0.5 %collective-permute-start = (f32[5,125,128]{2,1,0:T(8,128)}, f32[5,125,128]{2,1,0:T(8,128)S(1)}, u32[]{:S(2)}, u32[]{:S(2)}) collective-permute-start(f32[5,125,128]{2,1,0:T(8,128)} %state_ref.3), channel_id=1, source_target_pairs={{0,8},{1,9},{2,10},{3,11},{4,12},{5,13},{6,14},{7,15},{8,0},{9,1},... | collective-permute-start | bytes 960008 | tf_op jit(solution)/shard_map/ppermute | solution.py:586
  0.5 0.0 copy-start
  0.5 0.0 copy-start.6
  0.5 0.0 copy-start.7
  0.5 0.0 copy-start.9
  0.5 0.1 collective-permute-start.2
  0.6 0.5 %collective-permute-start.1 = (s32[1,1184]{1,0:T(1,128)}, s32[1,1184]{1,0:T(1,128)S(1)}, u32[]{:S(2)}, u32[]{:S(2)}) collective-permute-start(s32[1,1184]{1,0:T(1,128)} %refs_2_.1), channel_id=1, source_target_pairs={{0,8},{1,9},{2,10},{3,11},{4,12},{5,13},{6,14},{7,15},{8,0},{9,1},... | collective-permute-start | bytes 14216 | tf_op jit(solution)/shard_map/ppermute | solution.py:586
  1.1 0.3 %copy-done = f32[5,125,128]{2,1,0:T(8,128)S(1)} copy-done((f32[5,125,128]{2,1,0:T(8,128)S(1)}, f32[5,125,128]{2,1,0:T(8,128)}, u32[]{:S(2)}) %copy-start) | copy-done | bytes 320024
  1.4 0.0 copy-done.6
  1.4 0.0 copy-done.7
  1.4 0.0 copy-done.9
  1.5 0.0 copy-start.2
  1.5 0.0 copy-start.3
  1.5 0.6 %faces.1 = (f32[6,5,32,128]{3,2,1,0:T(8,128)S(1)}, f32[2,5,32,128]{3,2,1,0:T(8,128)S(1)}, f32[256,128]{1,0:T(8,128)S(1)}) custom-call(f32[5,125,128]{2,1,0:T(8,128)S(1)} %copy-done, s32[3,128]{1,0:T(4,128)S(1)} %copy-done.6, s32[3,128]{1,0:T(4,128)S(1)} %copy-done.7, f32[192,125]{1,0:T(8,128)S(1)} %copy-done.9, s32[8,128]{1,0:T(8,128)S(1)} %get-tuple-element.24.lanes_ref), custom_call_target="tpu_custom_call" | custom-call | flops 200000000 | bytes 1500000 | tf_op jit(solution)/shard_map/faces/pallas_call | solution.py:545
  2.1 0.0 collective-permute-done.1.refs_3_
  2.1 0.0 collective-permute-done.2.refs_5_
  2.1 0.0 collective-permute-done.refs_1_
  2.1 0.3 %copy-done.2 = f32[1,3,5,1184]{3,0,2,1:T(1,128)S(1)} copy-done((f32[1,3,5,1184]{3,0,2,1:T(1,128)S(1)}, f32[1,3,5,1184]{3,0,2,1:T(1,128)}, u32[]{:S(2)}) %copy-start.2) | copy-done | bytes 71064
  2.4 0.0 copy-done.3
  2.4 1.2 %donors.1 = (f32[4,8,128]{2,1,0:T(8,128)S(1)}, f32[160,128]{1,0:T(8,128)S(1)}, f32[4,8,128]{2,1,0:T(8,128)S(1)}, f32[4,8,128]{2,1,0:T(8,128)S(1)}) custom-call(f32[5,125,128]{2,1,0:T(8,128)S(1)} %copy-done, f32[5,125,128]{2,1,0:T(8,128)S(1)} %collective-permute-done.refs_1_, s32[1,1184]{1,0:T(1,128)S(1)} %copy-done.3, ...), custom_call_target="tpu_custom_call" | custom-call | flops 5000000 | bytes 500000 | tf_op jit(solution)/shard_map/donors/pallas_call | solution.py:545
  3.5 0.0 copy-start.8
  3.5 2.6 %collective-permute-start.4 = (f32[160,128]{1,0:T(8,128)S(1)}, f32[160,128]{1,0:T(8,128)S(1)}, u32[]{:S(2)}, u32[]{:S(2)}) collective-permute-start(f32[160,128]{1,0:T(8,128)S(1)} %get-tuple-element.29), channel_id=1, source_target_pairs={{0,1},{1,0},{2,3},{3,2},{4,5},{5,4},{6,7},{7,6},{8,9},{9,8},{10,11... | collective-permute-start | bytes 245768 | tf_op jit(solution)/shard_map/ppermute | solution.py:586
  6.2 1.5 %collective-permute-start.3 = (f32[4,8,128]{2,1,0:T(8,128)S(1)}, f32[4,8,128]{2,1,0:T(8,128)S(1)}, u32[]{:S(2)}, u32[]{:S(2)}) collective-permute-start(f32[4,8,128]{2,1,0:T(8,128)S(1)} %get-tuple-element.28), channel_id=1, source_target_pairs={{0,17},{1,16},{2,19},{3,18},{4,21},{5,20},{6,23},{7,22},{8,25},{9,... | collective-permute-start | bytes 49160 | tf_op jit(solution)/shard_map/ppermute | solution.py:586
  7.7 0.0 collective-permute-start.5
  7.7 3.1 %collective-permute-done.3.refs_0_ = f32[4,8,128]{2,1,0:T(8,128)S(1)} collective-permute-done((f32[4,8,128]{2,1,0:T(8,128)S(1)}, f32[4,8,128]{2,1,0:T(8,128)S(1)}, u32[]{:S(2)}, u32[]{:S(2)}) %collective-permute-start.3) | collective-permute-done | bytes 16416 | tf_op jit(solution)/shard_map/ppermute | solution.py:586
  10.8 0.6 %collective-permute-done.5.refs_2_ = f32[4,8,128]{2,1,0:T(8,128)S(1)} collective-permute-done((f32[4,8,128]{2,1,0:T(8,128)S(1)}, f32[4,8,128]{2,1,0:T(8,128)S(1)}, u32[]{:S(2)}, u32[]{:S(2)}) %collective-permute-start.5) | collective-permute-done | bytes 16416 | tf_op jit(solution)/shard_map/ppermute | solution.py:586
  11.4 0.0 collective-permute-done.4.refs_1_
  11.4 0.0 copy-start.10
  11.4 2.7 %collective-permute-start.6 = (f32[80,128]{1,0:T(8,128)S(1)}, f32[80,128]{1,0:T(8,128)S(1)}, u32[]{:S(2)}, u32[]{:S(2)}) collective-permute-start(f32[80,128]{1,0:T(8,128)S(1)} %get-tuple-element.32), channel_id=1, source_target_pairs={{0,4},{1,5},{2,6},{3,7},{4,0},{5,1},{6,2},{7,3},{8,12},{9,13},{10,... | collective-permute-start | bytes 122888 | tf_op jit(solution)/shard_map/ppermute | solution.py:586
  14.1 0.0 copy-start.5
  14.1 1.3 %collective-permute-start.7 = (f32[80,128]{1,0:T(8,128)S(1)}, f32[80,128]{1,0:T(8,128)S(1)}, u32[]{:S(2)}, u32[]{:S(2)}) collective-permute-start(f32[80,128]{1,0:T(8,128)S(1)} %get-tuple-element.33), channel_id=1, source_target_pairs={{0,6},{1,7},{2,4},{3,5},{4,2},{5,3},{6,0},{7,1},{8,14},{9,15},{10,... | collective-permute-start | bytes 122888 | tf_op jit(solution)/shard_map/ppermute | solution.py:586
  15.4 0.0 copy-start.4
  15.4 0.2 %collective-permute-start.8 = (f32[80,128]{1,0:T(8,128)S(1)}, f32[80,128]{1,0:T(8,128)S(1)}, u32[]{:S(2)}, u32[]{:S(2)}) collective-permute-start(f32[80,128]{1,0:T(8,128)S(1)} %get-tuple-element.34), channel_id=1, source_target_pairs={{0,2},{1,3},{2,0},{3,1},{4,6},{5,7},{6,4},{7,5},{8,10},{9,11},{10,... | collective-permute-start | bytes 122888 | tf_op jit(solution)/shard_map/ppermute | solution.py:586
  15.7 0.0 copy-done.8
  15.7 0.0 copy-done.10
  15.7 0.0 copy-done.5
  15.7 0.4 %copy-done.4 = f32[3,128]{1,0:T(4,128)S(1)} copy-done((f32[3,128]{1,0:T(4,128)S(1)}, f32[3,128]{1,0:T(4,128)}, u32[]{:S(2)}) %copy-start.4) | copy-done | bytes 1560
  16.1 0.0 copy-start.1
  16.1 0.8 %volume.1 = (f32[125,640]{1,0:T(8,128)S(1)}, f32[2,6,32,128]{3,2,1,0:T(8,128)S(1)}, f32[2,11,32,128]{3,2,1,0:T(8,128)S(1)}, f32[3,5,32,128]{3,2,1,0:T(8,128)S(1)...) custom-call(f32[5,125,128]{2,1,0:T(8,128)S(1)} %copy-done, f32[3,128]{1,0:T(4,128)S(1)} %copy-done.4, ...), custom_call_target="tpu_custom_call" | custom-call | flops 400000000 | bytes 3000000 | tf_op jit(solution)/shard_map/volume/pallas_call | solution.py:545
  16.9 0.0 collective-permute-done.6.refs_1_
  16.9 3.0 %collective-permute-done.7.refs_2_ = f32[80,128]{1,0:T(8,128)S(1)} collective-permute-done((f32[80,128]{1,0:T(8,128)S(1)}, f32[80,128]{1,0:T(8,128)S(1)}, u32[]{:S(2)}, u32[]{:S(2)}) %collective-permute-start.7) | collective-permute-done | bytes 40992 | tf_op jit(solution)/shard_map/ppermute | solution.py:586
  19.9 0.0 collective-permute-done.8.refs_3_
  19.9 0.0 copy-done.1
  19.9 1.5 %finish.1 = f32[5,125,128]{2,1,0:T(8,128)} custom-call(f32[80,128]{1,0:T(8,128)S(1)} %get-tuple-element.31.refs_0_, f32[80,128]{1,0:T(8,128)S(1)} %collective-permute-done.6.refs_1_, f32[80,128]{1,0:T(8,128)S(1)} %collective-permute-done.7.refs_2_, f32[80,128]{1,0:T(8,128)S(1)} %collective-permute-done.8.refs_3_, ...), custom_call_target="tpu_custom_call" | custom-call | flops 200000000 | bytes 3000000 | tf_op jit(solution)/shard_map/finish/pallas_call | solution.py:545
  (2 shorter events, 0.1 us)
Async XLA Ops:
  0.0 2.1 %collective-permute-start = (f32[5,125,128]{2,1,0:T(8,128)}, f32[5,125,128]{2,1,0:T(8,128)S(1)}, u32[]{:S(2)}, u32[]{:S(2)}) collective-permute-start(f32[5,125,128]{2,1,0:T(8,128)} %state_ref.3), channel_id=1, source_target_pairs={{0,8},{1,9},{2,10},{3,11},{4,12},{5,13},{6,14},{7,15},{8,0},{9,1},... | collective-permute-start | bytes 960008 | tf_op jit(solution)/shard_map/ppermute | solution.py:586
  0.5 1.0 %copy-start = (f32[5,125,128]{2,1,0:T(8,128)S(1)}, f32[5,125,128]{2,1,0:T(8,128)}, u32[]{:S(2)}) copy-start(f32[5,125,128]{2,1,0:T(8,128)} %state_ref.3) | copy-start | bytes 960004
  0.5 1.0 %copy-start.6 = (s32[3,128]{1,0:T(4,128)S(1)}, s32[3,128]{1,0:T(4,128)}, u32[]{:S(2)}) copy-start(s32[3,128]{1,0:T(4,128)} %plus_ref.3) | copy-start | bytes 4612
  0.5 1.0 %copy-start.7 = (s32[3,128]{1,0:T(4,128)S(1)}, s32[3,128]{1,0:T(4,128)}, u32[]{:S(2)}) copy-start(s32[3,128]{1,0:T(4,128)} %minus_ref.3) | copy-start | bytes 4612
  0.5 1.0 %copy-start.9 = (f32[192,125]{1,0:T(8,128)S(1)}, f32[192,125]{1,0:T(8,128)}, u32[]{:S(2)}) copy-start(f32[192,125]{1,0:T(8,128)} %constant.8.clone.faces_ref) | copy-start | bytes 288004
  0.5 1.6 %collective-permute-start.2 = (f32[15,1,1184]{2,1,0:T(1,128)}, f32[15,1,1184]{2,1,0:T(1,128)S(1)}, u32[]{:S(2)}, u32[]{:S(2)}) collective-permute-start(f32[15,1,1184]{2,1,0:T(1,128)} %bitcast.1), channel_id=1, source_target_pairs={{0,8},{1,9},{2,10},{3,11},{4,12},{5,13},{6,14},{7,15},{8,0},{9,1},... | collective-permute-start | bytes 213128 | tf_op jit(solution)/shard_map/ppermute | solution.py:586
  0.6 1.5 %collective-permute-start.1 = (s32[1,1184]{1,0:T(1,128)}, s32[1,1184]{1,0:T(1,128)S(1)}, u32[]{:S(2)}, u32[]{:S(2)}) collective-permute-start(s32[1,1184]{1,0:T(1,128)} %refs_2_.1), channel_id=1, source_target_pairs={{0,8},{1,9},{2,10},{3,11},{4,12},{5,13},{6,14},{7,15},{8,0},{9,1},... | collective-permute-start | bytes 14216 | tf_op jit(solution)/shard_map/ppermute | solution.py:586
  1.5 0.9 %copy-start.2 = (f32[1,3,5,1184]{3,0,2,1:T(1,128)S(1)}, f32[1,3,5,1184]{3,0,2,1:T(1,128)}, u32[]{:S(2)}) copy-start(f32[1,3,5,1184]{3,0,2,1:T(1,128)} %param.16) | copy-start | bytes 213124
  1.5 0.9 %copy-start.3 = (s32[1,1184]{1,0:T(1,128)S(1)}, s32[1,1184]{1,0:T(1,128)}, u32[]{:S(2)}) copy-start(s32[1,1184]{1,0:T(1,128)} %refs_2_.1) | copy-start | bytes 14212
  3.5 12.1 %copy-start.8 = (f32[125,384]{1,0:T(8,128)S(1)}, f32[125,384]{1,0:T(8,128)}, u32[]{:S(2)}) copy-start(f32[125,384]{1,0:T(8,128)} %constant.9.clone.volume_ref) | copy-start | bytes 576004
  3.5 7.9 %collective-permute-start.4 = (f32[160,128]{1,0:T(8,128)S(1)}, f32[160,128]{1,0:T(8,128)S(1)}, u32[]{:S(2)}, u32[]{:S(2)}) collective-permute-start(f32[160,128]{1,0:T(8,128)S(1)} %get-tuple-element.29), channel_id=1, source_target_pairs={{0,1},{1,0},{2,3},{3,2},{4,5},{5,4},{6,7},{7,6},{8,9},{9,8},{10,11... | collective-permute-start | bytes 245768 | tf_op jit(solution)/shard_map/ppermute | solution.py:586
  6.2 4.6 %collective-permute-start.3 = (f32[4,8,128]{2,1,0:T(8,128)S(1)}, f32[4,8,128]{2,1,0:T(8,128)S(1)}, u32[]{:S(2)}, u32[]{:S(2)}) collective-permute-start(f32[4,8,128]{2,1,0:T(8,128)S(1)} %get-tuple-element.28), channel_id=1, source_target_pairs={{0,17},{1,16},{2,19},{3,18},{4,21},{5,20},{6,23},{7,22},{8,25},{9,... | collective-permute-start | bytes 49160 | tf_op jit(solution)/shard_map/ppermute | solution.py:586
  7.7 3.7 %collective-permute-start.5 = (f32[4,8,128]{2,1,0:T(8,128)S(1)}, f32[4,8,128]{2,1,0:T(8,128)S(1)}, u32[]{:S(2)}, u32[]{:S(2)}) collective-permute-start(f32[4,8,128]{2,1,0:T(8,128)S(1)} %get-tuple-element.30), channel_id=1, source_target_pairs={{0,16},{1,17},{2,18},{3,19},{4,20},{5,21},{6,22},{7,23},{8,24},{9,... | collective-permute-start | bytes 49160 | tf_op jit(solution)/shard_map/ppermute | solution.py:586
  11.4 4.3 %copy-start.10 = (s32[8,128]{1,0:T(8,128)S(1)}, s32[8,128]{1,0:T(8,128)}, u32[]{:S(2)}) copy-start(s32[8,128]{1,0:T(8,128)} %constant.10.clone.points_ref) | copy-start | bytes 12292
  11.4 5.5 %collective-permute-start.6 = (f32[80,128]{1,0:T(8,128)S(1)}, f32[80,128]{1,0:T(8,128)S(1)}, u32[]{:S(2)}, u32[]{:S(2)}) collective-permute-start(f32[80,128]{1,0:T(8,128)S(1)} %get-tuple-element.32), channel_id=1, source_target_pairs={{0,4},{1,5},{2,6},{3,7},{4,0},{5,1},{6,2},{7,3},{8,12},{9,13},{10,... | collective-permute-start | bytes 122888 | tf_op jit(solution)/shard_map/ppermute | solution.py:586
  14.1 1.6 %copy-start.5 = (s32[1,600]{1,0:T(1,128)S(1)}, s32[1,600]{1,0:T(1,128)}, u32[]{:S(2)}) copy-start(s32[1,600]{1,0:T(1,128)} %recv_ref.1) | copy-start | bytes 7204
  14.1 5.8 %collective-permute-start.7 = (f32[80,128]{1,0:T(8,128)S(1)}, f32[80,128]{1,0:T(8,128)S(1)}, u32[]{:S(2)}, u32[]{:S(2)}) collective-permute-start(f32[80,128]{1,0:T(8,128)S(1)} %get-tuple-element.33), channel_id=1, source_target_pairs={{0,6},{1,7},{2,4},{3,5},{4,2},{5,3},{6,0},{7,1},{8,14},{9,15},{10,... | collective-permute-start | bytes 122888 | tf_op jit(solution)/shard_map/ppermute | solution.py:586
  15.4 0.7 %copy-start.4 = (f32[3,128]{1,0:T(4,128)S(1)}, f32[3,128]{1,0:T(4,128)}, u32[]{:S(2)}) copy-start(f32[3,128]{1,0:T(4,128)} %refs_11_.1) | copy-start | bytes 4612
  15.4 4.5 %collective-permute-start.8 = (f32[80,128]{1,0:T(8,128)S(1)}, f32[80,128]{1,0:T(8,128)S(1)}, u32[]{:S(2)}, u32[]{:S(2)}) collective-permute-start(f32[80,128]{1,0:T(8,128)S(1)} %get-tuple-element.34), channel_id=1, source_target_pairs={{0,2},{1,3},{2,0},{3,1},{4,6},{5,7},{6,4},{7,5},{8,10},{9,11},{10,... | collective-permute-start | bytes 122888 | tf_op jit(solution)/shard_map/ppermute | solution.py:586
  16.1 3.8 %copy-start.1 = (bf16[256,192]{1,0:T(8,128)(2,1)S(1)}, bf16[256,192]{1,0:T(8,128)(2,1)}, u32[]{:S(2)}) copy-start(bf16[256,192]{1,0:T(8,128)(2,1)} %constant.11.clone.refs_12_) | copy-start | bytes 294916

commit v9 on v8

--- a/solution.py
+++ b/solution.py
@@ -208,7 +208,7 @@
 
 
 def donor_kernel(grids, parts, count, height, *refs):
-    states, cell_refs, weight_refs = (refs[k : k + 2] for k in (0, 2, 4))
+    weight_refs, cell_refs, states = (refs[k : k + 2] for k in (0, 2, 4))
     expand_ref, pay_ref, keep_ref, side_ref = refs[6:10]
     outs = refs[10 : 8 + grids]
     cells, weights, padded, planes, values = refs[8 + grids :]
@@ -629,12 +629,12 @@
         ],
         5_000_000,
         500_000,
+        weights,
+        mates[2],
+        donor_cell,
+        mates[1],
         state,
         mates[0],
-        donor_cell,
-        mates[1],
-        weights,
-        mates[2],
         expand,
         pay,
     )

time: 21.6 us -> 21.6 us (level)
  no operation moved by 1% of the time
where the time goes in v9:
time: 21.6 us; the launch traced here: 21.5 us
  starting transfers between devices  9.43 us (44%)
  waiting for transfers between devices  6.71 us (31%)
  Pallas kernels  4.09 us (19%)
  local copies, waits for them, and re-layouts  1.15 us (5%)
    ppermute x9, starting transfers between devices, exchange(): return lax.ppermute(values, ('grid', 'dom'), pairs)  9.43 us
    ppermute x9, waiting for transfers between devices, exchange(): return lax.ppermute(values, ('grid', 'dom'), pairs)  6.71 us
    pallas_call x6, Pallas kernels, call(): pl.pallas_call(kernel, name=name, out_shape=out_shape, scratch_shapes=scr...  4.09 us
    unnamed x22, local copies, waits for them, and re-layouts  1.15 us
  transfers between devices with their start and end apart: 9, of which 3 were waited for; matrix products, arithmetic and copies ran while one was open for 0% of the time, Pallas kernels for 6%

profile of v9, /device:TPU:0, one launch (start us, length us, event | category | flops | bytes accessed | tf_op | source)
XLA Modules:
  0.0 21.5 jit_solution(3089368134557710248)
XLA Ops:
  0.0 0.5 %collective-permute-start.2 = (f32[5,125,128]{2,1,0:T(8,128)}, f32[5,125,128]{2,1,0:T(8,128)S(1)}, u32[]{:S(2)}, u32[]{:S(2)}) collective-permute-start(f32[5,125,128]{2,1,0:T(8,128)} %state_ref.3), channel_id=1, source_target_pairs={{0,8},{1,9},{2,10},{3,11},{4,12},{5,13},{6,14},{7,15},{8,0},{9,1},... | collective-permute-start | bytes 960008 | tf_op jit(solution)/shard_map/ppermute | solution.py:586
  0.5 0.0 copy-start
  0.5 0.0 copy-start.6
  0.5 0.0 copy-start.7
  0.5 0.0 copy-start.9
  0.5 0.1 collective-permute-start
  0.6 0.5 %collective-permute-start.1 = (s32[1,1184]{1,0:T(1,128)}, s32[1,1184]{1,0:T(1,128)S(1)}, u32[]{:S(2)}, u32[]{:S(2)}) collective-permute-start(s32[1,1184]{1,0:T(1,128)} %refs_2_.1), channel_id=1, source_target_pairs={{0,8},{1,9},{2,10},{3,11},{4,12},{5,13},{6,14},{7,15},{8,0},{9,1},... | collective-permute-start | bytes 14216 | tf_op jit(solution)/shard_map/ppermute | solution.py:586
  1.1 0.3 %copy-done = f32[5,125,128]{2,1,0:T(8,128)S(1)} copy-done((f32[5,125,128]{2,1,0:T(8,128)S(1)}, f32[5,125,128]{2,1,0:T(8,128)}, u32[]{:S(2)}) %copy-start) | copy-done | bytes 320024
  1.4 0.0 copy-done.6
  1.4 0.0 copy-done.7
  1.4 0.0 copy-done.9
  1.5 0.0 copy-start.2
  1.5 0.0 copy-start.3
  1.5 0.6 %faces.1 = (f32[6,5,32,128]{3,2,1,0:T(8,128)S(1)}, f32[2,5,32,128]{3,2,1,0:T(8,128)S(1)}, f32[256,128]{1,0:T(8,128)S(1)}) custom-call(f32[5,125,128]{2,1,0:T(8,128)S(1)} %copy-done, s32[3,128]{1,0:T(4,128)S(1)} %copy-done.6, s32[3,128]{1,0:T(4,128)S(1)} %copy-done.7, f32[192,125]{1,0:T(8,128)S(1)} %copy-done.9, s32[8,128]{1,0:T(8,128)S(1)} %get-tuple-element.24.lanes_ref), custom_call_target="tpu_custom_call" | custom-call | flops 200000000 | bytes 1500000 | tf_op jit(solution)/shard_map/faces/pallas_call | solution.py:545
  2.1 0.0 collective-permute-done.1.refs_3_
  2.1 0.0 collective-permute-done.refs_1_
  2.1 0.0 collective-permute-done.2.refs_5_
  2.1 0.3 %copy-done.2 = f32[1,3,5,1184]{3,0,2,1:T(1,128)S(1)} copy-done((f32[1,3,5,1184]{3,0,2,1:T(1,128)S(1)}, f32[1,3,5,1184]{3,0,2,1:T(1,128)}, u32[]{:S(2)}) %copy-start.2) | copy-done | bytes 71064
  2.4 0.0 copy-done.3
  2.4 1.2 %donors.1 = (f32[4,8,128]{2,1,0:T(8,128)S(1)}, f32[160,128]{1,0:T(8,128)S(1)}, f32[4,8,128]{2,1,0:T(8,128)S(1)}, f32[4,8,128]{2,1,0:T(8,128)S(1)}) custom-call(f32[15,1,1184]{2,1,0:T(1,128)S(1)} %bitcast.2, f32[15,1,1184]{2,1,0:T(1,128)S(1)} %collective-permute-done.refs_1_, s32[1,1184]{1,0:T(1,128)S(1)} %copy-done.3, ...), custom_call_target="tpu_custom_call" | custom-call | flops 5000000 | bytes 500000 | tf_op jit(solution)/shard_map/donors/pallas_call | solution.py:545
  3.5 0.0 copy-start.8
  3.5 2.6 %collective-permute-start.4 = (f32[160,128]{1,0:T(8,128)S(1)}, f32[160,128]{1,0:T(8,128)S(1)}, u32[]{:S(2)}, u32[]{:S(2)}) collective-permute-start(f32[160,128]{1,0:T(8,128)S(1)} %get-tuple-element.29), channel_id=1, source_target_pairs={{0,1},{1,0},{2,3},{3,2},{4,5},{5,4},{6,7},{7,6},{8,9},{9,8},{10,11... | collective-permute-start | bytes 245768 | tf_op jit(solution)/shard_map/ppermute | solution.py:586
  6.2 1.5 %collective-permute-start.3 = (f32[4,8,128]{2,1,0:T(8,128)S(1)}, f32[4,8,128]{2,1,0:T(8,128)S(1)}, u32[]{:S(2)}, u32[]{:S(2)}) collective-permute-start(f32[4,8,128]{2,1,0:T(8,128)S(1)} %get-tuple-element.28), channel_id=1, source_target_pairs={{0,17},{1,16},{2,19},{3,18},{4,21},{5,20},{6,23},{7,22},{8,25},{9,... | collective-permute-start | bytes 49160 | tf_op jit(solution)/shard_map/ppermute | solution.py:586
  7.7 0.0 collective-permute-start.5
  7.7 3.1 %collective-permute-done.3.refs_0_ = f32[4,8,128]{2,1,0:T(8,128)S(1)} collective-permute-done((f32[4,8,128]{2,1,0:T(8,128)S(1)}, f32[4,8,128]{2,1,0:T(8,128)S(1)}, u32[]{:S(2)}, u32[]{:S(2)}) %collective-permute-start.3) | collective-permute-done | bytes 16416 | tf_op jit(solution)/shard_map/ppermute | solution.py:586
  10.8 0.6 %collective-permute-done.5.refs_2_ = f32[4,8,128]{2,1,0:T(8,128)S(1)} collective-permute-done((f32[4,8,128]{2,1,0:T(8,128)S(1)}, f32[4,8,128]{2,1,0:T(8,128)S(1)}, u32[]{:S(2)}, u32[]{:S(2)}) %collective-permute-start.5) | collective-permute-done | bytes 16416 | tf_op jit(solution)/shard_map/ppermute | solution.py:586
  11.4 0.0 collective-permute-done.4.refs_1_
  11.4 0.0 copy-start.10
  11.4 2.7 %collective-permute-start.6 = (f32[80,128]{1,0:T(8,128)S(1)}, f32[80,128]{1,0:T(8,128)S(1)}, u32[]{:S(2)}, u32[]{:S(2)}) collective-permute-start(f32[80,128]{1,0:T(8,128)S(1)} %get-tuple-element.32), channel_id=1, source_target_pairs={{0,4},{1,5},{2,6},{3,7},{4,0},{5,1},{6,2},{7,3},{8,12},{9,13},{10,... | collective-permute-start | bytes 122888 | tf_op jit(solution)/shard_map/ppermute | solution.py:586
  14.1 0.0 copy-start.5
  14.1 1.3 %collective-permute-start.7 = (f32[80,128]{1,0:T(8,128)S(1)}, f32[80,128]{1,0:T(8,128)S(1)}, u32[]{:S(2)}, u32[]{:S(2)}) collective-permute-start(f32[80,128]{1,0:T(8,128)S(1)} %get-tuple-element.33), channel_id=1, source_target_pairs={{0,6},{1,7},{2,4},{3,5},{4,2},{5,3},{6,0},{7,1},{8,14},{9,15},{10,... | collective-permute-start | bytes 122888 | tf_op jit(solution)/shard_map/ppermute | solution.py:586
  15.4 0.0 copy-start.4
  15.4 0.2 %collective-permute-start.8 = (f32[80,128]{1,0:T(8,128)S(1)}, f32[80,128]{1,0:T(8,128)S(1)}, u32[]{:S(2)}, u32[]{:S(2)}) collective-permute-start(f32[80,128]{1,0:T(8,128)S(1)} %get-tuple-element.34), channel_id=1, source_target_pairs={{0,2},{1,3},{2,0},{3,1},{4,6},{5,7},{6,4},{7,5},{8,10},{9,11},{10,... | collective-permute-start | bytes 122888 | tf_op jit(solution)/shard_map/ppermute | solution.py:586
  15.7 0.0 copy-done.8
  15.7 0.0 copy-done.10
  15.7 0.0 copy-done.5
  15.7 0.4 %copy-done.4 = f32[3,128]{1,0:T(4,128)S(1)} copy-done((f32[3,128]{1,0:T(4,128)S(1)}, f32[3,128]{1,0:T(4,128)}, u32[]{:S(2)}) %copy-start.4) | copy-done | bytes 1560
  16.1 0.0 copy-start.1
  16.1 0.8 %volume.1 = (f32[125,640]{1,0:T(8,128)S(1)}, f32[2,6,32,128]{3,2,1,0:T(8,128)S(1)}, f32[2,11,32,128]{3,2,1,0:T(8,128)S(1)}, f32[3,5,32,128]{3,2,1,0:T(8,128)S(1)...) custom-call(f32[5,125,128]{2,1,0:T(8,128)S(1)} %copy-done, f32[3,128]{1,0:T(4,128)S(1)} %copy-done.4, ...), custom_call_target="tpu_custom_call" | custom-call | flops 400000000 | bytes 3000000 | tf_op jit(solution)/shard_map/volume/pallas_call | solution.py:545
  16.9 0.0 collective-permute-done.6.refs_1_
  16.9 3.0 %collective-permute-done.7.refs_2_ = f32[80,128]{1,0:T(8,128)S(1)} collective-permute-done((f32[80,128]{1,0:T(8,128)S(1)}, f32[80,128]{1,0:T(8,128)S(1)}, u32[]{:S(2)}, u32[]{:S(2)}) %collective-permute-start.7) | collective-permute-done | bytes 40992 | tf_op jit(solution)/shard_map/ppermute | solution.py:586
  19.9 0.0 collective-permute-done.8.refs_3_
  19.9 0.0 copy-done.1
  19.9 1.5 %finish.1 = f32[5,125,128]{2,1,0:T(8,128)} custom-call(f32[80,128]{1,0:T(8,128)S(1)} %get-tuple-element.31.refs_0_, f32[80,128]{1,0:T(8,128)S(1)} %collective-permute-done.6.refs_1_, f32[80,128]{1,0:T(8,128)S(1)} %collective-permute-done.7.refs_2_, f32[80,128]{1,0:T(8,128)S(1)} %collective-permute-done.8.refs_3_, ...), custom_call_target="tpu_custom_call" | custom-call | flops 200000000 | bytes 3000000 | tf_op jit(solution)/shard_map/finish/pallas_call | solution.py:545
  (2 shorter events, 0.1 us)
Async XLA Ops:
  0.0 2.1 %collective-permute-start.2 = (f32[5,125,128]{2,1,0:T(8,128)}, f32[5,125,128]{2,1,0:T(8,128)S(1)}, u32[]{:S(2)}, u32[]{:S(2)}) collective-permute-start(f32[5,125,128]{2,1,0:T(8,128)} %state_ref.3), channel_id=1, source_target_pairs={{0,8},{1,9},{2,10},{3,11},{4,12},{5,13},{6,14},{7,15},{8,0},{9,1},... | collective-permute-start | bytes 960008 | tf_op jit(solution)/shard_map/ppermute | solution.py:586
  0.5 1.0 %copy-start = (f32[5,125,128]{2,1,0:T(8,128)S(1)}, f32[5,125,128]{2,1,0:T(8,128)}, u32[]{:S(2)}) copy-start(f32[5,125,128]{2,1,0:T(8,128)} %state_ref.3) | copy-start | bytes 960004
  0.5 1.0 %copy-start.6 = (s32[3,128]{1,0:T(4,128)S(1)}, s32[3,128]{1,0:T(4,128)}, u32[]{:S(2)}) copy-start(s32[3,128]{1,0:T(4,128)} %plus_ref.3) | copy-start | bytes 4612
  0.5 1.0 %copy-start.7 = (s32[3,128]{1,0:T(4,128)S(1)}, s32[3,128]{1,0:T(4,128)}, u32[]{:S(2)}) copy-start(s32[3,128]{1,0:T(4,128)} %minus_ref.3) | copy-start | bytes 4612
  0.5 1.0 %copy-start.9 = (f32[192,125]{1,0:T(8,128)S(1)}, f32[192,125]{1,0:T(8,128)}, u32[]{:S(2)}) copy-start(f32[192,125]{1,0:T(8,128)} %constant.8.clone.faces_ref) | copy-start | bytes 288004
  0.5 1.6 %collective-permute-start = (f32[15,1,1184]{2,1,0:T(1,128)}, f32[15,1,1184]{2,1,0:T(1,128)S(1)}, u32[]{:S(2)}, u32[]{:S(2)}) collective-permute-start(f32[15,1,1184]{2,1,0:T(1,128)} %bitcast.1), channel_id=1, source_target_pairs={{0,8},{1,9},{2,10},{3,11},{4,12},{5,13},{6,14},{7,15},{8,0},{9,1},... | collective-permute-start | bytes 213128 | tf_op jit(solution)/shard_map/ppermute | solution.py:586
  0.6 1.5 %collective-permute-start.1 = (s32[1,1184]{1,0:T(1,128)}, s32[1,1184]{1,0:T(1,128)S(1)}, u32[]{:S(2)}, u32[]{:S(2)}) collective-permute-start(s32[1,1184]{1,0:T(1,128)} %refs_2_.1), channel_id=1, source_target_pairs={{0,8},{1,9},{2,10},{3,11},{4,12},{5,13},{6,14},{7,15},{8,0},{9,1},... | collective-permute-start | bytes 14216 | tf_op jit(solution)/shard_map/ppermute | solution.py:586
  1.5 0.9 %copy-start.2 = (f32[1,3,5,1184]{3,0,2,1:T(1,128)S(1)}, f32[1,3,5,1184]{3,0,2,1:T(1,128)}, u32[]{:S(2)}) copy-start(f32[1,3,5,1184]{3,0,2,1:T(1,128)} %param.16) | copy-start | bytes 213124
  1.5 0.9 %copy-start.3 = (s32[1,1184]{1,0:T(1,128)S(1)}, s32[1,1184]{1,0:T(1,128)}, u32[]{:S(2)}) copy-start(s32[1,1184]{1,0:T(1,128)} %refs_2_.1) | copy-start | bytes 14212
  3.5 12.1 %copy-start.8 = (f32[125,384]{1,0:T(8,128)S(1)}, f32[125,384]{1,0:T(8,128)}, u32[]{:S(2)}) copy-start(f32[125,384]{1,0:T(8,128)} %constant.9.clone.volume_ref) | copy-start | bytes 576004
  3.5 7.9 %collective-permute-start.4 = (f32[160,128]{1,0:T(8,128)S(1)}, f32[160,128]{1,0:T(8,128)S(1)}, u32[]{:S(2)}, u32[]{:S(2)}) collective-permute-start(f32[160,128]{1,0:T(8,128)S(1)} %get-tuple-element.29), channel_id=1, source_target_pairs={{0,1},{1,0},{2,3},{3,2},{4,5},{5,4},{6,7},{7,6},{8,9},{9,8},{10,11... | collective-permute-start | bytes 245768 | tf_op jit(solution)/shard_map/ppermute | solution.py:586
  6.2 4.6 %collective-permute-start.3 = (f32[4,8,128]{2,1,0:T(8,128)S(1)}, f32[4,8,128]{2,1,0:T(8,128)S(1)}, u32[]{:S(2)}, u32[]{:S(2)}) collective-permute-start(f32[4,8,128]{2,1,0:T(8,128)S(1)} %get-tuple-element.28), channel_id=1, source_target_pairs={{0,17},{1,16},{2,19},{3,18},{4,21},{5,20},{6,23},{7,22},{8,25},{9,... | collective-permute-start | bytes 49160 | tf_op jit(solution)/shard_map/ppermute | solution.py:586
  7.7 3.7 %collective-permute-start.5 = (f32[4,8,128]{2,1,0:T(8,128)S(1)}, f32[4,8,128]{2,1,0:T(8,128)S(1)}, u32[]{:S(2)}, u32[]{:S(2)}) collective-permute-start(f32[4,8,128]{2,1,0:T(8,128)S(1)} %get-tuple-element.30), channel_id=1, source_target_pairs={{0,16},{1,17},{2,18},{3,19},{4,20},{5,21},{6,22},{7,23},{8,24},{9,... | collective-permute-start | bytes 49160 | tf_op jit(solution)/shard_map/ppermute | solution.py:586
  11.4 4.3 %copy-start.10 = (s32[8,128]{1,0:T(8,128)S(1)}, s32[8,128]{1,0:T(8,128)}, u32[]{:S(2)}) copy-start(s32[8,128]{1,0:T(8,128)} %constant.10.clone.points_ref) | copy-start | bytes 12292
  11.4 5.5 %collective-permute-start.6 = (f32[80,128]{1,0:T(8,128)S(1)}, f32[80,128]{1,0:T(8,128)S(1)}, u32[]{:S(2)}, u32[]{:S(2)}) collective-permute-start(f32[80,128]{1,0:T(8,128)S(1)} %get-tuple-element.32), channel_id=1, source_target_pairs={{0,4},{1,5},{2,6},{3,7},{4,0},{5,1},{6,2},{7,3},{8,12},{9,13},{10,... | collective-permute-start | bytes 122888 | tf_op jit(solution)/shard_map/ppermute | solution.py:586
  14.1 1.6 %copy-start.5 = (s32[1,600]{1,0:T(1,128)S(1)}, s32[1,600]{1,0:T(1,128)}, u32[]{:S(2)}) copy-start(s32[1,600]{1,0:T(1,128)} %recv_ref.1) | copy-start | bytes 7204
  14.1 5.8 %collective-permute-start.7 = (f32[80,128]{1,0:T(8,128)S(1)}, f32[80,128]{1,0:T(8,128)S(1)}, u32[]{:S(2)}, u32[]{:S(2)}) collective-permute-start(f32[80,128]{1,0:T(8,128)S(1)} %get-tuple-element.33), channel_id=1, source_target_pairs={{0,6},{1,7},{2,4},{3,5},{4,2},{5,3},{6,0},{7,1},{8,14},{9,15},{10,... | collective-permute-start | bytes 122888 | tf_op jit(solution)/shard_map/ppermute | solution.py:586
  15.4 0.7 %copy-start.4 = (f32[3,128]{1,0:T(4,128)S(1)}, f32[3,128]{1,0:T(4,128)}, u32[]{:S(2)}) copy-start(f32[3,128]{1,0:T(4,128)} %refs_11_.1) | copy-start | bytes 4612
  15.4 4.5 %collective-permute-start.8 = (f32[80,128]{1,0:T(8,128)S(1)}, f32[80,128]{1,0:T(8,128)S(1)}, u32[]{:S(2)}, u32[]{:S(2)}) collective-permute-start(f32[80,128]{1,0:T(8,128)S(1)} %get-tuple-element.34), channel_id=1, source_target_pairs={{0,2},{1,3},{2,0},{3,1},{4,6},{5,7},{6,4},{7,5},{8,10},{9,11},{10,... | collective-permute-start | bytes 122888 | tf_op jit(solution)/shard_map/ppermute | solution.py:586
  16.1 3.8 %copy-start.1 = (bf16[256,192]{1,0:T(8,128)(2,1)S(1)}, bf16[256,192]{1,0:T(8,128)(2,1)}, u32[]{:S(2)}) copy-start(bf16[256,192]{1,0:T(8,128)(2,1)} %constant.11.clone.refs_12_) | copy-start | bytes 294916

commit v10 on v9

--- a/solution.py
+++ b/solution.py
@@ -14,7 +14,7 @@
 LANES = 128
 SHIFT = (1.0, 0.0, 0.0, 0.0, 2.5)
 ROWS = 32
-VMEM = 48 * 1024 * 1024
+VMEM = 24 * 1024 * 1024
 
 
 def gauss_nodes():

time: 21.6 us -> 21.6 us (level)
  no operation moved by 1% of the time
where the time goes in v10:
time: 21.6 us; the launch traced here: 21.5 us
  starting transfers between devices  9.43 us (44%)
  waiting for transfers between devices  6.71 us (31%)
  Pallas kernels  4.09 us (19%)
  local copies, waits for them, and re-layouts  1.15 us (5%)
    ppermute x9, starting transfers between devices, exchange(): return lax.ppermute(values, ('grid', 'dom'), pairs)  9.43 us
    ppermute x9, waiting for transfers between devices, exchange(): return lax.ppermute(values, ('grid', 'dom'), pairs)  6.71 us
    pallas_call x6, Pallas kernels, call(): pl.pallas_call(kernel, name=name, out_shape=out_shape, scratch_shapes=scr...  4.09 us
    unnamed x22, local copies, waits for them, and re-layouts  1.15 us
  transfers between devices with their start and end apart: 9, of which 3 were waited for; matrix products, arithmetic and copies ran while one was open for 0% of the time, Pallas kernels for 6%

profile of v10, /device:TPU:0, one launch (start us, length us, event | category | flops | bytes accessed | tf_op | source)
XLA Modules:
  0.0 21.5 jit_solution(18107625619063388402)
XLA Ops:
  0.0 0.5 %collective-permute-start.2 = (f32[5,125,128]{2,1,0:T(8,128)}, f32[5,125,128]{2,1,0:T(8,128)S(1)}, u32[]{:S(2)}, u32[]{:S(2)}) collective-permute-start(f32[5,125,128]{2,1,0:T(8,128)} %state_ref.3), channel_id=1, source_target_pairs={{0,8},{1,9},{2,10},{3,11},{4,12},{5,13},{6,14},{7,15},{8,0},{9,1},... | collective-permute-start | bytes 960008 | tf_op jit(solution)/shard_map/ppermute | solution.py:586
  0.5 0.0 copy-start
  0.5 0.0 copy-start.6
  0.5 0.0 copy-start.7
  0.5 0.0 copy-start.9
  0.5 0.1 collective-permute-start
  0.6 0.5 %collective-permute-start.1 = (s32[1,1184]{1,0:T(1,128)}, s32[1,1184]{1,0:T(1,128)S(1)}, u32[]{:S(2)}, u32[]{:S(2)}) collective-permute-start(s32[1,1184]{1,0:T(1,128)} %refs_2_.1), channel_id=1, source_target_pairs={{0,8},{1,9},{2,10},{3,11},{4,12},{5,13},{6,14},{7,15},{8,0},{9,1},... | collective-permute-start | bytes 14216 | tf_op jit(solution)/shard_map/ppermute | solution.py:586
  1.1 0.3 %copy-done = f32[5,125,128]{2,1,0:T(8,128)S(1)} copy-done((f32[5,125,128]{2,1,0:T(8,128)S(1)}, f32[5,125,128]{2,1,0:T(8,128)}, u32[]{:S(2)}) %copy-start) | copy-done | bytes 320024
  1.4 0.0 copy-done.6
  1.4 0.0 copy-done.7
  1.4 0.0 copy-done.9
  1.5 0.0 copy-start.2
  1.5 0.0 copy-start.3
  1.5 0.6 %faces.1 = (f32[6,5,32,128]{3,2,1,0:T(8,128)S(1)}, f32[2,5,32,128]{3,2,1,0:T(8,128)S(1)}, f32[256,128]{1,0:T(8,128)S(1)}) custom-call(f32[5,125,128]{2,1,0:T(8,128)S(1)} %copy-done, s32[3,128]{1,0:T(4,128)S(1)} %copy-done.6, s32[3,128]{1,0:T(4,128)S(1)} %copy-done.7, f32[192,125]{1,0:T(8,128)S(1)} %copy-done.9, s32[8,128]{1,0:T(8,128)S(1)} %get-tuple-element.24.lanes_ref), custom_call_target="tpu_custom_call" | custom-call | flops 200000000 | bytes 1500000 | tf_op jit(solution)/shard_map/faces/pallas_call | solution.py:545
  2.1 0.0 collective-permute-done.1.refs_3_
  2.1 0.0 collective-permute-done.refs_1_
  2.1 0.0 collective-permute-done.2.refs_5_
  2.1 0.3 %copy-done.2 = f32[1,3,5,1184]{3,0,2,1:T(1,128)S(1)} copy-done((f32[1,3,5,1184]{3,0,2,1:T(1,128)S(1)}, f32[1,3,5,1184]{3,0,2,1:T(1,128)}, u32[]{:S(2)}) %copy-start.2) | copy-done | bytes 71064
  2.4 0.0 copy-done.3
  2.4 1.2 %donors.1 = (f32[4,8,128]{2,1,0:T(8,128)S(1)}, f32[160,128]{1,0:T(8,128)S(1)}, f32[4,8,128]{2,1,0:T(8,128)S(1)}, f32[4,8,128]{2,1,0:T(8,128)S(1)}) custom-call(f32[15,1,1184]{2,1,0:T(1,128)S(1)} %bitcast.2, f32[15,1,1184]{2,1,0:T(1,128)S(1)} %collective-permute-done.refs_1_, s32[1,1184]{1,0:T(1,128)S(1)} %copy-done.3, ...), custom_call_target="tpu_custom_call" | custom-call | flops 5000000 | bytes 500000 | tf_op jit(solution)/shard_map/donors/pallas_call | solution.py:545
  3.5 0.0 copy-start.8
  3.5 2.6 %collective-permute-start.4 = (f32[160,128]{1,0:T(8,128)S(1)}, f32[160,128]{1,0:T(8,128)S(1)}, u32[]{:S(2)}, u32[]{:S(2)}) collective-permute-start(f32[160,128]{1,0:T(8,128)S(1)} %get-tuple-element.29), channel_id=1, source_target_pairs={{0,1},{1,0},{2,3},{3,2},{4,5},{5,4},{6,7},{7,6},{8,9},{9,8},{10,11... | collective-permute-start | bytes 245768 | tf_op jit(solution)/shard_map/ppermute | solution.py:586
  6.2 1.5 %collective-permute-start.3 = (f32[4,8,128]{2,1,0:T(8,128)S(1)}, f32[4,8,128]{2,1,0:T(8,128)S(1)}, u32[]{:S(2)}, u32[]{:S(2)}) collective-permute-start(f32[4,8,128]{2,1,0:T(8,128)S(1)} %get-tuple-element.28), channel_id=1, source_target_pairs={{0,17},{1,16},{2,19},{3,18},{4,21},{5,20},{6,23},{7,22},{8,25},{9,... | collective-permute-start | bytes 49160 | tf_op jit(solution)/shard_map/ppermute | solution.py:586
  7.7 0.0 collective-permute-start.5
  7.7 3.1 %collective-permute-done.3.refs_0_ = f32[4,8,128]{2,1,0:T(8,128)S(1)} collective-permute-done((f32[4,8,128]{2,1,0:T(8,128)S(1)}, f32[4,8,128]{2,1,0:T(8,128)S(1)}, u32[]{:S(2)}, u32[]{:S(2)}) %collective-permute-start.3) | collective-permute-done | bytes 16416 | tf_op jit(solution)/shard_map/ppermute | solution.py:586
  10.8 0.6 %collective-permute-done.5.refs_2_ = f32[4,8,128]{2,1,0:T(8,128)S(1)} collective-permute-done((f32[4,8,128]{2,1,0:T(8,128)S(1)}, f32[4,8,128]{2,1,0:T(8,128)S(1)}, u32[]{:S(2)}, u32[]{:S(2)}) %collective-permute-start.5) | collective-permute-done | bytes 16416 | tf_op jit(solution)/shard_map/ppermute | solution.py:586
  11.4 0.0 collective-permute-done.4.refs_1_
  11.4 0.0 copy-start.10
  11.4 2.7 %collective-permute-start.6 = (f32[80,128]{1,0:T(8,128)S(1)}, f32[80,128]{1,0:T(8,128)S(1)}, u32[]{:S(2)}, u32[]{:S(2)}) collective-permute-start(f32[80,128]{1,0:T(8,128)S(1)} %get-tuple-element.32), channel_id=1, source_target_pairs={{0,4},{1,5},{2,6},{3,7},{4,0},{5,1},{6,2},{7,3},{8,12},{9,13},{10,... | collective-permute-start | bytes 122888 | tf_op jit(solution)/shard_map/ppermute | solution.py:586
  14.1 0.0 copy-start.5
  14.1 1.3 %collective-permute-start.7 = (f32[80,128]{1,0:T(8,128)S(1)}, f32[80,128]{1,0:T(8,128)S(1)}, u32[]{:S(2)}, u32[]{:S(2)}) collective-permute-start(f32[80,128]{1,0:T(8,128)S(1)} %get-tuple-element.33), channel_id=1, source_target_pairs={{0,6},{1,7},{2,4},{3,5},{4,2},{5,3},{6,0},{7,1},{8,14},{9,15},{10,... | collective-permute-start | bytes 122888 | tf_op jit(solution)/shard_map/ppermute | solution.py:586
  15.4 0.0 copy-start.4
  15.4 0.2 %collective-permute-start.8 = (f32[80,128]{1,0:T(8,128)S(1)}, f32[80,128]{1,0:T(8,128)S(1)}, u32[]{:S(2)}, u32[]{:S(2)}) collective-permute-start(f32[80,128]{1,0:T(8,128)S(1)} %get-tuple-element.34), channel_id=1, source_target_pairs={{0,2},{1,3},{2,0},{3,1},{4,6},{5,7},{6,4},{7,5},{8,10},{9,11},{10,... | collective-permute-start | bytes 122888 | tf_op jit(solution)/shard_map/ppermute | solution.py:586
  15.7 0.0 copy-done.8
  15.7 0.0 copy-done.10
  15.7 0.0 copy-done.5
  15.7 0.4 %copy-done.4 = f32[3,128]{1,0:T(4,128)S(1)} copy-done((f32[3,128]{1,0:T(4,128)S(1)}, f32[3,128]{1,0:T(4,128)}, u32[]{:S(2)}) %copy-start.4) | copy-done | bytes 1560
  16.1 0.0 copy-start.1
  16.1 0.8 %volume.1 = (f32[125,640]{1,0:T(8,128)S(1)}, f32[2,6,32,128]{3,2,1,0:T(8,128)S(1)}, f32[2,11,32,128]{3,2,1,0:T(8,128)S(1)}, f32[3,5,32,128]{3,2,1,0:T(8,128)S(1)...) custom-call(f32[5,125,128]{2,1,0:T(8,128)S(1)} %copy-done, f32[3,128]{1,0:T(4,128)S(1)} %copy-done.4, ...), custom_call_target="tpu_custom_call" | custom-call | flops 400000000 | bytes 3000000 | tf_op jit(solution)/shard_map/volume/pallas_call | solution.py:545
  16.9 0.0 collective-permute-done.6.refs_1_
  16.9 3.0 %collective-permute-done.7.refs_2_ = f32[80,128]{1,0:T(8,128)S(1)} collective-permute-done((f32[80,128]{1,0:T(8,128)S(1)}, f32[80,128]{1,0:T(8,128)S(1)}, u32[]{:S(2)}, u32[]{:S(2)}) %collective-permute-start.7) | collective-permute-done | bytes 40992 | tf_op jit(solution)/shard_map/ppermute | solution.py:586
  19.9 0.0 collective-permute-done.8.refs_3_
  19.9 0.0 copy-done.1
  19.9 1.5 %finish.1 = f32[5,125,128]{2,1,0:T(8,128)} custom-call(f32[80,128]{1,0:T(8,128)S(1)} %get-tuple-element.31.refs_0_, f32[80,128]{1,0:T(8,128)S(1)} %collective-permute-done.6.refs_1_, f32[80,128]{1,0:T(8,128)S(1)} %collective-permute-done.7.refs_2_, f32[80,128]{1,0:T(8,128)S(1)} %collective-permute-done.8.refs_3_, ...), custom_call_target="tpu_custom_call" | custom-call | flops 200000000 | bytes 3000000 | tf_op jit(solution)/shard_map/finish/pallas_call | solution.py:545
  (2 shorter events, 0.1 us)
Async XLA Ops:
  0.0 2.1 %collective-permute-start.2 = (f32[5,125,128]{2,1,0:T(8,128)}, f32[5,125,128]{2,1,0:T(8,128)S(1)}, u32[]{:S(2)}, u32[]{:S(2)}) collective-permute-start(f32[5,125,128]{2,1,0:T(8,128)} %state_ref.3), channel_id=1, source_target_pairs={{0,8},{1,9},{2,10},{3,11},{4,12},{5,13},{6,14},{7,15},{8,0},{9,1},... | collective-permute-start | bytes 960008 | tf_op jit(solution)/shard_map/ppermute | solution.py:586
  0.5 1.0 %copy-start = (f32[5,125,128]{2,1,0:T(8,128)S(1)}, f32[5,125,128]{2,1,0:T(8,128)}, u32[]{:S(2)}) copy-start(f32[5,125,128]{2,1,0:T(8,128)} %state_ref.3) | copy-start | bytes 960004
  0.5 1.0 %copy-start.6 = (s32[3,128]{1,0:T(4,128)S(1)}, s32[3,128]{1,0:T(4,128)}, u32[]{:S(2)}) copy-start(s32[3,128]{1,0:T(4,128)} %plus_ref.3) | copy-start | bytes 4612
  0.5 1.0 %copy-start.7 = (s32[3,128]{1,0:T(4,128)S(1)}, s32[3,128]{1,0:T(4,128)}, u32[]{:S(2)}) copy-start(s32[3,128]{1,0:T(4,128)} %minus_ref.3) | copy-start | bytes 4612
  0.5 1.0 %copy-start.9 = (f32[192,125]{1,0:T(8,128)S(1)}, f32[192,125]{1,0:T(8,128)}, u32[]{:S(2)}) copy-start(f32[192,125]{1,0:T(8,128)} %constant.8.clone.faces_ref) | copy-start | bytes 288004
  0.5 1.6 %collective-permute-start = (f32[15,1,1184]{2,1,0:T(1,128)}, f32[15,1,1184]{2,1,0:T(1,128)S(1)}, u32[]{:S(2)}, u32[]{:S(2)}) collective-permute-start(f32[15,1,1184]{2,1,0:T(1,128)} %bitcast.1), channel_id=1, source_target_pairs={{0,8},{1,9},{2,10},{3,11},{4,12},{5,13},{6,14},{7,15},{8,0},{9,1},... | collective-permute-start | bytes 213128 | tf_op jit(solution)/shard_map/ppermute | solution.py:586
  0.6 1.5 %collective-permute-start.1 = (s32[1,1184]{1,0:T(1,128)}, s32[1,1184]{1,0:T(1,128)S(1)}, u32[]{:S(2)}, u32[]{:S(2)}) collective-permute-start(s32[1,1184]{1,0:T(1,128)} %refs_2_.1), channel_id=1, source_target_pairs={{0,8},{1,9},{2,10},{3,11},{4,12},{5,13},{6,14},{7,15},{8,0},{9,1},... | collective-permute-start | bytes 14216 | tf_op jit(solution)/shard_map/ppermute | solution.py:586
  1.5 0.9 %copy-start.2 = (f32[1,3,5,1184]{3,0,2,1:T(1,128)S(1)}, f32[1,3,5,1184]{3,0,2,1:T(1,128)}, u32[]{:S(2)}) copy-start(f32[1,3,5,1184]{3,0,2,1:T(1,128)} %param.16) | copy-start | bytes 213124
  1.5 0.9 %copy-start.3 = (s32[1,1184]{1,0:T(1,128)S(1)}, s32[1,1184]{1,0:T(1,128)}, u32[]{:S(2)}) copy-start(s32[1,1184]{1,0:T(1,128)} %refs_2_.1) | copy-start | bytes 14212
  3.5 12.1 %copy-start.8 = (f32[125,384]{1,0:T(8,128)S(1)}, f32[125,384]{1,0:T(8,128)}, u32[]{:S(2)}) copy-start(f32[125,384]{1,0:T(8,128)} %constant.9.clone.volume_ref) | copy-start | bytes 576004
  3.5 7.9 %collective-permute-start.4 = (f32[160,128]{1,0:T(8,128)S(1)}, f32[160,128]{1,0:T(8,128)S(1)}, u32[]{:S(2)}, u32[]{:S(2)}) collective-permute-start(f32[160,128]{1,0:T(8,128)S(1)} %get-tuple-element.29), channel_id=1, source_target_pairs={{0,1},{1,0},{2,3},{3,2},{4,5},{5,4},{6,7},{7,6},{8,9},{9,8},{10,11... | collective-permute-start | bytes 245768 | tf_op jit(solution)/shard_map/ppermute | solution.py:586
  6.2 4.6 %collective-permute-start.3 = (f32[4,8,128]{2,1,0:T(8,128)S(1)}, f32[4,8,128]{2,1,0:T(8,128)S(1)}, u32[]{:S(2)}, u32[]{:S(2)}) collective-permute-start(f32[4,8,128]{2,1,0:T(8,128)S(1)} %get-tuple-element.28), channel_id=1, source_target_pairs={{0,17},{1,16},{2,19},{3,18},{4,21},{5,20},{6,23},{7,22},{8,25},{9,... | collective-permute-start | bytes 49160 | tf_op jit(solution)/shard_map/ppermute | solution.py:586
  7.7 3.7 %collective-permute-start.5 = (f32[4,8,128]{2,1,0:T(8,128)S(1)}, f32[4,8,128]{2,1,0:T(8,128)S(1)}, u32[]{:S(2)}, u32[]{:S(2)}) collective-permute-start(f32[4,8,128]{2,1,0:T(8,128)S(1)} %get-tuple-element.30), channel_id=1, source_target_pairs={{0,16},{1,17},{2,18},{3,19},{4,20},{5,21},{6,22},{7,23},{8,24},{9,... | collective-permute-start | bytes 49160 | tf_op jit(solution)/shard_map/ppermute | solution.py:586
  11.4 4.3 %copy-start.10 = (s32[8,128]{1,0:T(8,128)S(1)}, s32[8,128]{1,0:T(8,128)}, u32[]{:S(2)}) copy-start(s32[8,128]{1,0:T(8,128)} %constant.10.clone.points_ref) | copy-start | bytes 12292
  11.4 5.5 %collective-permute-start.6 = (f32[80,128]{1,0:T(8,128)S(1)}, f32[80,128]{1,0:T(8,128)S(1)}, u32[]{:S(2)}, u32[]{:S(2)}) collective-permute-start(f32[80,128]{1,0:T(8,128)S(1)} %get-tuple-element.32), channel_id=1, source_target_pairs={{0,4},{1,5},{2,6},{3,7},{4,0},{5,1},{6,2},{7,3},{8,12},{9,13},{10,... | collective-permute-start | bytes 122888 | tf_op jit(solution)/shard_map/ppermute | solution.py:586
  14.1 1.6 %copy-start.5 = (s32[1,600]{1,0:T(1,128)S(1)}, s32[1,600]{1,0:T(1,128)}, u32[]{:S(2)}) copy-start(s32[1,600]{1,0:T(1,128)} %recv_ref.1) | copy-start | bytes 7204
  14.1 5.8 %collective-permute-start.7 = (f32[80,128]{1,0:T(8,128)S(1)}, f32[80,128]{1,0:T(8,128)S(1)}, u32[]{:S(2)}, u32[]{:S(2)}) collective-permute-start(f32[80,128]{1,0:T(8,128)S(1)} %get-tuple-element.33), channel_id=1, source_target_pairs={{0,6},{1,7},{2,4},{3,5},{4,2},{5,3},{6,0},{7,1},{8,14},{9,15},{10,... | collective-permute-start | bytes 122888 | tf_op jit(solution)/shard_map/ppermute | solution.py:586
  15.4 0.7 %copy-start.4 = (f32[3,128]{1,0:T(4,128)S(1)}, f32[3,128]{1,0:T(4,128)}, u32[]{:S(2)}) copy-start(f32[3,128]{1,0:T(4,128)} %refs_11_.1) | copy-start | bytes 4612
  15.4 4.5 %collective-permute-start.8 = (f32[80,128]{1,0:T(8,128)S(1)}, f32[80,128]{1,0:T(8,128)S(1)}, u32[]{:S(2)}, u32[]{:S(2)}) collective-permute-start(f32[80,128]{1,0:T(8,128)S(1)} %get-tuple-element.34), channel_id=1, source_target_pairs={{0,2},{1,3},{2,0},{3,1},{4,6},{5,7},{6,4},{7,5},{8,10},{9,11},{10,... | collective-permute-start | bytes 122888 | tf_op jit(solution)/shard_map/ppermute | solution.py:586
  16.1 3.8 %copy-start.1 = (bf16[256,192]{1,0:T(8,128)(2,1)S(1)}, bf16[256,192]{1,0:T(8,128)(2,1)}, u32[]{:S(2)}) copy-start(bf16[256,192]{1,0:T(8,128)(2,1)} %constant.11.clone.refs_12_) | copy-start | bytes 294916
